TPU v7x, 32 devices: a whole 2x2x4 slice. The times are simulated.
32 devices in a mesh: wide: 8 (over y, x, core), narrow: 4 (over z).
Axes of the slice: x: 2, y: 2, z: 4, core: 2. Of those that a mesh axis runs over, the one named last changes fastest.
Arguments:
- currents: float32 [2, 2, 1024, 8192], P(None, None, 'wide', 'narrow'), may hold values from -6 to 6
- far_gradient: float32 [2, 2, 1024, 1024], P(None, None, 'wide', 'narrow'), may hold values from -24 to 24
Outputs:
- far_field: float32 [2, 2, 1024, 1024], P(None, None, 'wide', 'narrow')
- aperture_grad: float32 [2, 2, 1024, 8192], P(None, None, 'wide', 'narrow')
All inputs are finite; a program needn't handle non-finite values.
Results may differ from a plain program's by a relative error of at most 0.0001.
Values sent between devices are 32-bit elements; how exact they have to be, the bound alone decides.
No kernel may reach another device: no remote copies, remote signals or barrier semaphores. Data moves between devices by JAX's collectives and lax.ppermute only.
A program may use at most 128 MiB of HBM per device.

v0:
```python
import math

import jax
import jax.numpy as jnp
from jax import lax
from jax.sharding import PartitionSpec as P

NX = 8192
MX = 1024
MY = 1024
STRIDE = 4


precise = lax.Precision.HIGHEST


def phase_table(pos_start, pos_count, pos_total, ang_count, modulus):
    position = pos_start + jnp.arange(pos_count, dtype=jnp.int32) - pos_total // 2
    angles = jnp.arange(ang_count, dtype=jnp.int32) - ang_count // 2
    cycles = jnp.mod(position[:, None] * angles[None, :] * STRIDE, modulus)
    radians = 2.0 * math.pi / modulus * cycles.astype(jnp.float32)
    return (jnp.cos(radians), jnp.sin(radians))


def contract(left, right, left_dim, right_dim):
    return lax.dot_general(
        left,
        right,
        (((left_dim,), (right_dim,)), ((), ())),
        precision=precise,
        preferred_element_type=jnp.float32,
    )


def body(currents, far_gradient):
    row_count = currents.shape[2]
    column_count = currents.shape[3]
    angle_rows = far_gradient.shape[2]
    angle_cols = far_gradient.shape[3]
    total_rows = row_count * lax.axis_size("wide")
    scale = 1.0 / math.sqrt(total_rows * NX)
    row_start = lax.axis_index("wide") * row_count
    column_start = lax.axis_index("narrow") * column_count
    cos_x, sin_x = phase_table(column_start, column_count, NX, MX, NX)
    cos_y, sin_y = phase_table(row_start, row_count, total_rows, MY, NX)
    real_cur = currents[:, 0].reshape(2 * row_count, column_count)
    imag_cur = currents[:, 1].reshape(2 * row_count, column_count)
    cos_block = cos_x
    sin_block = sin_x
    real_term = contract(cos_block, real_cur, 0, 1) + contract(sin_block, imag_cur, 0, 1)
    imag_term = contract(cos_block, imag_cur, 0, 1) - contract(sin_block, real_cur, 0, 1)
    column_sums = lax.psum_scatter(
        jnp.stack([real_term, imag_term], axis=1), "narrow", scatter_dimension=0, tiled=True
    )
    sum_real = column_sums[:, 0].reshape(angle_cols * 2, row_count)
    sum_imag = column_sums[:, 1].reshape(angle_cols * 2, row_count)
    cos_block = cos_y
    sin_block = sin_y
    real_term = contract(cos_block, sum_real, 0, 1) + contract(sin_block, sum_imag, 0, 1)
    imag_term = contract(cos_block, sum_imag, 0, 1) - contract(sin_block, sum_real, 0, 1)
    far_sums = lax.psum_scatter(
        scale * jnp.stack([real_term, imag_term], axis=1), "wide", scatter_dimension=0, tiled=True
    )
    far_field = far_sums.reshape(angle_rows, 2, angle_cols, 2).transpose(3, 1, 0, 2)
    grad_real = far_gradient[:, 0].transpose(1, 2, 0).reshape(angle_rows, angle_cols * 2)
    grad_imag = far_gradient[:, 1].transpose(1, 2, 0).reshape(angle_rows, angle_cols * 2)
    piece_real = lax.all_gather(grad_real, "wide", axis=0, tiled=True)
    piece_imag = lax.all_gather(grad_imag, "wide", axis=0, tiled=True)
    cos_block = cos_y
    sin_block = sin_y
    real_acc = contract(piece_real, cos_block, 0, 1) - contract(piece_imag, sin_block, 0, 1)
    imag_acc = contract(piece_imag, cos_block, 0, 1) + contract(piece_real, sin_block, 0, 1)
    half_real = real_acc
    half_imag = imag_acc
    half_real = half_real.reshape(angle_cols, 2, row_count)
    half_imag = half_imag.reshape(angle_cols, 2, row_count)
    piece_real = lax.all_gather(half_real, "narrow", axis=0, tiled=True)
    piece_imag = lax.all_gather(half_imag, "narrow", axis=0, tiled=True)
    width = piece_real.shape[0]
    flat_real = piece_real.reshape(width, 2 * row_count)
    flat_imag = piece_imag.reshape(width, 2 * row_count)
    cos_block = cos_x
    sin_block = sin_x
    real_acc = contract(flat_real, cos_block, 0, 1) - contract(flat_imag, sin_block, 0, 1)
    imag_acc = contract(flat_imag, cos_block, 0, 1) + contract(flat_real, sin_block, 0, 1)
    back_real = real_acc
    back_imag = imag_acc
    back_real = back_real.reshape(2, row_count, column_count)
    back_imag = back_imag.reshape(2, row_count, column_count)
    aperture_grad = scale * jnp.stack([back_real, back_imag], axis=1)
    return (far_field, aperture_grad)


def solution(mesh):
    in_specs = (P(None, None, "wide", "narrow"), P(None, None, "wide", "narrow"))
    out_specs = (P(None, None, "wide", "narrow"), P(None, None, "wide", "narrow"))
    return jax.shard_map(body, mesh=mesh, in_specs=in_specs, out_specs=out_specs, check_vma=False)
```

profile of v0, /device:TPU:0, one launch (start us, length us, event | category | flops | bytes accessed | tf_op | source)
XLA Modules:
  0.0 513.0 jit_solution(12802548340909733803)
XLA Ops:
  8.0 0.0 all-gather.7.cloned.1.call-start
  8.0 1.1 slice_bitcast_fusion.1
  9.1 0.8 copy.19
  10.0 0.0 all-gather.7.cloned.1.call-update
  10.0 0.0 all-gather.5.cloned.1.call-start
  10.0 0.8 copy.18
  10.9 0.0 all-gather.5.cloned.1.call-update
  10.9 0.0 reduce-scatter.3.cloned.1.call-start
  11.0 3.9 fusion.138
  14.9 45.0 %fusion.9 = f32[1024,256]{1,0:T(8,128)S(1)} fusion(f32[256,2048]{1,0:T(8,128)S(1)} %bitcast.63, s32[1024]{0:T(1024)S(1)} %iota_add_fusion, s32[2048]{0:T(1024)S(1)} %add_add_fusion), kind=kOutput, calls=%fused_computation.12 | convolution fusion | flops 6473908224 | bytes 3158016 | tf_op jit(solution)/shard_map/dot_general | solution.py:26
  59.9 0.0 copy-done
  59.9 45.0 %fusion.11 = f32[1024,256]{1,0:T(8,128)S(1)} fusion(f32[256,2048]{1,0:T(8,128)S(1)} %bitcast.65, s32[1024]{0:T(1024)S(1)} %iota_add_fusion, s32[2048]{0:T(1024)S(1)} %add_add_fusion), kind=kOutput, calls=%fused_computation.13 | convolution fusion | flops 6473908224 | bytes 3158016 | tf_op jit(solution)/shard_map/dot_general | solution.py:26
  104.9 45.7 %fusion.36 = f32[1024,1,256]{2,0,1:T(8,128)S(1)} fusion(f32[1024,256]{1,0:T(8,128)S(1)} %fusion.9, f32[256,2048]{1,0:T(8,128)S(1)} %bitcast.66, s32[1024]{0:T(1024)S(1)} %iota_add_fusion, s32[2048]{0:T(1024)S(1)} %add_add_fusion), kind=kOutput, calls=%fused_computation.26 | convolution fusion | flops 6474170368 | bytes 4206592 | tf_op jit(solution)/shard_map/dot_general | solution.py:26
  150.6 45.9 %fusion.30 = f32[1024,1,256]{2,0,1:T(8,128)S(1)} fusion(f32[1024,256]{1,0:T(8,128)S(1)} %fusion.11, f32[256,2048]{1,0:T(8,128)S(1)} %bitcast.64, s32[1024]{0:T(1024)S(1)} %iota_add_fusion, s32[2048]{0:T(1024)S(1)} %add_add_fusion), kind=kOutput, calls=%fused_computation.24 | convolution fusion | flops 6474170368 | bytes 4206592 | tf_op jit(solution)/shard_map/dot_general | solution.py:26
  196.5 1.5 pad_maximum_fusion
  197.9 0.0 reduce-scatter.3.cloned.1.call-update
  198.0 0.0 all-gather.11.cloned.1.call-start
  198.0 0.0 all-gather.7.cloned.1.call-done
  198.1 5.7 %fusion.46 = f32[128,512]{1,0:T(8,128)S(1)} fusion(f32[1024,512]{0,1:T(8,128)} %all-gather.7.cloned.1.call-done, s32[1024]{0:T(1024)S(1)} %iota_add_fusion, s32[128]{0:T(128)S(1)} %add_add_fusion.1), kind=kOutput, calls=%fused_computation.41 | convolution fusion | flops 807272448 | bytes 2363904 | tf_op jit(solution)/shard_map/dot_general | solution.py:26
  203.8 0.0 all-gather.5.cloned.1.call-done
  203.8 5.7 %fusion.39 = f32[512,128]{0,1:T(8,128)S(1)} fusion(f32[128,512]{1,0:T(8,128)S(1)} %fusion.46, f32[1024,512]{0,1:T(8,128)} %all-gather.5.cloned.1.call-done, s32[1024]{0:T(1024)S(1)} %iota_add_fusion, s32[128]{0:T(128)S(1)} %add_add_fusion.1), kind=kOutput, calls=%fused_computation.28 | convolution fusion | flops 807337984 | bytes 2626048 | tf_op jit(solution)/shard_map/dot_general | solution.py:26
  209.5 0.8 copy.22
  210.3 0.0 all-gather.11.cloned.1.call-update
  210.4 0.0 all-gather.9.cloned.1.call-start
  210.4 5.7 %fusion.48 = f32[128,512]{1,0:T(8,128)S(1)} fusion(f32[1024,512]{0,1:T(8,128)} %all-gather.5.cloned.1.call-done, s32[1024]{0:T(1024)S(1)} %iota_add_fusion, s32[128]{0:T(128)S(1)} %add_add_fusion.1), kind=kOutput, calls=%fused_computation.42 | convolution fusion | flops 807272448 | bytes 2363904 | tf_op jit(solution)/shard_map/dot_general | solution.py:26
  216.1 5.7 %fusion.40 = f32[512,128]{0,1:T(8,128)S(1)} fusion(f32[128,512]{1,0:T(8,128)S(1)} %fusion.48, f32[1024,512]{0,1:T(8,128)} %all-gather.7.cloned.1.call-done, s32[1024]{0:T(1024)S(1)} %iota_add_fusion, s32[128]{0:T(128)S(1)} %add_add_fusion.1), kind=kOutput, calls=%fused_computation.30 | convolution fusion | flops 807337984 | bytes 2626048 | tf_op jit(solution)/shard_map/dot_general | solution.py:26
  221.8 0.8 copy.20
  222.7 0.0 all-gather.9.cloned.1.call-update
  222.7 0.2 reduce-scatter.5.cloned.1.call-start
  222.9 21.3 %reduce-scatter.3.cloned.1.call-done = f32[256,2,256]{2,0,1:T(8,128)} async-done(((f32[1024,2,256]{2,0,1:T(8,128)}), f32[256,2,256]{2,0,1:T(8,128)}) %reduce-scatter.3.cloned.1.call-update) | async-done | bytes 524304 | tf_op jit(solution)/shard_map/reduce_scatter | solution.py:52
  244.3 1.1 fusion.139
  245.4 3.8 fusion.50
  249.2 3.8 subtract_bitcast_fusion
  253.0 3.8 fusion.52
  256.7 4.2 add_bitcast_fusion
  260.9 2.5 maximum_multiply_fusion
  263.4 0.0 reduce-scatter.5.cloned.1.call-update
  263.4 9.9 %all-gather.11.cloned.1.call-done = f32[1024,2,128]{2,1,0:T(2,128)} async-done(((f32[256,2,128]{2,1,0:T(2,128)}), f32[1024,2,128]{2,1,0:T(2,128)}) %all-gather.11.cloned.1.call-update) | async-done | bytes 1048592 | tf_op jit(solution)/shard_map/all_gather | solution.py:78
  273.3 1.5 copy.23
  274.9 27.3 %all-gather.9.cloned.1.call-done = f32[1024,2,128]{2,1,0:T(2,128)} async-done(((f32[256,2,128]{2,1,0:T(2,128)}), f32[1024,2,128]{2,1,0:T(2,128)}) %all-gather.9.cloned.1.call-update) | async-done | bytes 1048592 | tf_op jit(solution)/shard_map/all_gather | solution.py:77
  302.1 1.5 copy.21
  303.6 38.7 %fusion.5 = f32[256,2048]{1,0:T(8,128)S(1)} fusion(f32[1024,256]{0,1:T(8,128)S(1)} %bitcast.69, s32[1024]{0:T(1024)S(1)} %iota_add_fusion, s32[2048]{0:T(1024)S(1)} %add_add_fusion), kind=kOutput, calls=%fused_computation.10 | convolution fusion | flops 6473908224 | bytes 3158016 | tf_op jit(solution)/shard_map/dot_general | solution.py:26
  342.3 52.4 %fusion.7 = f32[256,2048]{1,0:T(8,128)S(1)} fusion(f32[1024,256]{0,1:T(8,128)S(1)} %bitcast.71, s32[1024]{0:T(1024)S(1)} %iota_add_fusion, s32[2048]{0:T(1024)S(1)} %add_add_fusion), kind=kOutput, calls=%fused_computation.11 | convolution fusion | flops 6473908224 | bytes 3158016 | tf_op jit(solution)/shard_map/dot_general | solution.py:26
  394.7 52.8 %fusion.24 = f32[256,2048]{1,0:T(8,128)S(1)} fusion(f32[256,2048]{1,0:T(8,128)S(1)} %fusion.5, f32[1024,256]{0,1:T(8,128)S(1)} %bitcast.72, s32[1024]{0:T(1024)S(1)} %iota_add_fusion, s32[2048]{0:T(1024)S(1)} %add_add_fusion), kind=kOutput, calls=%fused_computation.19 | convolution fusion | flops 6474432512 | bytes 5255168 | tf_op jit(solution)/shard_map/dot_general | solution.py:26
  447.5 53.3 %fusion.21 = f32[256,2048]{1,0:T(8,128)S(1)} fusion(f32[256,2048]{1,0:T(8,128)S(1)} %fusion.7, f32[1024,256]{0,1:T(8,128)S(1)} %bitcast.70, s32[1024]{0:T(1024)S(1)} %iota_add_fusion, s32[2048]{0:T(1024)S(1)} %add_add_fusion), kind=kOutput, calls=%fused_computation.18 | convolution fusion | flops 6474432512 | bytes 5255168 | tf_op jit(solution)/shard_map/dot_general | solution.py:26
  500.8 2.4 maximum_multiply_fusion.1
  503.2 1.2 copy.17
  504.5 1.0 copy.26
  (7 shorter events, 0.1 us)
Async XLA Ops:
  8.0 190.1 %all-gather.7.cloned.1.call-start = ((), (), s32[]{:S(2)}) async-start(), calls=%async_computation.5 | async-start | bytes 2359296 | tf_op jit(solution)/shard_map/all_gather | solution.py:68
  10.0 193.8 %all-gather.5.cloned.1.call-start = ((), (), s32[]{:S(2)}) async-start(), calls=%async_computation.4 | async-start | bytes 2359296 | tf_op jit(solution)/shard_map/all_gather | solution.py:67
  10.9 233.4 %reduce-scatter.3.cloned.1.call-start = ((), (), s32[]{:S(2)}) async-start(), calls=%async_computation.2 | async-start | bytes 2621440 | tf_op jit(solution)/shard_map/reduce_scatter | solution.py:52
  14.9 45.0 %copy-start = (f32[2,1,128,2048]{3,2,1,0:T(8,128)S(1)}, f32[2,1,128,2048]{3,2,1,0:T(8,128)}, u32[]{:S(2)}) copy-start(f32[2,1,128,2048]{3,2,1,0:T(8,128)} %get-tuple-element.6) | copy-start | bytes 6291460
  198.0 75.3 %all-gather.11.cloned.1.call-start = ((), (), s32[]{:S(2)}) async-start(), calls=%async_computation.7 | async-start | bytes 1310720 | tf_op jit(solution)/shard_map/all_gather | solution.py:78
  210.4 91.8 %all-gather.9.cloned.1.call-start = ((), (), s32[]{:S(2)}) async-start(), calls=%async_computation.6 | async-start | bytes 1310720 | tf_op jit(solution)/shard_map/all_gather | solution.py:77
  222.7 280.5 %reduce-scatter.5.cloned.1.call-start = ((), (), s32[]{:S(2)}) async-start(), calls=%async_computation.3 | async-start | bytes 4718592 | tf_op jit(solution)/shard_map/reduce_scatter | solution.py:61
Sparse Core Ops, SparseCore 0:
  11.3 30.8 all-gather.6
  44.1 28.1 all-gather.4
  263.6 50.5 reduce-scatter.4
Sparse Core Ops, SparseCore 1:
  198.1 46.2 reduce-scatter.2
  246.3 27.0 all-gather.10
  274.8 27.3 all-gather.8
where the time goes:
time: 522 us; the launch traced here: 513 us
  matrix products  417 us (80%)
  waiting for transfers between devices  58.7 us (11%)
  between operations  15.8 us (3%)
  local copies, waits for them, and re-layouts  14.7 us (3%)
  other arithmetic  6.38 us (1%)
    dot_general x16, matrix products, contract(): lax.dot_general(left, right, (((left_dim,), (right_dim,)), ((), ())), pre...  417 us
    all_gather x1, waiting for transfers between devices, body(): piece_real = lax.all_gather(half_real, 'narrow', axis=0, tiled=True)  27.3 us
    reduce_scatter x1, waiting for transfers between devices, body(): lax.psum_scatter(jnp.stack([real_term, imag_term], axis=1), 'narrow', sca...  21.3 us
  transfers between devices with their start and end apart: 6, of which 3 were waited for; matrix products, arithmetic and copies ran while one was open for 85% of the time, Pallas kernels for 0%

commit v1 on v0

v1 whole, which is shorter than its diff:
```python
import functools
import math

import jax
import jax.numpy as jnp
import numpy as np
from jax import lax
from jax.experimental import pallas as pl
from jax.experimental.pallas import tpu as pltpu
from jax.sharding import PartitionSpec as P

NX = 8192
MX = 1024
MY = 1024
STRIDE = 4

PERIOD = NX // STRIDE
RADIX = 4
SPAN = PERIOD // RADIX
BANDS = MX // RADIX
LANES = 128
HALF = LANES // 2

f32 = jnp.float32
bf16 = jnp.bfloat16
precise = lax.Precision.HIGHEST


def phase_table(pos_start, pos_count, pos_total, ang_count, modulus):
    position = pos_start + jnp.arange(pos_count, dtype=jnp.int32) - pos_total // 2
    angles = jnp.arange(ang_count, dtype=jnp.int32) - ang_count // 2
    cycles = jnp.mod(position[:, None] * angles[None, :] * STRIDE, modulus)
    radians = 2.0 * math.pi / modulus * cycles.astype(jnp.float32)
    return (jnp.cos(radians), jnp.sin(radians))


def contract(left, right, left_dim, right_dim):
    return lax.dot_general(
        left,
        right,
        (((left_dim,), (right_dim,)), ((), ())),
        precision=precise,
        preferred_element_type=jnp.float32,
    )


def general_body(currents, far_gradient):
    row_count = currents.shape[2]
    column_count = currents.shape[3]
    angle_rows = far_gradient.shape[2]
    angle_cols = far_gradient.shape[3]
    total_rows = row_count * lax.axis_size("wide")
    scale = 1.0 / math.sqrt(total_rows * NX)
    row_start = lax.axis_index("wide") * row_count
    column_start = lax.axis_index("narrow") * column_count
    cos_x, sin_x = phase_table(column_start, column_count, NX, MX, NX)
    cos_y, sin_y = phase_table(row_start, row_count, total_rows, MY, NX)
    real_cur = currents[:, 0].reshape(2 * row_count, column_count)
    imag_cur = currents[:, 1].reshape(2 * row_count, column_count)
    real_term = contract(cos_x, real_cur, 0, 1) + contract(sin_x, imag_cur, 0, 1)
    imag_term = contract(cos_x, imag_cur, 0, 1) - contract(sin_x, real_cur, 0, 1)
    column_sums = lax.psum_scatter(
        jnp.stack([real_term, imag_term], axis=1), "narrow", scatter_dimension=0, tiled=True
    )
    sum_real = column_sums[:, 0].reshape(angle_cols * 2, row_count)
    sum_imag = column_sums[:, 1].reshape(angle_cols * 2, row_count)
    real_term = contract(cos_y, sum_real, 0, 1) + contract(sin_y, sum_imag, 0, 1)
    imag_term = contract(cos_y, sum_imag, 0, 1) - contract(sin_y, sum_real, 0, 1)
    far_sums = lax.psum_scatter(
        scale * jnp.stack([real_term, imag_term], axis=1), "wide", scatter_dimension=0, tiled=True
    )
    far_field = far_sums.reshape(angle_rows, 2, angle_cols, 2).transpose(3, 1, 0, 2)
    grad_real = far_gradient[:, 0].transpose(1, 2, 0).reshape(angle_rows, angle_cols * 2)
    grad_imag = far_gradient[:, 1].transpose(1, 2, 0).reshape(angle_rows, angle_cols * 2)
    piece_real = lax.all_gather(grad_real, "wide", axis=0, tiled=True)
    piece_imag = lax.all_gather(grad_imag, "wide", axis=0, tiled=True)
    half_real = contract(piece_real, cos_y, 0, 1) - contract(piece_imag, sin_y, 0, 1)
    half_imag = contract(piece_imag, cos_y, 0, 1) + contract(piece_real, sin_y, 0, 1)
    half_real = half_real.reshape(angle_cols, 2, row_count)
    half_imag = half_imag.reshape(angle_cols, 2, row_count)
    piece_real = lax.all_gather(half_real, "narrow", axis=0, tiled=True)
    piece_imag = lax.all_gather(half_imag, "narrow", axis=0, tiled=True)
    width = piece_real.shape[0]
    flat_real = piece_real.reshape(width, 2 * row_count)
    flat_imag = piece_imag.reshape(width, 2 * row_count)
    back_real = contract(flat_real, cos_x, 0, 1) - contract(flat_imag, sin_x, 0, 1)
    back_imag = contract(flat_imag, cos_x, 0, 1) + contract(flat_real, sin_x, 0, 1)
    back_real = back_real.reshape(2, row_count, column_count)
    back_imag = back_imag.reshape(2, row_count, column_count)
    aperture_grad = scale * jnp.stack([back_real, back_imag], axis=1)
    return (far_field, aperture_grad)


def halves(table):
    hi = table.astype(np.float32).astype(bf16)
    return hi, (table - hi.astype(np.float64)).astype(np.float32).astype(bf16)


def angle(count_left, left_start, count_right, right_start, period):
    left = np.arange(count_left, dtype=np.int64) + left_start
    right = np.arange(count_right, dtype=np.int64) + right_start
    return 2.0 * np.pi / period * ((left[:, None] * right[None, :]) % period)


def make_tables(shards):
    theta = angle(SPAN, 0, BANDS, -(BANDS // 2), SPAN)
    cos, sin = np.cos(theta), np.sin(theta)
    each = BANDS // shards
    x_table = np.zeros((2, SPAN, shards, 2, each))
    x_table[0, :, :, 0] = cos.reshape(SPAN, shards, each)
    x_table[1, :, :, 0] = sin.reshape(SPAN, shards, each)
    x_table[0, :, :, 1] = -sin.reshape(SPAN, shards, each)
    x_table[1, :, :, 1] = cos.reshape(SPAN, shards, each)
    x_table = x_table.reshape(2 * SPAN, 2 * BANDS)
    y_table = np.concatenate([cos.T, sin.T], axis=0)
    y_back = np.concatenate([cos, sin], axis=0)
    twiddle = angle(RADIX, 0, SPAN, 0, PERIOD)
    cols = RADIX * each
    order = np.zeros((2, cols, RADIX, 2, each))
    for k0 in range(RADIX):
        for j in range(each):
            for part in range(2):
                order[part, RADIX * j + k0, k0, part, j] = 1.0
    order = order.reshape(2 * cols, 2 * cols).astype(bf16)
    return {
        "x": halves(x_table),
        "x_back": halves(np.ascontiguousarray(x_table.T)),
        "y": halves(y_table),
        "y_back": halves(y_back),
        "row_tw": np.concatenate([np.cos(twiddle), np.sin(twiddle)], axis=0).astype(np.float32),
        "col_tw": np.ascontiguousarray(
            np.concatenate([np.cos(twiddle), np.sin(twiddle)], axis=0).T
        ).astype(np.float32),
        "order": order,
        "order_back": np.ascontiguousarray(order.T),
    }


def split(value):
    hi = value.astype(bf16)
    return hi, (value - hi.astype(f32)).astype(bf16)


def dot(left, right):
    return jnp.dot(left, right, preferred_element_type=f32)


def dot3(left, right_hi, right_lo):
    hi, lo = split(left)
    return dot(hi, right_hi) + (dot(lo, right_hi) + dot(hi, right_lo))


def times(tw_cos, tw_sin, real, imag):
    return real * tw_cos + imag * tw_sin, imag * tw_cos - real * tw_sin


def x_kernel(cur, tw, t_hi, t_lo, out):
    rows = cur.shape[2]
    re = [cur[0, 0, :, a * SPAN : (a + 1) * SPAN] for a in range(RADIX)]
    im = [cur[0, 1, :, a * SPAN : (a + 1) * SPAN] for a in range(RADIX)]
    sum_re, dif_re = re[0] + re[2], re[0] - re[2]
    sum_im, dif_im = im[0] + im[2], im[0] - im[2]
    odd_re, gap_re = re[1] + re[3], re[1] - re[3]
    odd_im, gap_im = im[1] + im[3], im[1] - im[3]
    legs = [
        (sum_re + odd_re, sum_im + odd_im),
        (dif_re + gap_im, dif_im - gap_re),
        (sum_re - odd_re, sum_im - odd_im),
        (dif_re - gap_im, dif_im + gap_re),
    ]
    flat = []
    for k0, (real, imag) in enumerate(legs):
        if k0 > 0:
            real, imag = times(tw[k0 : k0 + 1], tw[RADIX + k0 : RADIX + k0 + 1], real, imag)
        flat.append(jnp.concatenate([real, imag], axis=1))
    sums = dot3(jnp.concatenate(flat, axis=0), t_hi[...], t_lo[...])
    for shard in range(out.shape[0]):
        for k0 in range(RADIX):
            out[shard, k0] = sums[k0 * rows : (k0 + 1) * rows, shard * LANES : (shard + 1) * LANES]


def sign_of(shape):
    lane = lax.broadcasted_iota(jnp.int32, shape, len(shape) - 1)
    return jnp.where(lane < HALF, 1.0, -1.0).astype(f32)


def swap(value):
    return pltpu.roll(value, HALF, axis=1)


def y_kernel(scale, col, tw, t_hi, t_lo, out):
    early, late = col[:SPAN], col[SPAN:]
    sign = sign_of(early.shape)
    turned = sign * swap(early)
    flat = []
    for k0, leg in enumerate([late + early, late - turned, late - early, late + turned]):
        if k0 > 0:
            leg = leg * tw[:, k0 : k0 + 1] + (sign * tw[:, RADIX + k0 : RADIX + k0 + 1]) * swap(leg)
        flat.append(leg)
    hi, lo = split(jnp.concatenate(flat, axis=1))
    both = dot(t_hi[...], hi) + (dot(t_hi[...], lo) + dot(t_lo[...], hi))
    half_sign = scale * sign_of((BANDS, LANES))
    for k0 in range(RADIX):
        cos_part = both[:BANDS, k0 * LANES : (k0 + 1) * LANES]
        sin_part = both[BANDS:, k0 * LANES : (k0 + 1) * LANES]
        out[pl.ds(k0, BANDS, stride=RADIX), :] = scale * cos_part + half_sign * swap(sin_part)


def y_back_kernel(scale, grad, tw, t_hi, t_lo, out):
    flat = [grad[pl.ds(k0, BANDS, stride=RADIX), :] for k0 in range(RADIX)]
    hi, lo = split(jnp.concatenate(flat, axis=1))
    both = dot(t_hi[...], hi) + (dot(t_hi[...], lo) + dot(t_lo[...], hi))
    sign = sign_of((SPAN, LANES))
    legs = []
    for k0 in range(RADIX):
        cos_part = both[:SPAN, k0 * LANES : (k0 + 1) * LANES]
        sin_part = both[SPAN:, k0 * LANES : (k0 + 1) * LANES]
        leg = cos_part - sign * swap(sin_part)
        if k0 > 0:
            leg = leg * tw[:, k0 : k0 + 1] - (sign * tw[:, RADIX + k0 : RADIX + k0 + 1]) * swap(leg)
        legs.append(leg)
    even, odd = legs[0] + legs[2], legs[1] + legs[3]
    out[SPAN:, :] = scale * (even + odd)
    out[:SPAN, :] = scale * ((legs[0] - legs[2]) + sign * swap(legs[1] - legs[3]))


def x_back_kernel(shards, place, *refs):
    own, rights, lefts = refs[0], refs[1:shards], refs[shards : 2 * shards - 1]
    tw, t_hi, t_lo, _, out, hi_ref, lo_ref = refs[2 * shards - 1 :]
    rows = own.shape[1]
    me = place[0]
    for step in range(shards):
        block = own[...] if step == 0 else lefts[step - 1][...] + rights[shards - 1 - step][...]
        hi, lo = split(block.reshape(RADIX * rows, LANES))
        at = pl.ds(pl.multiple_of(lax.rem(me + step, shards) * LANES, LANES), LANES)
        hi_ref[:, at] = hi
        lo_ref[:, at] = lo
    hi, lo = hi_ref[...], lo_ref[...]
    sums = dot(hi, t_hi[...]) + (dot(lo, t_hi[...]) + dot(hi, t_lo[...]))
    legs = []
    for k0 in range(RADIX):
        real = sums[k0 * rows : (k0 + 1) * rows, :SPAN]
        imag = sums[k0 * rows : (k0 + 1) * rows, SPAN:]
        if k0 > 0:
            real, imag = times(tw[k0 : k0 + 1], -tw[RADIX + k0 : RADIX + k0 + 1], real, imag)
        legs.append((real, imag))
    (r0, i0), (r1, i1), (r2, i2), (r3, i3) = legs
    even_r, even_i, gap_r, gap_i = r0 + r2, i0 + i2, r0 - r2, i0 - i2
    odd_r, odd_i, skew_r, skew_i = r1 + r3, i1 + i3, r1 - r3, i1 - i3
    results = [
        (even_r + odd_r, even_i + odd_i),
        (gap_r - skew_i, gap_i + skew_r),
        (even_r - odd_r, even_i - odd_i),
        (gap_r + skew_i, gap_i - skew_r),
    ]
    for a, (real, imag) in enumerate(results):
        out[0, 0, :, a * SPAN : (a + 1) * SPAN] = real
        out[0, 1, :, a * SPAN : (a + 1) * SPAN] = imag


def moved(value, order):
    hi = value.astype(bf16)
    rest = value - hi.astype(f32)
    mid = rest.astype(bf16)
    lo = (rest - mid.astype(f32)).astype(bf16)
    return dot(hi, order) + (dot(mid, order) + dot(lo, order))


def sort_kernel(grad, order, out):
    for component in range(2):
        flat = jnp.concatenate([grad[component, 0], grad[component, 1]], axis=1)
        sorted_ = moved(flat, order[...])
        for k0 in range(RADIX):
            out[component * RADIX + k0] = sorted_[:, k0 * LANES : (k0 + 1) * LANES]


def unsort_kernel(blocks, order, out):
    cols = out.shape[3]
    for component in range(2):
        flat = jnp.concatenate([blocks[component * RADIX + k0] for k0 in range(RADIX)], axis=1)
        far = moved(flat, order[...])
        out[component, 0] = far[:, :cols]
        out[component, 1] = far[:, cols:]


PARAMS = pltpu.CompilerParams(vmem_limit_bytes=40 * 1024 * 1024)


def cost(macs, nbytes):
    return pl.CostEstimate(flops=2 * macs, bytes_accessed=nbytes, transcendentals=0)


def whole(kernel, shape, *args, macs=1 << 28):
    return pl.pallas_call(
        kernel,
        out_shape=jax.ShapeDtypeStruct(shape, f32),
        in_specs=[pl.BlockSpec(memory_space=pltpu.VMEM)] * len(args),
        out_specs=pl.BlockSpec(memory_space=pltpu.VMEM),
        compiler_params=PARAMS,
        cost_estimate=cost(macs, 1 << 22),
    )(*args)


def fixed(shape):
    return pl.BlockSpec(shape, lambda *_: (0,) * len(shape))


def project_x(currents, component, shards, tables):
    rows, columns = currents.shape[2:]
    tile = rows // 2
    t_hi, t_lo = tables["x"]
    return pl.pallas_call(
        x_kernel,
        grid=(rows // tile,),
        out_shape=jax.ShapeDtypeStruct((shards, RADIX, rows, LANES), f32),
        in_specs=[
            pl.BlockSpec((1, 2, tile, columns), lambda i: (component, 0, i, 0)),
            fixed((2 * RADIX, SPAN)),
            fixed(t_hi.shape),
            fixed(t_lo.shape),
        ],
        out_specs=pl.BlockSpec((shards, RADIX, tile, LANES), lambda i: (0, 0, i, 0)),
        compiler_params=PARAMS,
        cost_estimate=cost(RADIX * rows * 3 * t_hi.size, 8 << 20),
    )(currents, tables["row_tw"], t_hi, t_lo)


def back_x(place, parts, component, grad, shape, tables):
    shards = (len(parts) + 1) // 2
    rows = shape[2]
    tile = rows // 2
    t_hi, t_lo = tables["x_back"]
    block = pl.BlockSpec((RADIX, tile, LANES), lambda i, _: (0, i, 0))
    first = grad is None
    kernel = functools.partial(x_back_kernel, shards)
    if first:
        grad = tables["row_tw"]
    return pl.pallas_call(
        kernel,
        grid_spec=pltpu.PrefetchScalarGridSpec(
            num_scalar_prefetch=1,
            grid=(rows // tile,),
            in_specs=[block] * len(parts)
            + [
                fixed((2 * RADIX, SPAN)),
                fixed(t_hi.shape),
                fixed(t_lo.shape),
                pl.BlockSpec(memory_space=pl.ANY),
            ],
            out_specs=pl.BlockSpec((1, 2, tile, shape[3]), lambda i, _: (component, 0, i, 0)),
            scratch_shapes=[
                pltpu.VMEM((RADIX * tile, 2 * BANDS), bf16),
                pltpu.VMEM((RADIX * tile, 2 * BANDS), bf16),
            ],
        ),
        out_shape=jax.ShapeDtypeStruct(shape, f32),
        input_output_aliases={} if first else {1 + len(parts) + 3: 0},
        compiler_params=PARAMS,
        cost_estimate=cost(RADIX * rows * 3 * t_hi.size, 8 << 20),
    )(place, *parts, tables["row_tw"], t_hi, t_lo, grad)


def line_sum(blocks, shards):
    me = lax.axis_index("narrow")

    def pick(index):
        return lax.dynamic_index_in_dim(blocks, jnp.clip(index, 0, shards - 1), 0, False)

    right = left = None
    for step in range(shards - 1):
        to_right = pick(me + shards - 1 - step)
        to_left = pick(me - (shards - 1 - step))
        if step > 0:
            to_right, to_left = to_right + right, to_left + left
        right = lax.ppermute(to_right, "narrow", [(i, i + 1) for i in range(step + 1)])
        left = lax.ppermute(
            to_left, "narrow", [(shards - 1 - i, shards - 2 - i) for i in range(step + 1)]
        )
    return pick(me) + (right + left)


def line_gather(block, shards):
    rights, lefts = [], []
    right = left = block
    for step in range(shards - 1):
        right = lax.ppermute(right, "narrow", [(i, i + 1) for i in range(step, shards - 1)])
        left = lax.ppermute(left, "narrow", [(i + 1, i) for i in range(shards - 1 - step)])
        rights.append(right)
        lefts.append(left)
    return [block, *rights, *lefts]


def fast_body(tables, currents, far_gradient):
    shards = lax.axis_size("narrow")
    wide = lax.axis_size("wide")
    rows = currents.shape[2]
    angle_rows = far_gradient.shape[2]
    scale = 1.0 / math.sqrt(rows * wide * NX)
    place = lax.axis_index("narrow").astype(jnp.int32).reshape(1)
    y_hi, y_lo = tables["y"]
    b_hi, b_lo = tables["y_back"]

    sums = [project_x(currents, c, shards, tables) for c in range(2)]
    sorted_ = whole(sort_kernel, (2 * RADIX, angle_rows, LANES), far_gradient, tables["order"])

    rows_in = lax.all_to_all(sorted_, "wide", 0, 0).reshape(MY, LANES)
    rows_out = whole(
        functools.partial(y_back_kernel, scale), (rows * wide, LANES), rows_in, tables["col_tw"], b_hi, b_lo
    )
    half = lax.all_to_all(rows_out.reshape(wide, rows, LANES), "wide", 0, 0)

    columns = jnp.concatenate([line_sum(s, shards) for s in sums], axis=0)
    rows_in = lax.all_to_all(columns, "wide", 0, 0).reshape(rows * wide, LANES)
    rows_out = whole(
        functools.partial(y_kernel, scale), (MY, LANES), rows_in, tables["col_tw"], y_hi, y_lo
    )
    far = lax.all_to_all(rows_out.reshape(wide, angle_rows, LANES), "wide", 0, 0)
    far_field = whole(unsort_kernel, far_gradient.shape, far, tables["order_back"])

    grad = None
    for c in range(2):
        parts = line_gather(half[c * RADIX : (c + 1) * RADIX], shards)
        grad = back_x(place, parts, c, grad, currents.shape, tables)
    return (far_field, grad)


def solution(mesh):
    spec = P(None, None, "wide", "narrow")
    shards, wide = mesh.shape["narrow"], mesh.shape["wide"]

    def run(currents, far_gradient):
        rows = currents.shape[2]
        fits = (
            currents.shape[3] == shards * PERIOD
            and rows == 2 * SPAN
            and far_gradient.shape[2] == MY == 2 * SPAN
            and BANDS // shards == HALF
            and wide == 2 * RADIX
        )
        body = functools.partial(fast_body, make_tables(shards)) if fits else general_body
        return jax.shard_map(
            body, mesh=mesh, in_specs=(spec, spec), out_specs=(spec, spec), check_vma=False
        )(currents, far_gradient)

    return run
```

time: 522 us -> 138 us (0.26); the launches traced: 513 us -> 136 us
  matrix products: 417 us -> 0 us
  starting transfers between devices: 0.43 us -> 74 us
  waiting for transfers between devices: 58.7 us -> 11.1 us
  Pallas kernels: 0 us -> 22.6 us
  between operations: 15.8 us -> 0.95 us
  other arithmetic: 6.38 us -> 13.6 us
    dot_general x16 -> x0, matrix products: 417 us -> none  [contract(): lax.dot_general(left, right, (((left_dim,), (right_dim,)), ((), ())), pre...]
    ppermute x0 -> x24, starting transfers between devices: none -> 57.8 us  [the longest x6 26.5 us: line_sum(): lax.ppermute(to_right, 'narrow', [(i, i + 1) for i in range(step + 1)])]
    all_gather x4 -> x0, waiting for transfers between devices: 37.2 us -> none  [the longest x1 27.3 us: body(): piece_real = lax.all_gather(half_real, 'narrow', axis=0, tiled=True)]
    pallas_call x0 -> x8, Pallas kernels: none -> 22.6 us  [the longest x2 9 us: back_x(): pl.pallas_call(kernel, grid_spec=pltpu.PrefetchScalarGridSpec(num_scalar_...]
    reduce_scatter x2 -> x0, waiting for transfers between devices: 21.3 us -> none  [the longest x1 21.3 us: body(): lax.psum_scatter(jnp.stack([real_term, imag_term], axis=1), 'narrow', sca...]
    all_to_all x0 -> x4, starting transfers between devices: none -> 16.3 us  [the longest x1 4.2 us: fast_body(): rows_in = lax.all_to_all(columns, 'wide', 0, 0).reshape(rows * wide, LANES)]
    add x0 -> x8, other arithmetic: none -> 12.7 us  [the longest x6 10.5 us: line_sum(): to_right, to_left = (to_right + right, to_left + left)]
    ppermute x0 -> x24, waiting for transfers between devices: none -> 11.1 us  [the longest x6 11 us: line_gather(): lax.ppermute(left, 'narrow', [(i + 1, i) for i in range(shards - 1 - step)])]
  transfers between devices with their start and end apart: 6 -> 28, of which waited for: 3 -> 3; matrix products, arithmetic and copies ran while one was open for 85% -> 12% of each run, Pallas kernels for 0% -> 13%
where the time goes in v1:
time: 138 us; the launch traced here: 136 us
  starting transfers between devices  74 us (54%)
  Pallas kernels  22.6 us (16%)
  local copies, waits for them, and re-layouts  14.1 us (10%)
  other arithmetic  13.6 us (10%)
  waiting for transfers between devices  11.1 us (8%)
    ppermute x6, starting transfers between devices, line_sum(): lax.ppermute(to_right, 'narrow', [(i, i + 1) for i in range(step + 1)])  26.5 us
    ppermute x6, starting transfers between devices, line_gather(): lax.ppermute(right, 'narrow', [(i, i + 1) for i in range(step, shards - 1)])  15.3 us
    ppermute x6, waiting for transfers between devices, line_gather(): lax.ppermute(left, 'narrow', [(i + 1, i) for i in range(shards - 1 - step)])  11 us
    unnamed x32, local copies, waits for them, and re-layouts  10.6 us
    add x6, other arithmetic, line_sum(): to_right, to_left = (to_right + right, to_left + left)  10.5 us
    pallas_call x2, Pallas kernels, back_x(): pl.pallas_call(kernel, grid_spec=pltpu.PrefetchScalarGridSpec(num_scalar_...  9 us
    pallas_call x4, Pallas kernels, whole(): pl.pallas_call(kernel, out_shape=jax.ShapeDtypeStruct(shape, f32), in_spe...  8.92 us
    ppermute x6, starting transfers between devices, line_sum(): lax.ppermute(to_left, 'narrow', [(shards - 1 - i, shards - 2 - i) for i i...  8.16 us
  transfers between devices with their start and end apart: 28, of which 3 were waited for; matrix products, arithmetic and copies ran while one was open for 12% of the time, Pallas kernels for 13%

profile of v1, /device:TPU:0, one launch (start us, length us, event | category | flops | bytes accessed | tf_op | source)
XLA Modules:
  0.0 136.4 jit_solution(4189459680856964003)
XLA Ops:
  0.6 2.2 %copy-done = f32[2,2,128,2048]{3,2,1,0:T(8,128)S(1)} copy-done((f32[2,2,128,2048]{3,2,1,0:T(8,128)S(1)}, f32[2,2,128,2048]{3,2,1,0:T(8,128)}, u32[]{:S(2)}) %copy-start) | copy-done | bytes 4194328
  2.8 1.2 copy-done.1
  4.1 1.2 copy-done.2
  6.0 2.4 %shard_map.150 = f32[4,4,128,128]{3,2,1,0:T(8,128)S(1)} custom-call(f32[2,2,128,2048]{3,2,1,0:T(8,128)S(1)} %copy-done, f32[8,512]{1,0:T(8,128)S(1)} %copy-done.11, bf16[1024,512]{1,0:T(8,128)(2,1)S(1)} %copy-done.2, bf16[1024,512]{1,0:T(8,128)(2,1)S(1)} %copy-done.1), custom_call_target="tpu_custom_call" | custom-call | flops 1610612736 | bytes 8388608 | tf_op jit(solution)/shard_map/pallas_call | solution.py:312
  9.2 1.5 %collective-permute-start.9 = (f32[4,128,128]{2,1,0:T(8,128)}, f32[4,128,128]{2,1,0:T(8,128)}, u32[]{:S(2)}, u32[]{:S(2)}) collective-permute-start(f32[4,128,128]{2,1,0:T(8,128)} %get-tuple-element.8), channel_id=1, source_target_pairs={{3,2},{7,6},{11,10},{15,14},{19,18},{23,22},{27,26},{31,30}} | collective-permute-start | bytes 786440 | tf_op jit(solution)/shard_map/ppermute | solution.py:376
  10.7 2.4 %shard_map.149 = f32[4,4,128,128]{3,2,1,0:T(8,128)S(1)} custom-call(f32[2,2,128,2048]{3,2,1,0:T(8,128)S(1)} %copy-done, f32[8,512]{1,0:T(8,128)S(1)} %copy-done.11, bf16[1024,512]{1,0:T(8,128)(2,1)S(1)} %copy-done.2, bf16[1024,512]{1,0:T(8,128)(2,1)S(1)} %copy-done.1), custom_call_target="tpu_custom_call" | custom-call | flops 1610612736 | bytes 8388608 | tf_op jit(solution)/shard_map/pallas_call | solution.py:312
  13.9 1.4 %collective-permute-start.3 = (f32[4,128,128]{2,1,0:T(8,128)}, f32[4,128,128]{2,1,0:T(8,128)}, u32[]{:S(2)}, u32[]{:S(2)}) collective-permute-start(f32[4,128,128]{2,1,0:T(8,128)} %get-tuple-element.4), channel_id=1, source_target_pairs={{3,2},{7,6},{11,10},{15,14},{19,18},{23,22},{27,26},{31,30}} | collective-permute-start | bytes 786440 | tf_op jit(solution)/shard_map/ppermute | solution.py:376
  15.3 5.6 %collective-permute-start.6 = (f32[4,128,128]{2,1,0:T(8,128)}, f32[4,128,128]{2,1,0:T(8,128)}, u32[]{:S(2)}, u32[]{:S(2)}) collective-permute-start(f32[4,128,128]{2,1,0:T(8,128)} %get-tuple-element.9), channel_id=1, source_target_pairs={{0,1},{4,5},{8,9},{12,13},{16,17},{20,21},{24,25},{28,29}} | collective-permute-start | bytes 786440 | tf_op jit(solution)/shard_map/ppermute | solution.py:375
  20.9 2.0 %collective-permute-start = (f32[4,128,128]{2,1,0:T(8,128)}, f32[4,128,128]{2,1,0:T(8,128)}, u32[]{:S(2)}, u32[]{:S(2)}) collective-permute-start(f32[4,128,128]{2,1,0:T(8,128)} %get-tuple-element.5), channel_id=1, source_target_pairs={{0,1},{4,5},{8,9},{12,13},{16,17},{20,21},{24,25},{28,29}} | collective-permute-start | bytes 786440 | tf_op jit(solution)/shard_map/ppermute | solution.py:375
  22.9 1.7 %bitcast_add_fusion = f32[4,128,128]{2,1,0:T(8,128)} fusion(f32[4,128,128]{2,1,0:T(8,128)} %collective-permute-done.9, f32[4,4,128,128]{3,2,1,0:T(8,128)S(1)} %shard_map.150, s32[]{:T(128)S(6)} %min.34), kind=kLoop, calls=%fused_computation.1 | loop fusion | flops 65536 | bytes 786436 | tf_op jit(solution)/shard_map/add | solution.py:374
  24.6 1.4 collective-permute-start.10
  26.0 1.7 %bitcast_add_fusion.5 = f32[4,128,128]{2,1,0:T(8,128)} fusion(f32[4,128,128]{2,1,0:T(8,128)} %collective-permute-done.3, f32[4,4,128,128]{3,2,1,0:T(8,128)S(1)} %shard_map.149, s32[]{:T(128)S(6)} %min.34), kind=kLoop, calls=%fused_computation.6 | loop fusion | flops 65536 | bytes 786436 | tf_op jit(solution)/shard_map/add | solution.py:374
  27.6 1.4 %collective-permute-start.4 = (f32[4,128,128]{2,1,0:T(8,128)}, f32[4,128,128]{2,1,0:T(8,128)}, u32[]{:S(2)}, u32[]{:S(2)}) collective-permute-start(f32[4,128,128]{2,1,0:T(8,128)} %bitcast_add_fusion.5), channel_id=1, source_target_pairs={{3,2},{2,1},{7,6},{6,5},{11,10},{10,9},{15,14},{14,13},{19,18},{18... | collective-permute-start | bytes 786440 | tf_op jit(solution)/shard_map/ppermute | solution.py:376
  30.0 1.4 %shard_map.153 = f32[8,128,128]{2,1,0:T(8,128)} custom-call(f32[2,2,128,256]{3,2,1,0:T(8,128)S(1)} %copy-done.13, bf16[512,512]{1,0:T(8,128)(2,1)S(1)} %copy-done.15), custom_call_target="tpu_custom_call" | custom-call | flops 536870912 | bytes 4194304 | tf_op jit(solution)/shard_map/pallas_call | solution.py:294
  31.4 3.7 %all-to-all-start.2 = ((f32[8,128,128]{2,1,0:T(8,128)}), f32[8,128,128]{2,1,0:T(8,128)S(1)}, u32[]{:S(2)}, u32[]{:S(2)}) async-start(f32[8,128,128]{2,1,0:T(8,128)} %shard_map.153), calls=%async_computation.2 | async-start | bytes 1048576 | tf_op jit(solution)/shard_map/all_to_all | solution.py:406
  35.2 1.9 %bitcast_add_fusion.1 = (f32[4,128,128]{2,1,0:T(8,128)}, f32[4,128,128]{2,1,0:T(8,128)}) fusion(f32[4,128,128]{2,1,0:T(8,128)} %collective-permute-done.10, f32[4,4,128,128]{3,2,1,0:T(8,128)S(1)} %shard_map.150, s32[]{:T(128)S(6)} %min.33, f32[4,128,128]{2,1,0:T(8,128)} %collective-permute-done.6, s32[]{:T(128)S(6)} %min.31), kind=kLoop, calls=%fused_computation.2 | loop fusion | flops 131072 | bytes 1572872 | tf_op jit(solution)/shard_map/add | solution.py:374
  37.1 2.0 %collective-permute-start.7 = (f32[4,128,128]{2,1,0:T(8,128)}, f32[4,128,128]{2,1,0:T(8,128)}, u32[]{:S(2)}, u32[]{:S(2)}) collective-permute-start(f32[4,128,128]{2,1,0:T(8,128)} %get-tuple-element.7), channel_id=1, source_target_pairs={{0,1},{1,2},{4,5},{5,6},{8,9},{9,10},{12,13},{13,14},{16,17},{17,1... | collective-permute-start | bytes 786440 | tf_op jit(solution)/shard_map/ppermute | solution.py:375
  39.1 1.9 %bitcast_add_fusion.6 = (f32[4,128,128]{2,1,0:T(8,128)}, f32[4,128,128]{2,1,0:T(8,128)}) fusion(f32[4,128,128]{2,1,0:T(8,128)} %collective-permute-done.4, f32[4,4,128,128]{3,2,1,0:T(8,128)S(1)} %shard_map.149, s32[]{:T(128)S(6)} %min.33, f32[4,128,128]{2,1,0:T(8,128)} %collective-permute-done, s32[]{:T(128)S(6)} %min.31), kind=kLoop, calls=%fused_computation.7 | loop fusion | flops 131072 | bytes 1572872 | tf_op jit(solution)/shard_map/add | solution.py:374
  41.0 6.9 %collective-permute-start.1 = (f32[4,128,128]{2,1,0:T(8,128)}, f32[4,128,128]{2,1,0:T(8,128)}, u32[]{:S(2)}, u32[]{:S(2)}) collective-permute-start(f32[4,128,128]{2,1,0:T(8,128)} %get-tuple-element.3), channel_id=1, source_target_pairs={{0,1},{1,2},{4,5},{5,6},{8,9},{9,10},{12,13},{13,14},{16,17},{17,1... | collective-permute-start | bytes 786440 | tf_op jit(solution)/shard_map/ppermute | solution.py:375
  48.9 2.3 %shard_map.154 = f32[1024,128]{1,0:T(8,128)} custom-call(f32[1024,128]{1,0:T(8,128)S(1)} %bitcast.33, f32[512,8]{1,0:T(8,128)S(1)} %copy-done.5, bf16[1024,256]{1,0:T(8,128)(2,1)S(1)} %copy-done.10, bf16[1024,256]{1,0:T(8,128)(2,1)S(1)} %copy-done.9), custom_call_target="tpu_custom_call" | custom-call | flops 536870912 | bytes 4194304 | tf_op jit(solution)/shard_map/pallas_call | solution.py:294
  51.2 4.2 %all-to-all-start.3 = ((f32[8,128,128]{2,1,0:T(8,128)}), f32[8,128,128]{2,1,0:T(8,128)}, u32[]{:S(2)}, u32[]{:S(2)}) async-start(f32[8,128,128]{2,1,0:T(8,128)} %bitcast.18), calls=%async_computation.3 | async-start | bytes 1048576 | tf_op jit(solution)/shard_map/all_to_all | solution.py:410
  55.4 1.3 collective-permute-start.11
  56.7 1.3 collective-permute-start.5
  58.0 1.7 %bitcast_add_fusion.3 = f32[4,128,128]{2,1,0:T(8,128)} fusion(f32[4,128,128]{2,1,0:T(8,128)} %collective-permute-done.7, f32[4,4,128,128]{3,2,1,0:T(8,128)S(1)} %shard_map.150, s32[]{:T(128)S(6)} %min.30), kind=kLoop, calls=%fused_computation.4 | loop fusion | flops 65536 | bytes 786436 | tf_op jit(solution)/shard_map/add | solution.py:374
  59.7 5.9 %collective-permute-start.8 = (f32[4,128,128]{2,1,0:T(8,128)}, f32[4,128,128]{2,1,0:T(8,128)}, u32[]{:S(2)}, u32[]{:S(2)}) collective-permute-start(f32[4,128,128]{2,1,0:T(8,128)} %bitcast_add_fusion.3), channel_id=1, source_target_pairs={{0,1},{1,2},{2,3},{4,5},{5,6},{6,7},{8,9},{9,10},{10,11},{12,13},{... | collective-permute-start | bytes 786440 | tf_op jit(solution)/shard_map/ppermute | solution.py:375
  65.6 1.7 %bitcast_add_fusion.8 = f32[4,128,128]{2,1,0:T(8,128)} fusion(f32[4,128,128]{2,1,0:T(8,128)} %collective-permute-done.1, f32[4,4,128,128]{3,2,1,0:T(8,128)S(1)} %shard_map.149, s32[]{:T(128)S(6)} %min.30), kind=kLoop, calls=%fused_computation.9 | loop fusion | flops 65536 | bytes 786436 | tf_op jit(solution)/shard_map/add | solution.py:374
  67.2 4.1 %collective-permute-start.2 = (f32[4,128,128]{2,1,0:T(8,128)}, f32[4,128,128]{2,1,0:T(8,128)}, u32[]{:S(2)}, u32[]{:S(2)}) collective-permute-start(f32[4,128,128]{2,1,0:T(8,128)} %bitcast_add_fusion.8), channel_id=1, source_target_pairs={{0,1},{1,2},{2,3},{4,5},{5,6},{6,7},{8,9},{9,10},{10,11},{12,13},{... | collective-permute-start | bytes 786440 | tf_op jit(solution)/shard_map/ppermute | solution.py:375
  71.3 1.9 %fusion = (f32[4,128,128]{2,1,0:T(8,128)}, f32[4,128,128]{2,1,0:T(8,128)}) fusion(f32[8,128,128]{2,1,0:T(8,128)} %all-to-all-done.3), kind=kLoop, calls=%fused_computation.15 | loop fusion | bytes 1048576 | tf_op jit(solution)/shard_map/slice | solution.py:422
  73.2 1.3 collective-permute-start.21
  74.5 5.3 %collective-permute-start.18 = (f32[4,128,128]{2,1,0:T(8,128)}, f32[4,128,128]{2,1,0:T(8,128)}, u32[]{:S(2)}, u32[]{:S(2)}) collective-permute-start(f32[4,128,128]{2,1,0:T(8,128)} %get-tuple-element.10.refs_0_), channel_id=1, source_target_pairs={{0,1},{1,2},{2,3},{4,5},{5,6},{6,7},{8,9},{9,10},{10,11},{12,13},{... | collective-permute-start | bytes 786440 | tf_op jit(solution)/shard_map/ppermute | solution.py:386
  82.8 4.2 %all-to-all-start = ((f32[8,128,128]{2,1,0:T(8,128)}), f32[8,128,128]{2,1,0:T(8,128)S(1)}, u32[]{:S(2)}, u32[]{:S(2)}) async-start(f32[8,128,128]{2,1,0:T(8,128)} %pad_maximum_fusion), calls=%async_computation | async-start | bytes 1048576 | tf_op jit(solution)/shard_map/all_to_all | solution.py:413
  87.0 1.3 collective-permute-start.15
  88.3 5.3 %collective-permute-start.12 = (f32[4,128,128]{2,1,0:T(8,128)}, f32[4,128,128]{2,1,0:T(8,128)}, u32[]{:S(2)}, u32[]{:S(2)}) collective-permute-start(f32[4,128,128]{2,1,0:T(8,128)} %get-tuple-element.11.refs_0_), channel_id=1, source_target_pairs={{0,1},{1,2},{2,3},{4,5},{5,6},{6,7},{8,9},{9,10},{10,11},{12,13},{... | collective-permute-start | bytes 786440 | tf_op jit(solution)/shard_map/ppermute | solution.py:386
  93.6 1.3 collective-permute-start.22
  94.9 1.4 %collective-permute-start.19 = (f32[4,128,128]{2,1,0:T(8,128)}, f32[4,128,128]{2,1,0:T(8,128)}, u32[]{:S(2)}, u32[]{:S(2)}) collective-permute-start(f32[4,128,128]{2,1,0:T(8,128)} %collective-permute-done.18.refs_1_), channel_id=1, source_target_pairs={{1,2},{2,3},{5,6},{6,7},{9,10},{10,11},{13,14},{14,15},{17,18},{18... | collective-permute-start | bytes 786440 | tf_op jit(solution)/shard_map/ppermute | solution.py:386
  96.3 1.7 %collective-permute-done.15.refs_4_ = f32[4,128,128]{2,1,0:T(8,128)} collective-permute-done((f32[4,128,128]{2,1,0:T(8,128)}, f32[4,128,128]{2,1,0:T(8,128)}, u32[]{:S(2)}, u32[]{:S(2)}) %collective-permute-start.15) | collective-permute-done | bytes 262176 | tf_op jit(solution)/shard_map/ppermute | solution.py:387
  98.0 1.3 collective-permute-start.16
  99.3 1.4 %collective-permute-start.13 = (f32[4,128,128]{2,1,0:T(8,128)}, f32[4,128,128]{2,1,0:T(8,128)}, u32[]{:S(2)}, u32[]{:S(2)}) collective-permute-start(f32[4,128,128]{2,1,0:T(8,128)} %collective-permute-done.12.refs_1_), channel_id=1, source_target_pairs={{1,2},{2,3},{5,6},{6,7},{9,10},{10,11},{13,14},{14,15},{17,18},{18... | collective-permute-start | bytes 786440 | tf_op jit(solution)/shard_map/ppermute | solution.py:386
  100.6 4.3 %collective-permute-done.22.refs_5_ = f32[4,128,128]{2,1,0:T(8,128)} collective-permute-done((f32[4,128,128]{2,1,0:T(8,128)}, f32[4,128,128]{2,1,0:T(8,128)}, u32[]{:S(2)}, u32[]{:S(2)}) %collective-permute-start.22) | collective-permute-done | bytes 262176 | tf_op jit(solution)/shard_map/ppermute | solution.py:387
  105.0 1.3 collective-permute-start.23
  106.3 1.4 %collective-permute-start.20 = (f32[4,128,128]{2,1,0:T(8,128)}, f32[4,128,128]{2,1,0:T(8,128)}, u32[]{:S(2)}, u32[]{:S(2)}) collective-permute-start(f32[4,128,128]{2,1,0:T(8,128)} %collective-permute-done.19.refs_2_), channel_id=1, source_target_pairs={{2,3},{6,7},{10,11},{14,15},{18,19},{22,23},{26,27},{30,31}} | collective-permute-start | bytes 786440 | tf_op jit(solution)/shard_map/ppermute | solution.py:386
  109.7 2.8 %shard_map.151 = f32[1024,128]{1,0:T(8,128)} custom-call(f32[1024,128]{1,0:T(8,128)S(1)} %bitcast.34, f32[512,8]{1,0:T(8,128)S(1)} %copy-done.5, bf16[512,512]{1,0:T(8,128)(2,1)S(1)} %copy-done.8, bf16[512,512]{1,0:T(8,128)(2,1)S(1)} %copy-done.7), custom_call_target="tpu_custom_call" | custom-call | flops 536870912 | bytes 4194304 | tf_op jit(solution)/shard_map/pallas_call | solution.py:294
  112.6 4.2 %all-to-all-start.1 = ((f32[8,128,128]{2,1,0:T(8,128)}), f32[8,128,128]{2,1,0:T(8,128)}, u32[]{:S(2)}, u32[]{:S(2)}) async-start(f32[8,128,128]{2,1,0:T(8,128)} %bitcast.15), calls=%async_computation.1 | async-start | bytes 1048576 | tf_op jit(solution)/shard_map/all_to_all | solution.py:417
  116.7 1.4 %collective-permute-start.17 = (f32[4,128,128]{2,1,0:T(8,128)}, f32[4,128,128]{2,1,0:T(8,128)S(1)}, u32[]{:S(2)}, u32[]{:S(2)}) collective-permute-start(f32[4,128,128]{2,1,0:T(8,128)} %collective-permute-done.16.refs_5_), channel_id=1, source_target_pairs={{1,0},{5,4},{9,8},{13,12},{17,16},{21,20},{25,24},{29,28}} | collective-permute-start | bytes 786440 | tf_op jit(solution)/shard_map/ppermute | solution.py:387
  118.9 4.6 %shard_map.155.refs_10_ = f32[2,2,128,2048]{3,2,1,0:T(8,128)} custom-call(s32[1]{0:T(128)} %bitcast.16.place, f32[4,128,128]{2,1,0:T(8,128)} %get-tuple-element.10.refs_0_, f32[4,128,128]{2,1,0:T(8,128)} %collective-permute-done.18.refs_1_, f32[4,128,128]{2,1,0:T(8,128)} %collective-permute-done.19.refs_2_, f32[4,128,128]{2,1,0:T(8,128)} %collective-permute-done.20.refs_3_, ...), custom_call_target="tpu_custom_call" | custom-call | flops 1610612736 | bytes 8388608 | tf_op jit(solution)/shard_map/pallas_call | solution.py:338
  123.5 5.0 %collective-permute-done.17.refs_6_ = f32[4,128,128]{2,1,0:T(8,128)S(1)} collective-permute-done((f32[4,128,128]{2,1,0:T(8,128)}, f32[4,128,128]{2,1,0:T(8,128)S(1)}, u32[]{:S(2)}, u32[]{:S(2)}) %collective-permute-start.17) | collective-permute-done | bytes 262176 | tf_op jit(solution)/shard_map/ppermute | solution.py:387
  128.5 4.4 %shard_map.156 = f32[2,2,128,2048]{3,2,1,0:T(8,128)} custom-call(s32[1]{0:T(128)} %bitcast.16.place, f32[4,128,128]{2,1,0:T(8,128)S(1)} %copy-done.6, f32[4,128,128]{2,1,0:T(8,128)} %collective-permute-done.12.refs_1_, f32[4,128,128]{2,1,0:T(8,128)} %collective-permute-done.13.refs_2_, ...), custom_call_target="tpu_custom_call", output_to_operand_aliasing={{}: (11, {})} | custom-call | flops 1610612736 | bytes 8388608 | tf_op jit(solution)/shard_map/pallas_call | solution.py:338
  134.0 2.4 %shard_map.152 = f32[2,2,128,256]{3,2,1,0:T(8,128)} custom-call(f32[8,128,128]{2,1,0:T(8,128)} %all-to-all-done.1.blocks, bf16[512,512]{1,0:T(8,128)(2,1)S(1)} %copy-done.14), custom_call_target="tpu_custom_call" | custom-call | flops 536870912 | bytes 4194304 | tf_op jit(solution)/shard_map/pallas_call | solution.py:294
  (60 shorter events, 11.4 us)
Async XLA Ops:
  0.6 2.2 %copy-start = (f32[2,2,128,2048]{3,2,1,0:T(8,128)S(1)}, f32[2,2,128,2048]{3,2,1,0:T(8,128)}, u32[]{:S(2)}) copy-start(f32[2,2,128,2048]{3,2,1,0:T(8,128)} %cur.3) | copy-start | bytes 12582916
  2.8 1.2 copy-start.1
  4.1 1.2 copy-start.2
  5.3 0.7 copy-start.11
  9.2 19.8 %copy-start.13 = (f32[2,2,128,256]{3,2,1,0:T(8,128)S(1)}, f32[2,2,128,256]{3,2,1,0:T(8,128)}, u32[]{:S(2)}) copy-start(f32[2,2,128,256]{3,2,1,0:T(8,128)} %grad.1) | copy-start | bytes 1572868
  9.2 13.7 %collective-permute-start.9 = (f32[4,128,128]{2,1,0:T(8,128)}, f32[4,128,128]{2,1,0:T(8,128)}, u32[]{:S(2)}, u32[]{:S(2)}) collective-permute-start(f32[4,128,128]{2,1,0:T(8,128)} %get-tuple-element.8), channel_id=1, source_target_pairs={{3,2},{7,6},{11,10},{15,14},{19,18},{23,22},{27,26},{31,30}} | collective-permute-start | bytes 786440 | tf_op jit(solution)/shard_map/ppermute | solution.py:376
  13.1 34.8 %copy-start.5 = (f32[512,8]{1,0:T(8,128)S(1)}, f32[512,8]{1,0:T(8,128)}, u32[]{:S(2)}) copy-start(f32[512,8]{1,0:T(8,128)} %constant.90.clone.tw) | copy-start | bytes 49156
  13.1 34.8 %copy-start.9 = (bf16[1024,256]{1,0:T(8,128)(2,1)S(1)}, bf16[1024,256]{1,0:T(8,128)(2,1)}, u32[]{:S(2)}) copy-start(bf16[1024,256]{1,0:T(8,128)(2,1)} %constant.92.clone.t_lo) | copy-start | bytes 1572868
  13.9 12.0 %collective-permute-start.3 = (f32[4,128,128]{2,1,0:T(8,128)}, f32[4,128,128]{2,1,0:T(8,128)}, u32[]{:S(2)}, u32[]{:S(2)}) collective-permute-start(f32[4,128,128]{2,1,0:T(8,128)} %get-tuple-element.4), channel_id=1, source_target_pairs={{3,2},{7,6},{11,10},{15,14},{19,18},{23,22},{27,26},{31,30}} | collective-permute-start | bytes 786440 | tf_op jit(solution)/shard_map/ppermute | solution.py:376
  15.3 19.9 %collective-permute-start.6 = (f32[4,128,128]{2,1,0:T(8,128)}, f32[4,128,128]{2,1,0:T(8,128)}, u32[]{:S(2)}, u32[]{:S(2)}) collective-permute-start(f32[4,128,128]{2,1,0:T(8,128)} %get-tuple-element.9), channel_id=1, source_target_pairs={{0,1},{4,5},{8,9},{12,13},{16,17},{20,21},{24,25},{28,29}} | collective-permute-start | bytes 786440 | tf_op jit(solution)/shard_map/ppermute | solution.py:375
  20.9 18.1 %collective-permute-start = (f32[4,128,128]{2,1,0:T(8,128)}, f32[4,128,128]{2,1,0:T(8,128)}, u32[]{:S(2)}, u32[]{:S(2)}) collective-permute-start(f32[4,128,128]{2,1,0:T(8,128)} %get-tuple-element.5), channel_id=1, source_target_pairs={{0,1},{4,5},{8,9},{12,13},{16,17},{20,21},{24,25},{28,29}} | collective-permute-start | bytes 786440 | tf_op jit(solution)/shard_map/ppermute | solution.py:375
  24.6 10.6 %collective-permute-start.10 = (f32[4,128,128]{2,1,0:T(8,128)}, f32[4,128,128]{2,1,0:T(8,128)}, u32[]{:S(2)}, u32[]{:S(2)}) collective-permute-start(f32[4,128,128]{2,1,0:T(8,128)} %bitcast_add_fusion), channel_id=1, source_target_pairs={{3,2},{2,1},{7,6},{6,5},{11,10},{10,9},{15,14},{14,13},{19,18},{18... | collective-permute-start | bytes 786440 | tf_op jit(solution)/shard_map/ppermute | solution.py:376
  27.6 11.4 %collective-permute-start.4 = (f32[4,128,128]{2,1,0:T(8,128)}, f32[4,128,128]{2,1,0:T(8,128)}, u32[]{:S(2)}, u32[]{:S(2)}) collective-permute-start(f32[4,128,128]{2,1,0:T(8,128)} %bitcast_add_fusion.5), channel_id=1, source_target_pairs={{3,2},{2,1},{7,6},{6,5},{11,10},{10,9},{15,14},{14,13},{19,18},{18... | collective-permute-start | bytes 786440 | tf_op jit(solution)/shard_map/ppermute | solution.py:376
  29.0 1.0 copy-start.15
  31.4 16.4 %all-to-all-start.2 = ((f32[8,128,128]{2,1,0:T(8,128)}), f32[8,128,128]{2,1,0:T(8,128)S(1)}, u32[]{:S(2)}, u32[]{:S(2)}) async-start(f32[8,128,128]{2,1,0:T(8,128)} %shard_map.153), calls=%async_computation.2 | async-start | bytes 1048576 | tf_op jit(solution)/shard_map/all_to_all | solution.py:406
  37.1 20.9 %collective-permute-start.7 = (f32[4,128,128]{2,1,0:T(8,128)}, f32[4,128,128]{2,1,0:T(8,128)}, u32[]{:S(2)}, u32[]{:S(2)}) collective-permute-start(f32[4,128,128]{2,1,0:T(8,128)} %get-tuple-element.7), channel_id=1, source_target_pairs={{0,1},{1,2},{4,5},{5,6},{8,9},{9,10},{12,13},{13,14},{16,17},{17,1... | collective-permute-start | bytes 786440 | tf_op jit(solution)/shard_map/ppermute | solution.py:375
  41.0 24.6 %collective-permute-start.1 = (f32[4,128,128]{2,1,0:T(8,128)}, f32[4,128,128]{2,1,0:T(8,128)}, u32[]{:S(2)}, u32[]{:S(2)}) collective-permute-start(f32[4,128,128]{2,1,0:T(8,128)} %get-tuple-element.3), channel_id=1, source_target_pairs={{0,1},{1,2},{4,5},{5,6},{8,9},{9,10},{12,13},{13,14},{16,17},{17,1... | collective-permute-start | bytes 786440 | tf_op jit(solution)/shard_map/ppermute | solution.py:375
  47.9 1.0 copy-start.10
  51.2 20.1 %all-to-all-start.3 = ((f32[8,128,128]{2,1,0:T(8,128)}), f32[8,128,128]{2,1,0:T(8,128)}, u32[]{:S(2)}, u32[]{:S(2)}) async-start(f32[8,128,128]{2,1,0:T(8,128)} %bitcast.18), calls=%async_computation.3 | async-start | bytes 1048576 | tf_op jit(solution)/shard_map/all_to_all | solution.py:410
  55.4 19.1 %collective-permute-start.11 = (f32[4,128,128]{2,1,0:T(8,128)}, f32[4,128,128]{2,1,0:T(8,128)}, u32[]{:S(2)}, u32[]{:S(2)}) collective-permute-start(f32[4,128,128]{2,1,0:T(8,128)} %get-tuple-element.6), channel_id=1, source_target_pairs={{3,2},{2,1},{1,0},{7,6},{6,5},{5,4},{11,10},{10,9},{9,8},{15,14},{... | collective-permute-start | bytes 786440 | tf_op jit(solution)/shard_map/ppermute | solution.py:376
  56.7 24.1 %collective-permute-start.5 = (f32[4,128,128]{2,1,0:T(8,128)}, f32[4,128,128]{2,1,0:T(8,128)}, u32[]{:S(2)}, u32[]{:S(2)}) collective-permute-start(f32[4,128,128]{2,1,0:T(8,128)} %get-tuple-element.2), channel_id=1, source_target_pairs={{3,2},{2,1},{1,0},{7,6},{6,5},{5,4},{11,10},{10,9},{9,8},{15,14},{... | collective-permute-start | bytes 786440 | tf_op jit(solution)/shard_map/ppermute | solution.py:376
  59.7 20.1 %collective-permute-start.8 = (f32[4,128,128]{2,1,0:T(8,128)}, f32[4,128,128]{2,1,0:T(8,128)}, u32[]{:S(2)}, u32[]{:S(2)}) collective-permute-start(f32[4,128,128]{2,1,0:T(8,128)} %bitcast_add_fusion.3), channel_id=1, source_target_pairs={{0,1},{1,2},{2,3},{4,5},{5,6},{6,7},{8,9},{9,10},{10,11},{12,13},{... | collective-permute-start | bytes 786440 | tf_op jit(solution)/shard_map/ppermute | solution.py:375
  67.2 51.7 %copy-start.3 = (bf16[512,1024]{1,0:T(8,128)(2,1)S(1)}, bf16[512,1024]{1,0:T(8,128)(2,1)}, u32[]{:S(2)}) copy-start(bf16[512,1024]{1,0:T(8,128)(2,1)} %constant.97.clone.refs_9_) | copy-start | bytes 3145732
  67.2 51.7 %copy-start.12 = (f32[8,512]{1,0:T(8,128)S(1)}, f32[8,512]{1,0:T(8,128)}, u32[]{:S(2)}) copy-start(f32[8,512]{1,0:T(8,128)} %constant.86.clone.tw.refs_7_.refs_10_) | copy-start | bytes 49156
  67.2 13.6 %collective-permute-start.2 = (f32[4,128,128]{2,1,0:T(8,128)}, f32[4,128,128]{2,1,0:T(8,128)}, u32[]{:S(2)}, u32[]{:S(2)}) collective-permute-start(f32[4,128,128]{2,1,0:T(8,128)} %bitcast_add_fusion.8), channel_id=1, source_target_pairs={{0,1},{1,2},{2,3},{4,5},{5,6},{6,7},{8,9},{9,10},{10,11},{12,13},{... | collective-permute-start | bytes 786440 | tf_op jit(solution)/shard_map/ppermute | solution.py:375
  73.2 20.4 %collective-permute-start.21 = (f32[4,128,128]{2,1,0:T(8,128)}, f32[4,128,128]{2,1,0:T(8,128)}, u32[]{:S(2)}, u32[]{:S(2)}) collective-permute-start(f32[4,128,128]{2,1,0:T(8,128)} %get-tuple-element.10.refs_0_), channel_id=1, source_target_pairs={{1,0},{2,1},{3,2},{5,4},{6,5},{7,6},{9,8},{10,9},{11,10},{13,12},{... | collective-permute-start | bytes 786440 | tf_op jit(solution)/shard_map/ppermute | solution.py:387
  74.5 20.4 %collective-permute-start.18 = (f32[4,128,128]{2,1,0:T(8,128)}, f32[4,128,128]{2,1,0:T(8,128)}, u32[]{:S(2)}, u32[]{:S(2)}) collective-permute-start(f32[4,128,128]{2,1,0:T(8,128)} %get-tuple-element.10.refs_0_), channel_id=1, source_target_pairs={{0,1},{1,2},{2,3},{4,5},{5,6},{6,7},{8,9},{9,10},{10,11},{12,13},{... | collective-permute-start | bytes 786440 | tf_op jit(solution)/shard_map/ppermute | solution.py:386
  80.8 38.1 %copy-start.4 = (bf16[512,1024]{1,0:T(8,128)(2,1)S(1)}, bf16[512,1024]{1,0:T(8,128)(2,1)}, u32[]{:S(2)}) copy-start(bf16[512,1024]{1,0:T(8,128)(2,1)} %constant.96.clone.refs_8_) | copy-start | bytes 3145732
  82.8 24.8 %all-to-all-start = ((f32[8,128,128]{2,1,0:T(8,128)}), f32[8,128,128]{2,1,0:T(8,128)S(1)}, u32[]{:S(2)}, u32[]{:S(2)}) async-start(f32[8,128,128]{2,1,0:T(8,128)} %pad_maximum_fusion), calls=%async_computation | async-start | bytes 1048576 | tf_op jit(solution)/shard_map/all_to_all | solution.py:413
  87.0 10.9 %collective-permute-start.15 = (f32[4,128,128]{2,1,0:T(8,128)}, f32[4,128,128]{2,1,0:T(8,128)}, u32[]{:S(2)}, u32[]{:S(2)}) collective-permute-start(f32[4,128,128]{2,1,0:T(8,128)} %get-tuple-element.11.refs_0_), channel_id=1, source_target_pairs={{1,0},{2,1},{3,2},{5,4},{6,5},{7,6},{9,8},{10,9},{11,10},{13,12},{... | collective-permute-start | bytes 786440 | tf_op jit(solution)/shard_map/ppermute | solution.py:387
  88.3 10.9 %collective-permute-start.12 = (f32[4,128,128]{2,1,0:T(8,128)}, f32[4,128,128]{2,1,0:T(8,128)}, u32[]{:S(2)}, u32[]{:S(2)}) collective-permute-start(f32[4,128,128]{2,1,0:T(8,128)} %get-tuple-element.11.refs_0_), channel_id=1, source_target_pairs={{0,1},{1,2},{2,3},{4,5},{5,6},{6,7},{8,9},{9,10},{10,11},{12,13},{... | collective-permute-start | bytes 786440 | tf_op jit(solution)/shard_map/ppermute | solution.py:386
  93.6 11.4 %collective-permute-start.22 = (f32[4,128,128]{2,1,0:T(8,128)}, f32[4,128,128]{2,1,0:T(8,128)}, u32[]{:S(2)}, u32[]{:S(2)}) collective-permute-start(f32[4,128,128]{2,1,0:T(8,128)} %collective-permute-done.21.refs_4_), channel_id=1, source_target_pairs={{1,0},{2,1},{5,4},{6,5},{9,8},{10,9},{13,12},{14,13},{17,16},{18,1... | collective-permute-start | bytes 786440 | tf_op jit(solution)/shard_map/ppermute | solution.py:387
  94.9 11.4 %collective-permute-start.19 = (f32[4,128,128]{2,1,0:T(8,128)}, f32[4,128,128]{2,1,0:T(8,128)}, u32[]{:S(2)}, u32[]{:S(2)}) collective-permute-start(f32[4,128,128]{2,1,0:T(8,128)} %collective-permute-done.18.refs_1_), channel_id=1, source_target_pairs={{1,2},{2,3},{5,6},{6,7},{9,10},{10,11},{13,14},{14,15},{17,18},{18... | collective-permute-start | bytes 786440 | tf_op jit(solution)/shard_map/ppermute | solution.py:386
  98.0 18.8 %collective-permute-start.16 = (f32[4,128,128]{2,1,0:T(8,128)}, f32[4,128,128]{2,1,0:T(8,128)}, u32[]{:S(2)}, u32[]{:S(2)}) collective-permute-start(f32[4,128,128]{2,1,0:T(8,128)} %collective-permute-done.15.refs_4_), channel_id=1, source_target_pairs={{1,0},{2,1},{5,4},{6,5},{9,8},{10,9},{13,12},{14,13},{17,16},{18,1... | collective-permute-start | bytes 786440 | tf_op jit(solution)/shard_map/ppermute | solution.py:387
  99.3 18.9 %collective-permute-start.13 = (f32[4,128,128]{2,1,0:T(8,128)}, f32[4,128,128]{2,1,0:T(8,128)}, u32[]{:S(2)}, u32[]{:S(2)}) collective-permute-start(f32[4,128,128]{2,1,0:T(8,128)} %collective-permute-done.12.refs_1_), channel_id=1, source_target_pairs={{1,2},{2,3},{5,6},{6,7},{9,10},{10,11},{13,14},{14,15},{17,18},{18... | collective-permute-start | bytes 786440 | tf_op jit(solution)/shard_map/ppermute | solution.py:386
  105.0 13.9 %collective-permute-start.23 = (f32[4,128,128]{2,1,0:T(8,128)}, f32[4,128,128]{2,1,0:T(8,128)}, u32[]{:S(2)}, u32[]{:S(2)}) collective-permute-start(f32[4,128,128]{2,1,0:T(8,128)} %collective-permute-done.22.refs_5_), channel_id=1, source_target_pairs={{1,0},{5,4},{9,8},{13,12},{17,16},{21,20},{25,24},{29,28}} | collective-permute-start | bytes 786440 | tf_op jit(solution)/shard_map/ppermute | solution.py:387
  106.3 12.6 %collective-permute-start.20 = (f32[4,128,128]{2,1,0:T(8,128)}, f32[4,128,128]{2,1,0:T(8,128)}, u32[]{:S(2)}, u32[]{:S(2)}) collective-permute-start(f32[4,128,128]{2,1,0:T(8,128)} %collective-permute-done.19.refs_2_), channel_id=1, source_target_pairs={{2,3},{6,7},{10,11},{14,15},{18,19},{22,23},{26,27},{30,31}} | collective-permute-start | bytes 786440 | tf_op jit(solution)/shard_map/ppermute | solution.py:386
  107.6 1.0 copy-start.7
  108.7 1.0 copy-start.8
  112.6 20.4 %all-to-all-start.1 = ((f32[8,128,128]{2,1,0:T(8,128)}), f32[8,128,128]{2,1,0:T(8,128)}, u32[]{:S(2)}, u32[]{:S(2)}) async-start(f32[8,128,128]{2,1,0:T(8,128)} %bitcast.15), calls=%async_computation.1 | async-start | bytes 1048576 | tf_op jit(solution)/shard_map/all_to_all | solution.py:417
  116.7 11.8 %copy-start.6 = (f32[4,128,128]{2,1,0:T(8,128)S(1)}, f32[4,128,128]{2,1,0:T(8,128)}, u32[]{:S(2)}) copy-start(f32[4,128,128]{2,1,0:T(8,128)} %get-tuple-element.11.refs_0_) | copy-start | bytes 786436
  116.7 11.8 %collective-permute-start.17 = (f32[4,128,128]{2,1,0:T(8,128)}, f32[4,128,128]{2,1,0:T(8,128)S(1)}, u32[]{:S(2)}, u32[]{:S(2)}) collective-permute-start(f32[4,128,128]{2,1,0:T(8,128)} %collective-permute-done.16.refs_5_), channel_id=1, source_target_pairs={{1,0},{5,4},{9,8},{13,12},{17,16},{21,20},{25,24},{29,28}} | collective-permute-start | bytes 786440 | tf_op jit(solution)/shard_map/ppermute | solution.py:387
  118.2 10.3 %collective-permute-start.14 = (f32[4,128,128]{2,1,0:T(8,128)}, f32[4,128,128]{2,1,0:T(8,128)S(1)}, u32[]{:S(2)}, u32[]{:S(2)}) collective-permute-start(f32[4,128,128]{2,1,0:T(8,128)} %collective-permute-done.13.refs_2_), channel_id=1, source_target_pairs={{2,3},{6,7},{10,11},{14,15},{18,19},{22,23},{26,27},{30,31}} | collective-permute-start | bytes 786440 | tf_op jit(solution)/shard_map/ppermute | solution.py:386
  133.0 1.0 copy-start.14

commit v2 on v1

v2 whole, which is shorter than its diff:
```python
import functools
import math

import jax
import jax.numpy as jnp
import numpy as np
from jax import lax
from jax.experimental import pallas as pl
from jax.experimental.pallas import tpu as pltpu
from jax.sharding import PartitionSpec as P

NX = 8192
MX = 1024
MY = 1024
STRIDE = 4

PERIOD = NX // STRIDE
RADIX = 4
SPAN = PERIOD // RADIX
BANDS = MX // RADIX
LANES = 128
HALF = LANES // 2

f32 = jnp.float32
bf16 = jnp.bfloat16
precise = lax.Precision.HIGHEST


def phase_table(pos_start, pos_count, pos_total, ang_count, modulus):
    position = pos_start + jnp.arange(pos_count, dtype=jnp.int32) - pos_total // 2
    angles = jnp.arange(ang_count, dtype=jnp.int32) - ang_count // 2
    cycles = jnp.mod(position[:, None] * angles[None, :] * STRIDE, modulus)
    radians = 2.0 * math.pi / modulus * cycles.astype(jnp.float32)
    return (jnp.cos(radians), jnp.sin(radians))


def contract(left, right, left_dim, right_dim):
    return lax.dot_general(
        left,
        right,
        (((left_dim,), (right_dim,)), ((), ())),
        precision=precise,
        preferred_element_type=jnp.float32,
    )


def general_body(currents, far_gradient):
    row_count = currents.shape[2]
    column_count = currents.shape[3]
    angle_rows = far_gradient.shape[2]
    angle_cols = far_gradient.shape[3]
    total_rows = row_count * lax.axis_size("wide")
    scale = 1.0 / math.sqrt(total_rows * NX)
    row_start = lax.axis_index("wide") * row_count
    column_start = lax.axis_index("narrow") * column_count
    cos_x, sin_x = phase_table(column_start, column_count, NX, MX, NX)
    cos_y, sin_y = phase_table(row_start, row_count, total_rows, MY, NX)
    real_cur = currents[:, 0].reshape(2 * row_count, column_count)
    imag_cur = currents[:, 1].reshape(2 * row_count, column_count)
    real_term = contract(cos_x, real_cur, 0, 1) + contract(sin_x, imag_cur, 0, 1)
    imag_term = contract(cos_x, imag_cur, 0, 1) - contract(sin_x, real_cur, 0, 1)
    column_sums = lax.psum_scatter(
        jnp.stack([real_term, imag_term], axis=1), "narrow", scatter_dimension=0, tiled=True
    )
    sum_real = column_sums[:, 0].reshape(angle_cols * 2, row_count)
    sum_imag = column_sums[:, 1].reshape(angle_cols * 2, row_count)
    real_term = contract(cos_y, sum_real, 0, 1) + contract(sin_y, sum_imag, 0, 1)
    imag_term = contract(cos_y, sum_imag, 0, 1) - contract(sin_y, sum_real, 0, 1)
    far_sums = lax.psum_scatter(
        scale * jnp.stack([real_term, imag_term], axis=1), "wide", scatter_dimension=0, tiled=True
    )
    far_field = far_sums.reshape(angle_rows, 2, angle_cols, 2).transpose(3, 1, 0, 2)
    grad_real = far_gradient[:, 0].transpose(1, 2, 0).reshape(angle_rows, angle_cols * 2)
    grad_imag = far_gradient[:, 1].transpose(1, 2, 0).reshape(angle_rows, angle_cols * 2)
    piece_real = lax.all_gather(grad_real, "wide", axis=0, tiled=True)
    piece_imag = lax.all_gather(grad_imag, "wide", axis=0, tiled=True)
    half_real = contract(piece_real, cos_y, 0, 1) - contract(piece_imag, sin_y, 0, 1)
    half_imag = contract(piece_imag, cos_y, 0, 1) + contract(piece_real, sin_y, 0, 1)
    half_real = half_real.reshape(angle_cols, 2, row_count)
    half_imag = half_imag.reshape(angle_cols, 2, row_count)
    piece_real = lax.all_gather(half_real, "narrow", axis=0, tiled=True)
    piece_imag = lax.all_gather(half_imag, "narrow", axis=0, tiled=True)
    width = piece_real.shape[0]
    flat_real = piece_real.reshape(width, 2 * row_count)
    flat_imag = piece_imag.reshape(width, 2 * row_count)
    back_real = contract(flat_real, cos_x, 0, 1) - contract(flat_imag, sin_x, 0, 1)
    back_imag = contract(flat_imag, cos_x, 0, 1) + contract(flat_real, sin_x, 0, 1)
    back_real = back_real.reshape(2, row_count, column_count)
    back_imag = back_imag.reshape(2, row_count, column_count)
    aperture_grad = scale * jnp.stack([back_real, back_imag], axis=1)
    return (far_field, aperture_grad)


def halves(table):
    hi = table.astype(np.float32).astype(bf16)
    return hi, (table - hi.astype(np.float64)).astype(np.float32).astype(bf16)


def angle(count_left, left_start, count_right, right_start, period):
    left = np.arange(count_left, dtype=np.int64) + left_start
    right = np.arange(count_right, dtype=np.int64) + right_start
    return 2.0 * np.pi / period * ((left[:, None] * right[None, :]) % period)


def make_tables(shards):
    theta = angle(SPAN, 0, BANDS, -(BANDS // 2), SPAN)
    cos, sin = np.cos(theta), np.sin(theta)
    each = BANDS // shards
    x_table = np.stack([cos.reshape(SPAN, shards, each), -sin.reshape(SPAN, shards, each)], axis=2)
    x_table = x_table.reshape(SPAN, 2 * BANDS)
    y_table = np.concatenate([cos.T, sin.T], axis=0)
    y_back = np.concatenate([cos, sin], axis=0)
    twiddle = angle(RADIX, 0, SPAN, 0, PERIOD)
    cols = RADIX * each
    order = np.zeros((each, RADIX, RADIX, each))
    for k0 in range(RADIX):
        order[np.arange(each), k0, k0, np.arange(each)] = 1.0
    order = order.reshape(cols, cols).astype(bf16)
    return {
        "x": halves(x_table),
        "x_back": halves(np.ascontiguousarray(x_table.T)),
        "y": halves(y_table),
        "y_back": halves(y_back),
        "row_tw": np.concatenate([np.cos(twiddle), np.sin(twiddle)], axis=0).astype(np.float32),
        "col_tw": np.ascontiguousarray(
            np.concatenate([np.cos(twiddle), np.sin(twiddle)], axis=0).T
        ).astype(np.float32),
        "order": order,
        "order_back": np.ascontiguousarray(order.T),
    }


def split(value):
    hi = value.astype(bf16)
    return hi, (value - hi.astype(f32)).astype(bf16)


def dot(left, right):
    return jnp.dot(left, right, preferred_element_type=f32)


def dot3(left, right):
    return dot(left[0], right[0]) + (dot(left[1], right[0]) + dot(left[0], right[1]))


def times(tw_cos, tw_sin, real, imag):
    return real * tw_cos + imag * tw_sin, imag * tw_cos - real * tw_sin


def sign_of(shape):
    lane = lax.broadcasted_iota(jnp.int32, shape, len(shape) - 1)
    return jnp.where(lane < HALF, 1.0, -1.0).astype(f32)


def swap(value):
    return pltpu.roll(value, HALF, axis=1)


def moved(value, order):
    hi = value.astype(bf16)
    rest = value - hi.astype(f32)
    mid = rest.astype(bf16)
    lo = (rest - mid.astype(f32)).astype(bf16)
    return dot(hi, order) + (dot(mid, order) + dot(lo, order))


def paired(first, second):
    left = lax.broadcasted_iota(jnp.int32, first.shape, 1) < HALF
    return jnp.where(left, first, swap(second)), jnp.where(left, swap(first), second)


def sort(grad, order, out):
    rows = grad.shape[2]
    for component in range(2):
        flat = jnp.concatenate([grad[component, 0], grad[component, 1]], axis=0)
        places = moved(flat, order[...])
        for pair in range(RADIX // 2):
            lanes = places[:, pair * LANES : (pair + 1) * LANES]
            at = component * RADIX + 2 * pair
            out[at], out[at + 1] = paired(lanes[:rows], lanes[rows:])


def start_kernel(shards, place, cur, tw, t_hi, t_lo, grad, order, sorted_, *refs):
    outs, held = refs[:-1], refs[-1]
    rows = cur.shape[2]

    @pl.when((pl.program_id(0) == 0) & (pl.program_id(1) == 0))
    def _():
        sort(grad, order, sorted_)

    re = [cur[0, 0, :, a * SPAN : (a + 1) * SPAN] for a in range(RADIX)]
    im = [cur[0, 1, :, a * SPAN : (a + 1) * SPAN] for a in range(RADIX)]
    sum_re, dif_re = re[0] + re[2], re[0] - re[2]
    sum_im, dif_im = im[0] + im[2], im[0] - im[2]
    odd_re, gap_re = re[1] + re[3], re[1] - re[3]
    odd_im, gap_im = im[1] + im[3], im[1] - im[3]
    legs = [
        (sum_re + odd_re, sum_im + odd_im),
        (dif_re + gap_im, dif_im - gap_re),
        (sum_re - odd_re, sum_im - odd_im),
        (dif_re - gap_im, dif_im + gap_re),
    ]
    flat = []
    for k0, (real, imag) in enumerate(legs):
        if k0 > 0:
            real, imag = times(tw[k0 : k0 + 1], tw[RADIX + k0 : RADIX + k0 + 1], real, imag)
        flat += [real, imag]
    sums = dot3(split(jnp.concatenate(flat, axis=0)), (t_hi[...], t_lo[...]))
    sign = sign_of((rows, LANES))
    for shard in range(shards):
        lanes = sums[:, shard * LANES : (shard + 1) * LANES]
        for k0 in range(RADIX):
            of_real = lanes[2 * k0 * rows : (2 * k0 + 1) * rows]
            of_imag = lanes[(2 * k0 + 1) * rows : (2 * k0 + 2) * rows]
            held[shard, k0] = of_real - sign * swap(of_imag)
    for away, out in enumerate(outs):
        out[...] = held[place[0] ^ away]


def y_kernel(scale, col, tw, t_hi, t_lo, *refs):
    out = refs[-1]
    early, late = col[:SPAN], col[SPAN:]
    sign = sign_of(early.shape)
    turned = sign * swap(early)
    flat = []
    for k0, leg in enumerate([late + early, late - turned, late - early, late + turned]):
        if k0 > 0:
            leg = leg * tw[:, k0 : k0 + 1] + (sign * tw[:, RADIX + k0 : RADIX + k0 + 1]) * swap(leg)
        flat.append(leg)
    hi, lo = split(jnp.concatenate(flat, axis=1))
    both = dot3((t_hi[...], t_lo[...]), (hi, lo))
    half_sign = scale * sign_of((BANDS, LANES))
    for k0 in range(RADIX):
        cos_part = both[:BANDS, k0 * LANES : (k0 + 1) * LANES]
        sin_part = both[BANDS:, k0 * LANES : (k0 + 1) * LANES]
        out[pl.ds(k0, BANDS, stride=RADIX), :] = scale * cos_part + half_sign * swap(sin_part)


def y_back_kernel(scale, grad, tw, t_hi, t_lo, *refs):
    out = refs[-1]
    flat = [grad[pl.ds(k0, BANDS, stride=RADIX), :] for k0 in range(RADIX)]
    hi, lo = split(jnp.concatenate(flat, axis=1))
    both = dot3((t_hi[...], t_lo[...]), (hi, lo))
    sign = sign_of((SPAN, LANES))
    legs = []
    for k0 in range(RADIX):
        cos_part = both[:SPAN, k0 * LANES : (k0 + 1) * LANES]
        sin_part = both[SPAN:, k0 * LANES : (k0 + 1) * LANES]
        leg = cos_part - sign * swap(sin_part)
        if k0 > 0:
            leg = leg * tw[:, k0 : k0 + 1] - (sign * tw[:, RADIX + k0 : RADIX + k0 + 1]) * swap(leg)
        legs.append(leg)
    even, odd = legs[0] + legs[2], legs[1] + legs[3]
    out[SPAN:, :] = scale * (even + odd)
    out[:SPAN, :] = scale * ((legs[0] - legs[2]) + sign * swap(legs[1] - legs[3]))


def x_back_kernel(place, _, *refs):
    blocks, (tw, t_hi, t_lo, out, hi_ref, lo_ref) = refs[:-6], refs[-6:]
    rows = out.shape[2]
    flat = RADIX * rows
    sign = sign_of((flat, LANES))
    for away, block in enumerate(blocks):
        value = block[...].reshape(flat, LANES)
        at = pl.ds(pl.multiple_of((place[0] ^ away) * LANES, LANES), LANES)
        hi_ref[:flat, at], lo_ref[:flat, at] = split(value)
        hi_ref[flat:, at], lo_ref[flat:, at] = split(sign * swap(value))
    sums = dot3((hi_ref[...], lo_ref[...]), (t_hi[...], t_lo[...]))
    legs = []
    for k0 in range(RADIX):
        real = sums[k0 * rows : (k0 + 1) * rows]
        imag = sums[flat + k0 * rows : flat + (k0 + 1) * rows]
        if k0 > 0:
            real, imag = times(tw[k0 : k0 + 1], -tw[RADIX + k0 : RADIX + k0 + 1], real, imag)
        legs.append((real, imag))
    (r0, i0), (r1, i1), (r2, i2), (r3, i3) = legs
    even_r, even_i, gap_r, gap_i = r0 + r2, i0 + i2, r0 - r2, i0 - i2
    odd_r, odd_i, skew_r, skew_i = r1 + r3, i1 + i3, r1 - r3, i1 - i3
    results = [
        (even_r + odd_r, even_i + odd_i),
        (gap_r - skew_i, gap_i + skew_r),
        (even_r - odd_r, even_i - odd_i),
        (gap_r + skew_i, gap_i - skew_r),
    ]
    for a, (real, imag) in enumerate(results):
        out[0, 0, :, a * SPAN : (a + 1) * SPAN] = real
        out[0, 1, :, a * SPAN : (a + 1) * SPAN] = imag


def unsort_kernel(blocks, order, *refs):
    out = refs[-1]
    rows = out.shape[2]
    for component in range(2):
        real, imag = [], []
        for pair in range(RADIX // 2):
            at = component * RADIX + 2 * pair
            halves_of = paired(blocks[at], blocks[at + 1])
            real.append(halves_of[0])
            imag.append(halves_of[1])
        flat = jnp.concatenate([jnp.concatenate(real, axis=1), jnp.concatenate(imag, axis=1)], axis=0)
        far = moved(flat, order[...])
        out[component, 0] = far[:rows]
        out[component, 1] = far[rows:]


ALONE = pltpu.CompilerParams(vmem_limit_bytes=60 * 1024 * 1024)
SHARED = pltpu.CompilerParams(vmem_limit_bytes=24 * 1024 * 1024)


COST = pl.CostEstimate(flops=1 << 20, bytes_accessed=1 << 16, transcendentals=0)


def whole(kernel, shapes, *args, after=(), params=SHARED):
    shapes = [jax.ShapeDtypeStruct(shape, f32) for shape in shapes]
    in_vmem = pl.BlockSpec(memory_space=pltpu.VMEM)
    result = pl.pallas_call(
        kernel,
        out_shape=shapes,
        in_specs=[in_vmem] * len(args) + [pl.BlockSpec(memory_space=pl.ANY)] * len(after),
        out_specs=[in_vmem] * len(shapes),
        compiler_params=params,
        cost_estimate=COST,
    )(*args, *after)
    return result if len(shapes) > 1 else result[0]


def onward_kernel(blocks, far, near, *refs):
    refs[-2][...] = blocks[...] + far[...]
    refs[-1][...] = near[...]


def total_kernel(own, near, skip, half, *refs):
    out, first, second = refs[-3:]
    out[...] = (own[...] + near[...]) + skip[...]
    first[...] = half[:RADIX]
    second[...] = half[RADIX:]


def fixed(shape):
    return pl.BlockSpec(shape, lambda *_: (0,) * len(shape))


def start(place, currents, far_gradient, shards, tables):
    rows, columns = currents.shape[2:]
    tile = rows // 2
    t_hi, t_lo = tables["x"]
    sorted_shape = (2 * RADIX, far_gradient.shape[2], LANES)
    return pl.pallas_call(
        functools.partial(start_kernel, shards),
        grid_spec=pltpu.PrefetchScalarGridSpec(
            num_scalar_prefetch=1,
            grid=(2, rows // tile),
            in_specs=[
                pl.BlockSpec((1, 2, tile, columns), lambda c, i, _: (c, 0, i, 0)),
                fixed((2 * RADIX, SPAN)),
                fixed(t_hi.shape),
                fixed(t_lo.shape),
                fixed(far_gradient.shape),
                fixed(tables["order"].shape),
            ],
            out_specs=[fixed(sorted_shape)]
            + [pl.BlockSpec((RADIX, tile, LANES), lambda c, i, _: (c, i, 0))] * shards,
            scratch_shapes=[pltpu.VMEM((shards, RADIX, tile, LANES), f32)],
        ),
        out_shape=[jax.ShapeDtypeStruct(sorted_shape, f32)]
        + [jax.ShapeDtypeStruct((2 * RADIX, rows, LANES), f32)] * shards,
        compiler_params=ALONE,
        cost_estimate=COST,
    )(place, currents, tables["row_tw"], t_hi, t_lo, far_gradient, tables["order"])


def back_x(place, parts, component, grad, shape, tables):
    rows = shape[2]
    tile = rows // 2
    t_hi, t_lo = tables["x_back"]
    both = pl.BlockSpec((RADIX, tile, LANES), lambda i, _: (component, i, 0))
    one = pl.BlockSpec((RADIX, tile, LANES), lambda i, _: (0, i, 0))
    first = grad is None
    return pl.pallas_call(
        x_back_kernel,
        grid_spec=pltpu.PrefetchScalarGridSpec(
            num_scalar_prefetch=1,
            grid=(rows // tile,),
            in_specs=[pl.BlockSpec(memory_space=pl.ANY)]
            + [both if part.shape[0] > RADIX else one for part in parts]
            + [fixed((2 * RADIX, SPAN)), fixed(t_hi.shape), fixed(t_lo.shape)],
            out_specs=pl.BlockSpec((1, 2, tile, shape[3]), lambda i, _: (component, 0, i, 0)),
            scratch_shapes=[
                pltpu.VMEM((2 * RADIX * tile, 2 * BANDS), bf16),
                pltpu.VMEM((2 * RADIX * tile, 2 * BANDS), bf16),
            ],
        ),
        out_shape=jax.ShapeDtypeStruct(shape, f32),
        input_output_aliases={} if first else {1: 0},
        compiler_params=SHARED,
        cost_estimate=COST,
    )(place, tables["row_tw"] if first else grad, *parts, tables["row_tw"], t_hi, t_lo)


PAIRS = [(0, 1), (1, 0), (2, 3), (3, 2)]
SKIPS = [(0, 2), (2, 0), (1, 3), (3, 1)]


def send(value, pairs):
    return lax.ppermute(value, "narrow", pairs)


def fast_body(tables, currents, far_gradient):
    shards = lax.axis_size("narrow")
    wide = lax.axis_size("wide")
    rows = currents.shape[2]
    angle_rows = far_gradient.shape[2]
    scale = 1.0 / math.sqrt(rows * wide * NX)
    place = lax.axis_index("narrow").astype(jnp.int32).reshape(1)
    y_hi, y_lo = tables["y"]
    b_hi, b_lo = tables["y_back"]

    group = (RADIX, rows, LANES)
    sorted_, *blocks = start(place, currents, far_gradient, shards, tables)
    far = send(blocks[3], PAIRS)

    onward, close = whole(onward_kernel, [blocks[0].shape] * 2, blocks[2], far, blocks[1])
    skip = send(onward, SKIPS)
    near = send(close, PAIRS)

    rows_in = lax.all_to_all(sorted_, "wide", 0, 0).reshape(MY, LANES)
    rows_out = whole(
        functools.partial(y_back_kernel, scale),
        [(rows * wide, LANES)],
        rows_in,
        tables["col_tw"],
        b_hi,
        b_lo,
        after=[onward],
    )
    half = lax.all_to_all(rows_out.reshape(wide, rows, LANES), "wide", 0, 0)

    beside = send(half, PAIRS)
    columns, *mine = whole(
        total_kernel, [blocks[0].shape, group, group], blocks[0], near, skip, half
    )

    there = [send(m, SKIPS) for m in mine]

    rows_in = lax.all_to_all(columns, "wide", 0, 0).reshape(rows * wide, LANES)
    rows_out = whole(
        functools.partial(y_kernel, scale),
        [(MY, LANES)],
        rows_in,
        tables["col_tw"],
        y_hi,
        y_lo,
    )
    far = lax.all_to_all(rows_out.reshape(wide, angle_rows, LANES), "wide", 0, 0)

    across = [send(t, PAIRS) for t in there]
    far_field = whole(unsort_kernel, [far_gradient.shape], far, tables["order_back"])
    grad = None
    for c in range(2):
        grad = back_x(place, [half, beside, there[c], across[c]], c, grad, currents.shape, tables)
    return (far_field, grad)


def solution(mesh):
    spec = P(None, None, "wide", "narrow")
    shards, wide = mesh.shape["narrow"], mesh.shape["wide"]

    def run(currents, far_gradient):
        rows = currents.shape[2]
        fits = (
            shards == 4
            and currents.shape[3] == shards * PERIOD
            and rows == 2 * SPAN
            and far_gradient.shape[2] == MY == 2 * SPAN
            and BANDS // shards == HALF
            and wide == 2 * RADIX
        )
        body = functools.partial(fast_body, make_tables(shards)) if fits else general_body
        return jax.shard_map(
            body, mesh=mesh, in_specs=(spec, spec), out_specs=(spec, spec), check_vma=False
        )(currents, far_gradient)

    return run
```

time: 138 us -> 104 us (0.75)
  starting transfers between devices: 74 us -> 25 us
  waiting for transfers between devices: 11.1 us -> 34 us
  other arithmetic: 13.6 us -> 0 us
  blocking collectives: 0 us -> 13.4 us
  local copies, waits for them, and re-layouts: 14.1 us -> 4.6 us
  Pallas kernels: 22.6 us -> 25.9 us
    ppermute x24 -> x8, starting transfers between devices: 57.8 us -> 14.1 us  [send(): return lax.ppermute(value, 'narrow', pairs)]
    ppermute x24 -> x8, waiting for transfers between devices: 11.1 us -> 27.6 us  [send(): return lax.ppermute(value, 'narrow', pairs)]
    all_to_all x0 -> x1, blocking collectives: none -> 13.4 us  [fast_body(): half = lax.all_to_all(rows_out.reshape(wide, rows, LANES), 'wide', 0, 0)]
    add x8 -> x0, other arithmetic: 12.7 us -> none  [the longest x6 10.5 us: line_sum(): to_right, to_left = (to_right + right, to_left + left)]
    all_to_all x1, waiting for transfers between devices: 0.01 us -> 6.37 us  [fast_body(): rows_in = lax.all_to_all(columns, 'wide', 0, 0).reshape(rows * wide, LANES)]
    unnamed x32 -> x28, local copies, waits for them, and re-layouts: 10.6 us -> 4.6 us
    all_to_all x1 -> x0, starting transfers between devices: 4.19 us -> none  [fast_body(): half = lax.all_to_all(rows_out.reshape(wide, rows, LANES), 'wide', 0, 0)]
    pallas_call x8, Pallas kernels: 22.6 us -> 25.9 us  [the longest x2 9.18 us: back_x(): pl.pallas_call(x_back_kernel, grid_spec=pltpu.PrefetchScalarGridSpec(num_...]
  transfers between devices with their start and end apart: 28 -> 11, of which waited for: 3 -> 8; matrix products, arithmetic and copies ran while one was open for 12% -> 0% of each run, Pallas kernels for 13% -> 14%
where the time goes in v2:
time: 104 us
  waiting for transfers between devices  34 us (33%)
  Pallas kernels  25.9 us (25%)
  starting transfers between devices  25 us (24%)
  blocking collectives  13.4 us (13%)
  local copies, waits for them, and re-layouts  4.6 us (4%)
    ppermute x8, waiting for transfers between devices, send(): return lax.ppermute(value, 'narrow', pairs)  27.6 us
    ppermute x8, starting transfers between devices, send(): return lax.ppermute(value, 'narrow', pairs)  14.1 us
    all_to_all x1, blocking collectives, fast_body(): half = lax.all_to_all(rows_out.reshape(wide, rows, LANES), 'wide', 0, 0)  13.4 us
    pallas_call x2, Pallas kernels, back_x(): pl.pallas_call(x_back_kernel, grid_spec=pltpu.PrefetchScalarGridSpec(num_...  9.18 us
    pallas_call x5, Pallas kernels, whole(): pl.pallas_call(kernel, out_shape=shapes, in_specs=[in_vmem] * len(args) +...  8.63 us
    pallas_call x1, Pallas kernels, start(): pl.pallas_call(functools.partial(start_kernel, shards), grid_spec=pltpu.P...  8.11 us
    all_to_all x1, waiting for transfers between devices, fast_body(): rows_in = lax.all_to_all(columns, 'wide', 0, 0).reshape(rows * wide, LANES)  6.37 us
    unnamed x28, local copies, waits for them, and re-layouts  4.6 us
  transfers between devices with their start and end apart: 11, of which 8 were waited for; matrix products, arithmetic and copies ran while one was open for 0% of the time, Pallas kernels for 14%

profile of v2, /device:TPU:0, one launch (start us, length us, event | category | flops | bytes accessed | tf_op | source)
XLA Modules:
  0.0 103.7 jit_solution(449026656079748586)
XLA Ops:
  0.6 0.0 copy-start.2
  0.6 0.0 copy-start.7
  0.7 0.0 copy-start.8
  0.7 8.1 %shard_map.149 = (f32[8,128,128]{2,1,0:T(8,128)}, f32[8,128,128]{2,1,0:T(8,128)}, f32[8,128,128]{2,1,0:T(8,128)}, f32[8,128,128]{2,1,0:T(8,128)}, f32[8,128,128]{2,1,0:T(8,128)}) custom-call(s32[1]{0:T(128)} %bitcast.place, f32[2,2,128,2048]{3,2,1,0:T(8,128)} %cur.1, f32[8,512]{1,0:T(8,128)} %constant.28.clone.tw._.refs_4_, ...), custom_call_target="tpu_custom_call" | custom-call | flops 1048576 | bytes 65536 | tf_op jit(solution)/shard_map/pallas_call | solution.py:348
  8.8 3.1 %collective-permute-start = (f32[8,128,128]{2,1,0:T(8,128)}, f32[8,128,128]{2,1,0:T(8,128)S(1)}, u32[]{:S(2)}, u32[]{:S(2)}) collective-permute-start(f32[8,128,128]{2,1,0:T(8,128)} %get-tuple-element.14), channel_id=1, source_target_pairs={{0,1},{1,0},{2,3},{3,2},{4,5},{5,4},{6,7},{7,6},{8,9},{9,8},{10,11... | collective-permute-start | bytes 1572872 | tf_op jit(solution)/shard_map/ppermute | solution.py:405
  11.9 3.7 %all-to-all-start = ((f32[8,128,128]{2,1,0:T(8,128)}), f32[8,128,128]{2,1,0:T(8,128)S(1)}, u32[]{:S(2)}, u32[]{:S(2)}) async-start(f32[8,128,128]{2,1,0:T(8,128)} %get-tuple-element.18), calls=%async_computation | async-start | bytes 1048576 | tf_op jit(solution)/shard_map/all_to_all | solution.py:426
  15.6 8.4 %collective-permute-done.far = f32[8,128,128]{2,1,0:T(8,128)S(1)} collective-permute-done((f32[8,128,128]{2,1,0:T(8,128)}, f32[8,128,128]{2,1,0:T(8,128)S(1)}, u32[]{:S(2)}, u32[]{:S(2)}) %collective-permute-start) | collective-permute-done | bytes 524320 | tf_op jit(solution)/shard_map/ppermute | solution.py:405
  24.0 1.0 %copy-done.3 = f32[8,128,128]{2,1,0:T(8,128)S(1)} copy-done((f32[8,128,128]{2,1,0:T(8,128)S(1)}, f32[8,128,128]{2,1,0:T(8,128)}, u32[]{:S(2)}) %copy-start.3) | copy-done | bytes 524312
  25.0 1.0 %copy-done.4 = f32[8,128,128]{2,1,0:T(8,128)S(1)} copy-done((f32[8,128,128]{2,1,0:T(8,128)S(1)}, f32[8,128,128]{2,1,0:T(8,128)}, u32[]{:S(2)}) %copy-start.4) | copy-done | bytes 524312
  26.1 1.1 %shard_map.150 = (f32[8,128,128]{2,1,0:T(8,128)}, f32[8,128,128]{2,1,0:T(8,128)}) custom-call(f32[8,128,128]{2,1,0:T(8,128)S(1)} %copy-done.4, f32[8,128,128]{2,1,0:T(8,128)S(1)} %collective-permute-done.far, f32[8,128,128]{2,1,0:T(8,128)S(1)} %copy-done.3), custom_call_target="tpu_custom_call" | custom-call | flops 1048576 | bytes 65536 | tf_op jit(solution)/shard_map/pallas_call | solution.py:316
  27.2 1.7 %collective-permute-start.1 = (f32[8,128,128]{2,1,0:T(8,128)}, f32[8,128,128]{2,1,0:T(8,128)S(1)}, u32[]{:S(2)}, u32[]{:S(2)}) collective-permute-start(f32[8,128,128]{2,1,0:T(8,128)} %get-tuple-element.16), channel_id=1, source_target_pairs={{0,1},{1,0},{2,3},{3,2},{4,5},{5,4},{6,7},{7,6},{8,9},{9,8},{10,11... | collective-permute-start | bytes 1572872 | tf_op jit(solution)/shard_map/ppermute | solution.py:405
  28.9 2.6 %collective-permute-start.2 = (f32[8,128,128]{2,1,0:T(8,128)}, f32[8,128,128]{2,1,0:T(8,128)}, u32[]{:S(2)}, u32[]{:S(2)}) collective-permute-start(f32[8,128,128]{2,1,0:T(8,128)} %get-tuple-element.17.refs_0_), channel_id=1, source_target_pairs={{0,2},{2,0},{1,3},{3,1},{4,6},{6,4},{5,7},{7,5},{8,10},{10,8},{9,1... | collective-permute-start | bytes 1572872 | tf_op jit(solution)/shard_map/ppermute | solution.py:405
  31.5 0.0 all-to-all-done
  31.5 0.0 copy-done.2
  31.5 0.0 copy-done.7
  31.5 0.0 copy-done.8
  31.5 1.5 %shard_map.151 = f32[1024,128]{1,0:T(8,128)S(1)} custom-call(f32[1024,128]{1,0:T(8,128)S(1)} %bitcast.5, f32[512,8]{1,0:T(8,128)S(1)} %copy-done.2, bf16[1024,256]{1,0:T(8,128)(2,1)S(1)} %copy-done.8, bf16[1024,256]{1,0:T(8,128)(2,1)S(1)} %copy-done.7, f32[8,128,128]{2,1,0:T(8,128)} %get-tuple-element.17.refs_0_), custom_call_target="tpu_custom_call" | custom-call | flops 1048576 | bytes 65536 | tf_op jit(solution)/shard_map/pallas_call | solution.py:316
  33.0 0.0 copy-start
  33.0 0.0 copy-start.1
  33.0 0.0 copy-start.10
  33.1 13.4 %all_to_all.20.half.refs_0_ = f32[8,128,128]{2,1,0:T(8,128)S(1)} all-to-all(f32[8,128,128]{2,1,0:T(8,128)S(1)} %bitcast.7), channel_id=1, replica_groups=mesh['wide'=8,'narrow'=4] {'wide'}, dimensions={0} | all-to-all | bytes 1048576 | tf_op jit(solution)/shard_map/all_to_all | solution.py:436
  46.5 5.1 %collective-permute-done.1.near = f32[8,128,128]{2,1,0:T(8,128)S(1)} collective-permute-done((f32[8,128,128]{2,1,0:T(8,128)}, f32[8,128,128]{2,1,0:T(8,128)S(1)}, u32[]{:S(2)}, u32[]{:S(2)}) %collective-permute-start.1) | collective-permute-done | bytes 524320 | tf_op jit(solution)/shard_map/ppermute | solution.py:405
  51.6 2.3 %collective-permute-done.2.skip = f32[8,128,128]{2,1,0:T(8,128)} collective-permute-done((f32[8,128,128]{2,1,0:T(8,128)}, f32[8,128,128]{2,1,0:T(8,128)}, u32[]{:S(2)}, u32[]{:S(2)}) %collective-permute-start.2) | collective-permute-done | bytes 524320 | tf_op jit(solution)/shard_map/ppermute | solution.py:405
  53.9 0.0 copy-done.9
  53.9 1.9 %shard_map.152 = (f32[8,128,128]{2,1,0:T(8,128)}, f32[4,128,128]{2,1,0:T(8,128)S(1)}, f32[4,128,128]{2,1,0:T(8,128)S(1)}) custom-call(f32[8,128,128]{2,1,0:T(8,128)S(1)} %copy-done.9, f32[8,128,128]{2,1,0:T(8,128)S(1)} %collective-permute-done.1.near, f32[8,128,128]{2,1,0:T(8,128)} %collective-permute-done.2.skip, f32[8,128,128]{2,1,0:T(8,128)S(1)} %all_to_all.20.half.refs_0_), custom_call_target="tpu_custom_call" | custom-call | flops 1048576 | bytes 65536 | tf_op jit(solution)/shard_map/pallas_call | solution.py:316
  55.9 0.7 copy-done.12
  56.6 0.7 copy-done.13
  57.3 3.7 %all-to-all-start.2 = ((f32[8,128,128]{2,1,0:T(8,128)}), f32[8,128,128]{2,1,0:T(8,128)S(1)}, u32[]{:S(2)}, u32[]{:S(2)}) async-start(f32[8,128,128]{2,1,0:T(8,128)} %get-tuple-element.19), calls=%async_computation.2 | async-start | bytes 1048576 | tf_op jit(solution)/shard_map/all_to_all | solution.py:445
  61.0 0.4 collective-permute-start.3
  61.5 2.6 %collective-permute-start.4 = (f32[4,128,128]{2,1,0:T(8,128)}, f32[4,128,128]{2,1,0:T(8,128)}, u32[]{:S(2)}, u32[]{:S(2)}) collective-permute-start(f32[4,128,128]{2,1,0:T(8,128)} %copy-done.13), channel_id=1, source_target_pairs={{0,2},{2,0},{1,3},{3,1},{4,6},{6,4},{5,7},{7,5},{8,10},{10,8},{9,1... | collective-permute-start | bytes 786440 | tf_op jit(solution)/shard_map/ppermute | solution.py:405
  64.0 0.3 collective-permute-start.6
  64.4 6.4 %all-to-all-done.2 = f32[8,128,128]{2,1,0:T(8,128)S(1)} async-done(((f32[8,128,128]{2,1,0:T(8,128)}), f32[8,128,128]{2,1,0:T(8,128)S(1)}, u32[]{:S(2)}, u32[]{:S(2)}) %all-to-all-start.2) | async-done | bytes 524320 | tf_op jit(solution)/shard_map/all_to_all | solution.py:445
  70.8 0.0 copy-done.5
  70.8 1.0 %copy-done.6 = bf16[512,512]{1,0:T(8,128)(2,1)S(1)} copy-done((bf16[512,512]{1,0:T(8,128)(2,1)S(1)}, bf16[512,512]{1,0:T(8,128)(2,1)}, u32[]{:S(2)}) %copy-start.6) | copy-done | bytes 524312
  71.8 2.8 %shard_map.153 = f32[1024,128]{1,0:T(8,128)} custom-call(f32[1024,128]{1,0:T(8,128)S(1)} %bitcast.6, f32[512,8]{1,0:T(8,128)S(1)} %copy-done.2, bf16[512,512]{1,0:T(8,128)(2,1)S(1)} %copy-done.6, bf16[512,512]{1,0:T(8,128)(2,1)S(1)} %copy-done.5), custom_call_target="tpu_custom_call" | custom-call | flops 1048576 | bytes 65536 | tf_op jit(solution)/shard_map/pallas_call | solution.py:316
  74.6 3.5 %all-to-all-start.3 = ((f32[8,128,128]{2,1,0:T(8,128)}), f32[8,128,128]{2,1,0:T(8,128)S(1)}, u32[]{:S(2)}, u32[]{:S(2)}) async-start(f32[8,128,128]{2,1,0:T(8,128)} %bitcast.4), calls=%async_computation.3 | async-start | bytes 1048576 | tf_op jit(solution)/shard_map/all_to_all | solution.py:454
  78.1 1.3 %collective-permute-done.4.refs_2_ = f32[4,128,128]{2,1,0:T(8,128)} collective-permute-done((f32[4,128,128]{2,1,0:T(8,128)}, f32[4,128,128]{2,1,0:T(8,128)}, u32[]{:S(2)}, u32[]{:S(2)}) %collective-permute-start.4) | collective-permute-done | bytes 262176 | tf_op jit(solution)/shard_map/ppermute | solution.py:405
  79.5 3.2 %collective-permute-start.5 = (f32[4,128,128]{2,1,0:T(8,128)}, f32[4,128,128]{2,1,0:T(8,128)S(1)}, u32[]{:S(2)}, u32[]{:S(2)}) collective-permute-start(f32[4,128,128]{2,1,0:T(8,128)} %collective-permute-done.4.refs_2_), channel_id=1, source_target_pairs={{0,1},{1,0},{2,3},{3,2},{4,5},{5,4},{6,7},{7,6},{8,9},{9,8},{10,11... | collective-permute-start | bytes 786440 | tf_op jit(solution)/shard_map/ppermute | solution.py:405
  82.6 5.5 %collective-permute-done.6.refs_2_ = f32[4,128,128]{2,1,0:T(8,128)} collective-permute-done((f32[4,128,128]{2,1,0:T(8,128)}, f32[4,128,128]{2,1,0:T(8,128)}, u32[]{:S(2)}, u32[]{:S(2)}) %collective-permute-start.6) | collective-permute-done | bytes 262176 | tf_op jit(solution)/shard_map/ppermute | solution.py:405
  88.1 0.1 collective-permute-start.7
  88.2 0.0 collective-permute-done.3.refs_1_
  88.2 4.4 %collective-permute-done.5.refs_3_ = f32[4,128,128]{2,1,0:T(8,128)S(1)} collective-permute-done((f32[4,128,128]{2,1,0:T(8,128)}, f32[4,128,128]{2,1,0:T(8,128)S(1)}, u32[]{:S(2)}, u32[]{:S(2)}) %collective-permute-start.5) | collective-permute-done | bytes 262176 | tf_op jit(solution)/shard_map/ppermute | solution.py:405
  92.6 0.0 copy-done
  92.6 4.6 %shard_map.155._ = f32[2,2,128,2048]{3,2,1,0:T(8,128)} custom-call(s32[1]{0:T(128)} %bitcast.place, f32[8,512]{1,0:T(8,128)S(1)} %copy-done.10, f32[8,128,128]{2,1,0:T(8,128)S(1)} %all_to_all.20.half.refs_0_, f32[8,128,128]{2,1,0:T(8,128)S(1)} %collective-permute-done.3.refs_1_, f32[4,128,128]{2,1,0:T(8,128)} %collective-permute-done.4.refs_2_, ...), custom_call_target="tpu_custom_call" | custom-call | flops 1048576 | bytes 65536 | tf_op jit(solution)/shard_map/pallas_call | solution.py:379
  97.2 0.6 collective-permute-done.7.refs_3_
  97.8 4.6 %shard_map.156 = f32[2,2,128,2048]{3,2,1,0:T(8,128)} custom-call(s32[1]{0:T(128)} %bitcast.place, f32[2,2,128,2048]{3,2,1,0:T(8,128)} %shard_map.155._, f32[8,128,128]{2,1,0:T(8,128)S(1)} %all_to_all.20.half.refs_0_, f32[8,128,128]{2,1,0:T(8,128)S(1)} %collective-permute-done.3.refs_1_, ...), custom_call_target="tpu_custom_call", output_to_operand_aliasing={{}: (1, {})} | custom-call | flops 1048576 | bytes 65536 | tf_op jit(solution)/shard_map/pallas_call | solution.py:379
  102.4 0.0 all-to-all-done.3.blocks
  102.4 1.3 %shard_map.154 = f32[2,2,128,256]{3,2,1,0:T(8,128)} custom-call(f32[8,128,128]{2,1,0:T(8,128)S(1)} %all-to-all-done.3.blocks, bf16[256,256]{1,0:T(8,128)(2,1)S(1)} %copy-done.11), custom_call_target="tpu_custom_call" | custom-call | flops 1048576 | bytes 65536 | tf_op jit(solution)/shard_map/pallas_call | solution.py:316
  (11 shorter events, 0.0 us)
Async XLA Ops:
  0.6 30.9 %copy-start.2 = (f32[512,8]{1,0:T(8,128)S(1)}, f32[512,8]{1,0:T(8,128)}, u32[]{:S(2)}) copy-start(f32[512,8]{1,0:T(8,128)} %constant.32.clone.tw) | copy-start | bytes 49156
  0.6 30.9 %copy-start.7 = (bf16[1024,256]{1,0:T(8,128)(2,1)S(1)}, bf16[1024,256]{1,0:T(8,128)(2,1)}, u32[]{:S(2)}) copy-start(bf16[1024,256]{1,0:T(8,128)(2,1)} %constant.34.clone.t_lo) | copy-start | bytes 1572868
  0.7 30.8 %copy-start.8 = (bf16[1024,256]{1,0:T(8,128)(2,1)S(1)}, bf16[1024,256]{1,0:T(8,128)(2,1)}, u32[]{:S(2)}) copy-start(bf16[1024,256]{1,0:T(8,128)(2,1)} %constant.33.clone.t_hi) | copy-start | bytes 1572868
  8.8 45.1 %copy-start.9 = (f32[8,128,128]{2,1,0:T(8,128)S(1)}, f32[8,128,128]{2,1,0:T(8,128)}, u32[]{:S(2)}) copy-start(f32[8,128,128]{2,1,0:T(8,128)} %get-tuple-element.12.own) | copy-start | bytes 1572868
  8.8 15.2 %collective-permute-start = (f32[8,128,128]{2,1,0:T(8,128)}, f32[8,128,128]{2,1,0:T(8,128)S(1)}, u32[]{:S(2)}, u32[]{:S(2)}) collective-permute-start(f32[8,128,128]{2,1,0:T(8,128)} %get-tuple-element.14), channel_id=1, source_target_pairs={{0,1},{1,0},{2,3},{3,2},{4,5},{5,4},{6,7},{7,6},{8,9},{9,8},{10,11... | collective-permute-start | bytes 1572872 | tf_op jit(solution)/shard_map/ppermute | solution.py:405
  11.9 19.6 %all-to-all-start = ((f32[8,128,128]{2,1,0:T(8,128)}), f32[8,128,128]{2,1,0:T(8,128)S(1)}, u32[]{:S(2)}, u32[]{:S(2)}) async-start(f32[8,128,128]{2,1,0:T(8,128)} %get-tuple-element.18), calls=%async_computation | async-start | bytes 1048576 | tf_op jit(solution)/shard_map/all_to_all | solution.py:426
  24.0 1.0 %copy-start.3 = (f32[8,128,128]{2,1,0:T(8,128)S(1)}, f32[8,128,128]{2,1,0:T(8,128)}, u32[]{:S(2)}) copy-start(f32[8,128,128]{2,1,0:T(8,128)} %get-tuple-element.15.near) | copy-start | bytes 1572868
  25.0 1.0 %copy-start.4 = (f32[8,128,128]{2,1,0:T(8,128)S(1)}, f32[8,128,128]{2,1,0:T(8,128)}, u32[]{:S(2)}) copy-start(f32[8,128,128]{2,1,0:T(8,128)} %get-tuple-element.13.blocks) | copy-start | bytes 1572868
  26.1 44.7 %copy-start.5 = (bf16[512,512]{1,0:T(8,128)(2,1)S(1)}, bf16[512,512]{1,0:T(8,128)(2,1)}, u32[]{:S(2)}) copy-start(bf16[512,512]{1,0:T(8,128)(2,1)} %constant.36.clone.t_lo) | copy-start | bytes 1572868
  27.2 24.4 %collective-permute-start.1 = (f32[8,128,128]{2,1,0:T(8,128)}, f32[8,128,128]{2,1,0:T(8,128)S(1)}, u32[]{:S(2)}, u32[]{:S(2)}) collective-permute-start(f32[8,128,128]{2,1,0:T(8,128)} %get-tuple-element.16), channel_id=1, source_target_pairs={{0,1},{1,0},{2,3},{3,2},{4,5},{5,4},{6,7},{7,6},{8,9},{9,8},{10,11... | collective-permute-start | bytes 1572872 | tf_op jit(solution)/shard_map/ppermute | solution.py:405
  28.9 25.0 %collective-permute-start.2 = (f32[8,128,128]{2,1,0:T(8,128)}, f32[8,128,128]{2,1,0:T(8,128)}, u32[]{:S(2)}, u32[]{:S(2)}) collective-permute-start(f32[8,128,128]{2,1,0:T(8,128)} %get-tuple-element.17.refs_0_), channel_id=1, source_target_pairs={{0,2},{2,0},{1,3},{3,1},{4,6},{6,4},{5,7},{7,5},{8,10},{10,8},{9,1... | collective-permute-start | bytes 1572872 | tf_op jit(solution)/shard_map/ppermute | solution.py:405
  33.0 59.6 %copy-start = (bf16[512,512]{1,0:T(8,128)(2,1)S(1)}, bf16[512,512]{1,0:T(8,128)(2,1)}, u32[]{:S(2)}) copy-start(bf16[512,512]{1,0:T(8,128)(2,1)} %constant.39.clone.refs_6_) | copy-start | bytes 1572868
  33.0 59.5 %copy-start.1 = (bf16[512,512]{1,0:T(8,128)(2,1)S(1)}, bf16[512,512]{1,0:T(8,128)(2,1)}, u32[]{:S(2)}) copy-start(bf16[512,512]{1,0:T(8,128)(2,1)} %constant.38.clone.refs_5_) | copy-start | bytes 1572868
  33.0 59.5 %copy-start.10 = (f32[8,512]{1,0:T(8,128)S(1)}, f32[8,512]{1,0:T(8,128)}, u32[]{:S(2)}) copy-start(f32[8,512]{1,0:T(8,128)} %constant.28.clone.tw._.refs_4_) | copy-start | bytes 49156
  55.9 0.7 copy-start.12
  56.6 0.7 copy-start.13
  57.3 13.5 %all-to-all-start.2 = ((f32[8,128,128]{2,1,0:T(8,128)}), f32[8,128,128]{2,1,0:T(8,128)S(1)}, u32[]{:S(2)}, u32[]{:S(2)}) async-start(f32[8,128,128]{2,1,0:T(8,128)} %get-tuple-element.19), calls=%async_computation.2 | async-start | bytes 1048576 | tf_op jit(solution)/shard_map/all_to_all | solution.py:445
  61.0 27.2 %collective-permute-start.3 = (f32[8,128,128]{2,1,0:T(8,128)S(1)}, f32[8,128,128]{2,1,0:T(8,128)S(1)}, u32[]{:S(2)}, u32[]{:S(2)}) collective-permute-start(f32[8,128,128]{2,1,0:T(8,128)S(1)} %all_to_all.20.half.refs_0_), channel_id=1, source_target_pairs={{0,1},{1,0},{2,3},{3,2},{4,5},{5,4},{6,7},{7,6},{8,9},{9,8},{10,11... | collective-permute-start | bytes 1572872 | tf_op jit(solution)/shard_map/ppermute | solution.py:405
  61.5 18.0 %collective-permute-start.4 = (f32[4,128,128]{2,1,0:T(8,128)}, f32[4,128,128]{2,1,0:T(8,128)}, u32[]{:S(2)}, u32[]{:S(2)}) collective-permute-start(f32[4,128,128]{2,1,0:T(8,128)} %copy-done.13), channel_id=1, source_target_pairs={{0,2},{2,0},{1,3},{3,1},{4,6},{6,4},{5,7},{7,5},{8,10},{10,8},{9,1... | collective-permute-start | bytes 786440 | tf_op jit(solution)/shard_map/ppermute | solution.py:405
  64.0 24.1 %collective-permute-start.6 = (f32[4,128,128]{2,1,0:T(8,128)}, f32[4,128,128]{2,1,0:T(8,128)}, u32[]{:S(2)}, u32[]{:S(2)}) collective-permute-start(f32[4,128,128]{2,1,0:T(8,128)} %copy-done.12), channel_id=1, source_target_pairs={{0,2},{2,0},{1,3},{3,1},{4,6},{6,4},{5,7},{7,5},{8,10},{10,8},{9,1... | collective-permute-start | bytes 786440 | tf_op jit(solution)/shard_map/ppermute | solution.py:405
  70.8 1.0 %copy-start.6 = (bf16[512,512]{1,0:T(8,128)(2,1)S(1)}, bf16[512,512]{1,0:T(8,128)(2,1)}, u32[]{:S(2)}) copy-start(bf16[512,512]{1,0:T(8,128)(2,1)} %constant.35.clone.t_hi) | copy-start | bytes 1572868
  74.6 27.8 %all-to-all-start.3 = ((f32[8,128,128]{2,1,0:T(8,128)}), f32[8,128,128]{2,1,0:T(8,128)S(1)}, u32[]{:S(2)}, u32[]{:S(2)}) async-start(f32[8,128,128]{2,1,0:T(8,128)} %bitcast.4), calls=%async_computation.3 | async-start | bytes 1048576 | tf_op jit(solution)/shard_map/all_to_all | solution.py:454
  79.5 13.1 %collective-permute-start.5 = (f32[4,128,128]{2,1,0:T(8,128)}, f32[4,128,128]{2,1,0:T(8,128)S(1)}, u32[]{:S(2)}, u32[]{:S(2)}) collective-permute-start(f32[4,128,128]{2,1,0:T(8,128)} %collective-permute-done.4.refs_2_), channel_id=1, source_target_pairs={{0,1},{1,0},{2,3},{3,2},{4,5},{5,4},{6,7},{7,6},{8,9},{9,8},{10,11... | collective-permute-start | bytes 786440 | tf_op jit(solution)/shard_map/ppermute | solution.py:405
  88.1 9.7 %collective-permute-start.7 = (f32[4,128,128]{2,1,0:T(8,128)}, f32[4,128,128]{2,1,0:T(8,128)S(1)}, u32[]{:S(2)}, u32[]{:S(2)}) collective-permute-start(f32[4,128,128]{2,1,0:T(8,128)} %collective-permute-done.6.refs_2_), channel_id=1, source_target_pairs={{0,1},{1,0},{2,3},{3,2},{4,5},{5,4},{6,7},{7,6},{8,9},{9,8},{10,11... | collective-permute-start | bytes 786440 | tf_op jit(solution)/shard_map/ppermute | solution.py:405
  97.2 5.2 %copy-start.11 = (bf16[256,256]{1,0:T(8,128)(2,1)S(1)}, bf16[256,256]{1,0:T(8,128)(2,1)}, u32[]{:S(2)}) copy-start(bf16[256,256]{1,0:T(8,128)(2,1)} %constant.37.clone.order) | copy-start | bytes 393220

commit v3 on v2

--- a/solution.py
+++ b/solution.py
@@ -180,13 +180,15 @@
             out[at], out[at + 1] = paired(lanes[:rows], lanes[rows:])
 
 
-def start_kernel(shards, place, cur, tw, t_hi, t_lo, grad, order, sorted_, *refs):
-    outs, held = refs[:-1], refs[-1]
+def x_kernel(shards, place, cur, tw, t_hi, t_lo, *refs):
+    outs, held = refs[-shards - 1 : -1], refs[-1]
     rows = cur.shape[2]
 
-    @pl.when((pl.program_id(0) == 0) & (pl.program_id(1) == 0))
-    def _():
-        sort(grad, order, sorted_)
+    if len(refs) > shards + 1:
+
+        @pl.when(pl.program_id(0) == 0)
+        def _():
+            sort(*refs[1:4])
 
     re = [cur[0, 0, :, a * SPAN : (a + 1) * SPAN] for a in range(RADIX)]
     im = [cur[0, 1, :, a * SPAN : (a + 1) * SPAN] for a in range(RADIX)]
@@ -256,7 +258,8 @@
 
 
 def x_back_kernel(place, _, *refs):
-    blocks, (tw, t_hi, t_lo, out, hi_ref, lo_ref) = refs[:-6], refs[-6:]
+    blocks, (tw, t_hi, t_lo, out, done, hi_ref, lo_ref) = refs[:-7], refs[-7:]
+    done[...] = jnp.zeros(done.shape, f32)
     rows = out.shape[2]
     flat = RADIX * rows
     sign = sign_of((flat, LANES))
@@ -310,7 +313,10 @@
 COST = pl.CostEstimate(flops=1 << 20, bytes_accessed=1 << 16, transcendentals=0)
 
 
-def whole(kernel, shapes, *args, after=(), params=SHARED):
+LONG = pl.CostEstimate(flops=1 << 37, bytes_accessed=1 << 29, transcendentals=0)
+
+
+def whole(kernel, shapes, *args, after=(), params=SHARED, cost=COST):
     shapes = [jax.ShapeDtypeStruct(shape, f32) for shape in shapes]
     in_vmem = pl.BlockSpec(memory_space=pltpu.VMEM)
     result = pl.pallas_call(
@@ -319,54 +325,61 @@
         in_specs=[in_vmem] * len(args) + [pl.BlockSpec(memory_space=pl.ANY)] * len(after),
         out_specs=[in_vmem] * len(shapes),
         compiler_params=params,
-        cost_estimate=COST,
+        cost_estimate=cost,
     )(*args, *after)
     return result if len(shapes) > 1 else result[0]
 
 
-def onward_kernel(blocks, far, near, *refs):
-    refs[-2][...] = blocks[...] + far[...]
-    refs[-1][...] = near[...]
-
-
-def total_kernel(own, near, skip, half, *refs):
-    out, first, second = refs[-3:]
-    out[...] = (own[...] + near[...]) + skip[...]
-    first[...] = half[:RADIX]
-    second[...] = half[RADIX:]
+def zero_kernel(*refs):
+    refs[-1][...] = jnp.zeros(refs[-1].shape, f32)
+
+
+def zeros_after(*arrays):
+    return whole(zero_kernel, [(8, LANES)], after=arrays, cost=LONG)
+
+
+def halves_kernel(both, *refs):
+    first, second = refs[-2:]
+    first[...] = both[:RADIX]
+    second[...] = both[RADIX:]
 
 
 def fixed(shape):
     return pl.BlockSpec(shape, lambda *_: (0,) * len(shape))
 
 
-def start(place, currents, far_gradient, shards, tables):
+def project_x(place, currents, component, shards, tables, far_gradient=None, after=None):
     rows, columns = currents.shape[2:]
     tile = rows // 2
     t_hi, t_lo = tables["x"]
-    sorted_shape = (2 * RADIX, far_gradient.shape[2], LANES)
+    args = [place, currents, tables["row_tw"], t_hi, t_lo]
+    in_specs = [
+        pl.BlockSpec((1, 2, tile, columns), lambda i, _: (component, 0, i, 0)),
+        fixed((2 * RADIX, SPAN)),
+        fixed(t_hi.shape),
+        fixed(t_lo.shape),
+    ]
+    out_specs = [pl.BlockSpec((RADIX, tile, LANES), lambda i, _: (0, i, 0))] * shards
+    shapes = [(RADIX, rows, LANES)] * shards
+    if far_gradient is not None:
+        args += [after, far_gradient, tables["order"]]
+        in_specs += [pl.BlockSpec(memory_space=pl.ANY)]
+        in_specs += [fixed(far_gradient.shape), fixed(tables["order"].shape)]
+        shapes.insert(0, (2 * RADIX, far_gradient.shape[2], LANES))
+        out_specs.insert(0, fixed(shapes[0]))
     return pl.pallas_call(
-        functools.partial(start_kernel, shards),
+        functools.partial(x_kernel, shards),
         grid_spec=pltpu.PrefetchScalarGridSpec(
             num_scalar_prefetch=1,
-            grid=(2, rows // tile),
-            in_specs=[
-                pl.BlockSpec((1, 2, tile, columns), lambda c, i, _: (c, 0, i, 0)),
-                fixed((2 * RADIX, SPAN)),
-                fixed(t_hi.shape),
-                fixed(t_lo.shape),
-                fixed(far_gradient.shape),
-                fixed(tables["order"].shape),
-            ],
-            out_specs=[fixed(sorted_shape)]
-            + [pl.BlockSpec((RADIX, tile, LANES), lambda c, i, _: (c, i, 0))] * shards,
+            grid=(rows // tile,),
+            in_specs=in_specs,
+            out_specs=out_specs,
             scratch_shapes=[pltpu.VMEM((shards, RADIX, tile, LANES), f32)],
         ),
-        out_shape=[jax.ShapeDtypeStruct(sorted_shape, f32)]
-        + [jax.ShapeDtypeStruct((2 * RADIX, rows, LANES), f32)] * shards,
+        out_shape=[jax.ShapeDtypeStruct(shape, f32) for shape in shapes],
         compiler_params=ALONE,
         cost_estimate=COST,
-    )(place, currents, tables["row_tw"], t_hi, t_lo, far_gradient, tables["order"])
+    )(*args)
 
 
 def back_x(place, parts, component, grad, shape, tables):
@@ -384,16 +397,19 @@
             in_specs=[pl.BlockSpec(memory_space=pl.ANY)]
             + [both if part.shape[0] > RADIX else one for part in parts]
             + [fixed((2 * RADIX, SPAN)), fixed(t_hi.shape), fixed(t_lo.shape)],
-            out_specs=pl.BlockSpec((1, 2, tile, shape[3]), lambda i, _: (component, 0, i, 0)),
+            out_specs=[
+                pl.BlockSpec((1, 2, tile, shape[3]), lambda i, _: (component, 0, i, 0)),
+                fixed((8, LANES)),
+            ],
             scratch_shapes=[
                 pltpu.VMEM((2 * RADIX * tile, 2 * BANDS), bf16),
                 pltpu.VMEM((2 * RADIX * tile, 2 * BANDS), bf16),
             ],
         ),
-        out_shape=jax.ShapeDtypeStruct(shape, f32),
+        out_shape=[jax.ShapeDtypeStruct(shape, f32), jax.ShapeDtypeStruct((8, LANES), f32)],
         input_output_aliases={} if first else {1: 0},
         compiler_params=SHARED,
-        cost_estimate=COST,
+        cost_estimate=LONG if first else COST,
     )(place, tables["row_tw"] if first else grad, *parts, tables["row_tw"], t_hi, t_lo)
 
 
@@ -416,12 +432,17 @@
     b_hi, b_lo = tables["y_back"]
 
     group = (RADIX, rows, LANES)
-    sorted_, *blocks = start(place, currents, far_gradient, shards, tables)
-    far = send(blocks[3], PAIRS)
-
-    onward, close = whole(onward_kernel, [blocks[0].shape] * 2, blocks[2], far, blocks[1])
+    blocks = [project_x(place, currents, 0, shards, tables)]
+    far = [send(blocks[0][3], PAIRS)]
+    sorted_, *rest = project_x(
+        place, currents, 1, shards, tables, far_gradient, blocks[0][0]
+    )
+    blocks.append(rest)
+    far.append(send(blocks[1][3], PAIRS))
+    later = zeros_after(far[0])[0, 0]
+    onward = jnp.concatenate([blocks[0][2] + far[0], blocks[1][2] + far[1] + later], axis=0)
     skip = send(onward, SKIPS)
-    near = send(close, PAIRS)
+    near = send(jnp.concatenate([blocks[c][1] + later for c in range(2)], axis=0), PAIRS)
 
     rows_in = lax.all_to_all(sorted_, "wide", 0, 0).reshape(MY, LANES)
     rows_out = whole(
@@ -434,12 +455,12 @@
         after=[onward],
     )
     half = lax.all_to_all(rows_out.reshape(wide, rows, LANES), "wide", 0, 0)
-
     beside = send(half, PAIRS)
-    columns, *mine = whole(
-        total_kernel, [blocks[0].shape, group, group], blocks[0], near, skip, half
-    )
-
+
+    columns = jnp.concatenate([blocks[c][0] for c in range(2)], axis=0) + near + skip
+    columns = columns + zeros_after(near)[0, 0]
+
+    mine = whole(halves_kernel, [group, group], half, after=[columns])
     there = [send(m, SKIPS) for m in mine]
 
     rows_in = lax.all_to_all(columns, "wide", 0, 0).reshape(rows * wide, LANES)
@@ -450,14 +471,14 @@
         tables["col_tw"],
         y_hi,
         y_lo,
+        after=[zeros_after(there[0], beside)],
     )
     far = lax.all_to_all(rows_out.reshape(wide, angle_rows, LANES), "wide", 0, 0)
 
     across = [send(t, PAIRS) for t in there]
+    grad, _ = back_x(place, [mine[0], beside, there[0], across[0]], 0, None, currents.shape, tables)
     far_field = whole(unsort_kernel, [far_gradient.shape], far, tables["order_back"])
-    grad = None
-    for c in range(2):
-        grad = back_x(place, [half, beside, there[c], across[c]], c, grad, currents.shape, tables)
+    grad, _ = back_x(place, [mine[1], beside, there[1], across[1]], 1, grad, currents.shape, tables)
     return (far_field, grad)
 
 

time: 104 us -> 96.6 us (0.929)
  blocking collectives: 13.4 us -> 0 us
  other arithmetic: 0 us -> 4.7 us
  local copies, waits for them, and re-layouts: 4.6 us -> 1.16 us
  waiting for transfers between devices: 34 us -> 36.7 us
    all_to_all x1 -> x0, blocking collectives: 13.4 us -> none  [fast_body(): half = lax.all_to_all(rows_out.reshape(wide, rows, LANES), 'wide', 0, 0)]
    all_to_all x0 -> x1, waiting for transfers between devices: none -> 7.26 us  [fast_body(): half = lax.all_to_all(rows_out.reshape(wide, rows, LANES), 'wide', 0, 0)]
    all_to_all x1, waiting for transfers between devices: 6.37 us -> 0.01 us  [fast_body(): rows_in = lax.all_to_all(columns, 'wide', 0, 0).reshape(rows * wide, LANES)]
    unnamed x28 -> x30, local copies, waits for them, and re-layouts: 4.6 us -> 0.07 us
    all_to_all x1, waiting for transfers between devices: 0.01 us -> 4.52 us  [fast_body(): rows_in = lax.all_to_all(sorted_, 'wide', 0, 0).reshape(MY, LANES)]
    add x0 -> x4, other arithmetic: none -> 3.83 us  [the longest x1 1.61 us: fast_body(): blocks[1][2] + far[1] + later]
    all_to_all x0 -> x1, starting transfers between devices: none -> 3.49 us  [fast_body(): half = lax.all_to_all(rows_out.reshape(wide, rows, LANES), 'wide', 0, 0)]
    ppermute x8 -> x9, starting transfers between devices: 14.1 us -> 11 us  [send(): return lax.ppermute(value, 'narrow', pairs)]
  transfers between devices with their start and end apart: 11 -> 13, of which waited for: 8 -> 9; matrix products, arithmetic and copies ran while one was open for 0% -> 6% of each run, Pallas kernels for 14% -> 22%
where the time goes in v3:
time: 96.6 us; the launch traced here: 96.1 us
  waiting for transfers between devices  36.7 us (38%)
  Pallas kernels  26.9 us (28%)
  starting transfers between devices  25.8 us (27%)
  other arithmetic  4.7 us (5%)
  local copies, waits for them, and re-layouts  1.16 us (1%)
    ppermute x9, waiting for transfers between devices, send(): return lax.ppermute(value, 'narrow', pairs)  24.8 us
    ppermute x9, starting transfers between devices, send(): return lax.ppermute(value, 'narrow', pairs)  11 us
    pallas_call x2, Pallas kernels, project_x(): pl.pallas_call(functools.partial(x_kernel, shards), grid_spec=pltpu.Prefe...  10 us
    pallas_call x2, Pallas kernels, back_x(): pl.pallas_call(x_back_kernel, grid_spec=pltpu.PrefetchScalarGridSpec(num_...  9.6 us
    all_to_all x1, waiting for transfers between devices, fast_body(): half = lax.all_to_all(rows_out.reshape(wide, rows, LANES), 'wide', 0, 0)  7.26 us
    pallas_call x7, Pallas kernels, whole(): pl.pallas_call(kernel, out_shape=shapes, in_specs=[in_vmem] * len(args) +...  7.25 us
    all_to_all x1, waiting for transfers between devices, fast_body(): rows_in = lax.all_to_all(sorted_, 'wide', 0, 0).reshape(MY, LANES)  4.52 us
    all_to_all x1, starting transfers between devices, fast_body(): lax.all_to_all(rows_out.reshape(wide, angle_rows, LANES), 'wide', 0, 0)  3.87 us
  transfers between devices with their start and end apart: 13, of which 9 were waited for; matrix products, arithmetic and copies ran while one was open for 6% of the time, Pallas kernels for 22%

profile of v3, /device:TPU:0, one launch (start us, length us, event | category | flops | bytes accessed | tf_op | source)
XLA Modules:
  0.0 96.1 jit_solution(5402955583771314574)
XLA Ops:
  0.6 4.7 %shard_map.149 = (f32[4,128,128]{2,1,0:T(8,128)}, f32[4,128,128]{2,1,0:T(8,128)}, f32[4,128,128]{2,1,0:T(8,128)}, f32[4,128,128]{2,1,0:T(8,128)}) custom-call(s32[1]{0:T(128)} %bitcast.place, f32[2,2,128,2048]{3,2,1,0:T(8,128)} %cur.3, f32[8,512]{1,0:T(8,128)} %constant.28.clone.tw._.refs_4_, bf16[512,512]{1,0:T(8,128)(2,1)} %constant.29.clone.t_hi, ...), custom_call_target="tpu_custom_call" | custom-call | flops 1048576 | bytes 65536 | tf_op jit(solution)/shard_map/pallas_call | solution.py:370
  5.3 3.0 %collective-permute-start = (f32[4,128,128]{2,1,0:T(8,128)}, f32[4,128,128]{2,1,0:T(8,128)S(1)}, u32[]{:S(2)}, u32[]{:S(2)}) collective-permute-start(f32[4,128,128]{2,1,0:T(8,128)} %get-tuple-element.18), channel_id=1, source_target_pairs={{0,1},{1,0},{2,3},{3,2},{4,5},{5,4},{6,7},{7,6},{8,9},{9,8},{10,11... | collective-permute-start | bytes 786440 | tf_op jit(solution)/shard_map/ppermute | solution.py:421
  8.3 5.3 %shard_map.150 = (f32[8,128,128]{2,1,0:T(8,128)}, f32[4,128,128]{2,1,0:T(8,128)}, f32[4,128,128]{2,1,0:T(8,128)}, f32[4,128,128]{2,1,0:T(8,128)}, f32[4,128,128]{2,1,0:T(8,128)}) custom-call(s32[1]{0:T(128)} %bitcast.place, f32[2,2,128,2048]{3,2,1,0:T(8,128)} %cur.3, f32[8,512]{1,0:T(8,128)} %constant.28.clone.tw._.refs_4_, ...), custom_call_target="tpu_custom_call" | custom-call | flops 1048576 | bytes 65536 | tf_op jit(solution)/shard_map/pallas_call | solution.py:370
  13.7 0.1 collective-permute-start.2
  13.8 1.0 %collective-permute-done.refs_0_ = f32[4,128,128]{2,1,0:T(8,128)S(1)} collective-permute-done((f32[4,128,128]{2,1,0:T(8,128)}, f32[4,128,128]{2,1,0:T(8,128)S(1)}, u32[]{:S(2)}, u32[]{:S(2)}) %collective-permute-start) | collective-permute-done | bytes 262176 | tf_op jit(solution)/shard_map/ppermute | solution.py:421
  14.9 0.6 slice.6
  15.4 0.0 copy-done.14
  15.4 0.7 broadcast_add_fusion
  16.1 0.8 pad_maximum_fusion
  16.9 1.8 %collective-permute-start.1 = (f32[8,128,128]{2,1,0:T(8,128)}, f32[8,128,128]{2,1,0:T(8,128)S(1)}, u32[]{:S(2)}, u32[]{:S(2)}) collective-permute-start(f32[8,128,128]{2,1,0:T(8,128)} %pad_maximum_fusion), channel_id=1, source_target_pairs={{0,1},{1,0},{2,3},{3,2},{4,5},{5,4},{6,7},{7,6},{8,9},{9,8},{10,11... | collective-permute-start | bytes 1572872 | tf_op jit(solution)/shard_map/ppermute | solution.py:421
  18.8 3.6 %all-to-all-start.1 = ((f32[8,128,128]{2,1,0:T(8,128)}), f32[8,128,128]{2,1,0:T(8,128)S(1)}, u32[]{:S(2)}, u32[]{:S(2)}) async-start(f32[8,128,128]{2,1,0:T(8,128)} %get-tuple-element.23), calls=%async_computation.1 | async-start | bytes 1048576 | tf_op jit(solution)/shard_map/all_to_all | solution.py:447
  22.5 0.9 collective-permute-done.2
  23.3 1.6 %add_add_fusion = f32[4,128,128]{2,1,0:T(8,128)S(1)} fusion(f32[4,128,128]{2,1,0:T(8,128)S(1)} %copy-done.12, f32[4,128,128]{2,1,0:T(8,128)} %collective-permute-done.2, f32[]{:T(128)} %bitcast.1), kind=kLoop, calls=%fused_computation.5 | loop fusion | flops 131072 | bytes 786436 | tf_op jit(solution)/shard_map/add | solution.py:443
  25.0 2.7 %collective-permute-start.3 = (f32[8,128,128]{2,1,0:T(8,128)S(1)}, f32[8,128,128]{2,1,0:T(8,128)S(1)}, u32[]{:S(2)}, u32[]{:S(2)}) collective-permute-start(f32[8,128,128]{2,1,0:T(8,128)S(1)} %pad_maximum_fusion.1.refs_0_), channel_id=1, source_target_pairs={{0,2},{2,0},{1,3},{3,1},{4,6},{6,4},{5,7},{7,5},{8,10},{10,8},{9,1... | collective-permute-start | bytes 1572872 | tf_op jit(solution)/shard_map/ppermute | solution.py:421
  27.6 4.5 %all-to-all-done.1 = f32[8,128,128]{2,1,0:T(8,128)S(1)} async-done(((f32[8,128,128]{2,1,0:T(8,128)}), f32[8,128,128]{2,1,0:T(8,128)S(1)}, u32[]{:S(2)}, u32[]{:S(2)}) %all-to-all-start.1) | async-done | bytes 524320 | tf_op jit(solution)/shard_map/all_to_all | solution.py:447
  32.2 0.0 copy-done.3
  32.2 2.3 %shard_map.153 = f32[1024,128]{1,0:T(8,128)} custom-call(f32[1024,128]{1,0:T(8,128)S(1)} %bitcast.8, f32[512,8]{1,0:T(8,128)S(1)} %copy-done, bf16[1024,256]{1,0:T(8,128)(2,1)S(1)} %copy-done.4, bf16[1024,256]{1,0:T(8,128)(2,1)S(1)} %copy-done.3, f32[8,128,128]{2,1,0:T(8,128)S(1)} %pad_maximum_fusion.1.refs_0_), custom_call_target="tpu_custom_call" | custom-call | flops 1048576 | bytes 65536 | tf_op jit(solution)/shard_map/pallas_call | solution.py:322
  34.5 3.5 %all-to-all-start.2 = ((f32[8,128,128]{2,1,0:T(8,128)}), f32[8,128,128]{2,1,0:T(8,128)S(1)}, u32[]{:S(2)}, u32[]{:S(2)}) async-start(f32[8,128,128]{2,1,0:T(8,128)} %bitcast.5), calls=%async_computation.2 | async-start | bytes 1048576 | tf_op jit(solution)/shard_map/all_to_all | solution.py:457
  38.0 1.9 %collective-permute-done.1.refs_0_ = f32[8,128,128]{2,1,0:T(8,128)S(1)} collective-permute-done((f32[8,128,128]{2,1,0:T(8,128)}, f32[8,128,128]{2,1,0:T(8,128)S(1)}, u32[]{:S(2)}, u32[]{:S(2)}) %collective-permute-start.1) | collective-permute-done | bytes 524320 | tf_op jit(solution)/shard_map/ppermute | solution.py:421
  39.9 0.5 slice.7
  40.4 7.3 %all-to-all-done.2.both = f32[8,128,128]{2,1,0:T(8,128)S(1)} async-done(((f32[8,128,128]{2,1,0:T(8,128)}), f32[8,128,128]{2,1,0:T(8,128)S(1)}, u32[]{:S(2)}, u32[]{:S(2)}) %all-to-all-start.2) | async-done | bytes 524320 | tf_op jit(solution)/shard_map/all_to_all | solution.py:457
  47.7 0.4 collective-permute-start.5
  48.1 2.7 %collective-permute-done.3 = f32[8,128,128]{2,1,0:T(8,128)S(1)} collective-permute-done((f32[8,128,128]{2,1,0:T(8,128)S(1)}, f32[8,128,128]{2,1,0:T(8,128)S(1)}, u32[]{:S(2)}, u32[]{:S(2)}) %collective-permute-start.3) | collective-permute-done | bytes 524320 | tf_op jit(solution)/shard_map/ppermute | solution.py:421
  50.8 0.0 copy-done.10
  50.8 1.5 %fusion.1.refs_0_ = f32[8,128,128]{2,1,0:T(8,128)} fusion(f32[8,128,128]{2,1,0:T(8,128)S(1)} %collective-permute-done.3, f32[8,128,128]{2,1,0:T(8,128)S(1)} %collective-permute-done.1.refs_0_, f32[4,128,128]{2,1,0:T(8,128)S(1)} %copy-done.10, f32[4,128,128]{2,1,0:T(8,128)S(1)} %copy-done.9, f32[]{:T(128)} %bitcast.2), kind=kLoop, calls=%fused_computation.2 | loop fusion | flops 524288 | bytes 2097156 | tf_op jit(solution)/shard_map/add | solution.py:461
  52.3 0.8 shard_map.154
  53.2 0.0 collective-permute-start.4
  53.2 2.9 %collective-permute-start.7 = (f32[4,128,128]{2,1,0:T(8,128)}, f32[4,128,128]{2,1,0:T(8,128)}, u32[]{:S(2)}, u32[]{:S(2)}) collective-permute-start(f32[4,128,128]{2,1,0:T(8,128)} %get-tuple-element.26.refs_0_), channel_id=1, source_target_pairs={{0,2},{2,0},{1,3},{3,1},{4,6},{6,4},{5,7},{7,5},{8,10},{10,8},{9,1... | collective-permute-start | bytes 786440 | tf_op jit(solution)/shard_map/ppermute | solution.py:421
  56.1 3.8 %all-to-all-start = ((f32[8,128,128]{2,1,0:T(8,128)}), f32[8,128,128]{2,1,0:T(8,128)S(1)}, u32[]{:S(2)}, u32[]{:S(2)}) async-start(f32[8,128,128]{2,1,0:T(8,128)} %fusion.1.refs_0_), calls=%async_computation | async-start | bytes 1048576 | tf_op jit(solution)/shard_map/all_to_all | solution.py:466
  59.9 0.0 copy-start.2
  60.0 0.0 copy-start.5
  60.0 0.0 copy-start.6
  60.0 0.0 copy-start.7
  60.0 14.8 %collective-permute-done.4.refs_0_.refs_2_ = f32[4,128,128]{2,1,0:T(8,128)} collective-permute-done((f32[4,128,128]{2,1,0:T(8,128)}, f32[4,128,128]{2,1,0:T(8,128)}, u32[]{:S(2)}, u32[]{:S(2)}) %collective-permute-start.4) | collective-permute-done | bytes 262176 | tf_op jit(solution)/shard_map/ppermute | solution.py:421
  74.8 0.0 collective-permute-start.6
  74.8 3.5 %collective-permute-done.7.refs_2_ = f32[4,128,128]{2,1,0:T(8,128)} collective-permute-done((f32[4,128,128]{2,1,0:T(8,128)}, f32[4,128,128]{2,1,0:T(8,128)}, u32[]{:S(2)}, u32[]{:S(2)}) %collective-permute-start.7) | collective-permute-done | bytes 262176 | tf_op jit(solution)/shard_map/ppermute | solution.py:421
  78.3 0.0 collective-permute-start.8
  78.3 0.0 collective-permute-done.5.refs_1_
  78.3 0.0 all-to-all-done
  78.3 0.0 copy-done.1
  78.3 2.8 %shard_map.156 = f32[1024,128]{1,0:T(8,128)} custom-call(f32[1024,128]{1,0:T(8,128)S(1)} %bitcast.7, f32[512,8]{1,0:T(8,128)S(1)} %copy-done, bf16[512,512]{1,0:T(8,128)(2,1)S(1)} %copy-done.2, bf16[512,512]{1,0:T(8,128)(2,1)S(1)} %copy-done.1, f32[8,128]{1,0:T(8,128)S(1)} %shard_map.155.refs_0_), custom_call_target="tpu_custom_call" | custom-call | flops 1048576 | bytes 65536 | tf_op jit(solution)/shard_map/pallas_call | solution.py:322
  81.2 3.9 %all-to-all-start.3 = ((f32[8,128,128]{2,1,0:T(8,128)}), f32[8,128,128]{2,1,0:T(8,128)S(1)}, u32[]{:S(2)}, u32[]{:S(2)}) async-start(f32[8,128,128]{2,1,0:T(8,128)} %bitcast.6), calls=%async_computation.3 | async-start | bytes 1048576 | tf_op jit(solution)/shard_map/all_to_all | solution.py:476
  85.0 0.0 collective-permute-done.6.refs_3_
  85.1 4.8 %shard_map.158 = (f32[2,2,128,2048]{3,2,1,0:T(8,128)}, f32[8,128]{1,0:T(8,128)}) custom-call(s32[1]{0:T(128)} %bitcast.place, f32[8,512]{1,0:T(8,128)S(1)} %copy-done.7, f32[4,128,128]{2,1,0:T(8,128)} %get-tuple-element.24.refs_0_, f32[8,128,128]{2,1,0:T(8,128)} %collective-permute-done.5.refs_1_, f32[4,128,128]{2,1,0:T(8,128)} %collective-permute-done.4.refs_0_.refs_2_, ...), custom_call_target="tpu_custom_call" | custom-call | flops 137438953472 | bytes 536870912 | tf_op jit(solution)/shard_map/pallas_call | solution.py:392
  89.9 0.0 collective-permute-done.8.refs_3_
  89.9 4.8 %shard_map.159 = (f32[2,2,128,2048]{3,2,1,0:T(8,128)}, f32[8,128]{1,0:T(8,128)}) custom-call(s32[1]{0:T(128)} %bitcast.place, f32[2,2,128,2048]{3,2,1,0:T(8,128)} %get-tuple-element.25._, f32[4,128,128]{2,1,0:T(8,128)} %get-tuple-element.26.refs_0_, f32[8,128,128]{2,1,0:T(8,128)} %collective-permute-done.5.refs_1_, ...), custom_call_target="tpu_custom_call", output_to_operand_aliasing={{0}: (1, {})} | custom-call | flops 1048576 | bytes 65536 | tf_op jit(solution)/shard_map/pallas_call | solution.py:392
  94.7 0.1 all-to-all-done.3.blocks
  94.8 1.3 %shard_map.157 = f32[2,2,128,256]{3,2,1,0:T(8,128)} custom-call(f32[8,128,128]{2,1,0:T(8,128)S(1)} %all-to-all-done.3.blocks, bf16[256,256]{1,0:T(8,128)(2,1)S(1)} %copy-done.8), custom_call_target="tpu_custom_call" | custom-call | flops 1048576 | bytes 65536 | tf_op jit(solution)/shard_map/pallas_call | solution.py:322
  (27 shorter events, 0.1 us)
Async XLA Ops:
  5.3 9.5 %collective-permute-start = (f32[4,128,128]{2,1,0:T(8,128)}, f32[4,128,128]{2,1,0:T(8,128)S(1)}, u32[]{:S(2)}, u32[]{:S(2)}) collective-permute-start(f32[4,128,128]{2,1,0:T(8,128)} %get-tuple-element.18), channel_id=1, source_target_pairs={{0,1},{1,0},{2,3},{3,2},{4,5},{5,4},{6,7},{7,6},{8,9},{9,8},{10,11... | collective-permute-start | bytes 786440 | tf_op jit(solution)/shard_map/ppermute | solution.py:421
  13.7 1.8 %copy-start.13 = (f32[4,128,128]{2,1,0:T(8,128)S(1)}, f32[4,128,128]{2,1,0:T(8,128)}, u32[]{:S(2)}) copy-start(f32[4,128,128]{2,1,0:T(8,128)} %get-tuple-element.17) | copy-start | bytes 786436
  13.7 1.8 %copy-start.14 = (f32[4,128,128]{2,1,0:T(8,128)S(1)}, f32[4,128,128]{2,1,0:T(8,128)}, u32[]{:S(2)}) copy-start(f32[4,128,128]{2,1,0:T(8,128)} %get-tuple-element.19) | copy-start | bytes 786436
  13.7 8.7 %copy-start.11 = (f32[4,128,128]{2,1,0:T(8,128)S(1)}, f32[4,128,128]{2,1,0:T(8,128)}, u32[]{:S(2)}) copy-start(f32[4,128,128]{2,1,0:T(8,128)} %get-tuple-element.20) | copy-start | bytes 786436
  13.7 9.6 %copy-start.12 = (f32[4,128,128]{2,1,0:T(8,128)S(1)}, f32[4,128,128]{2,1,0:T(8,128)}, u32[]{:S(2)}) copy-start(f32[4,128,128]{2,1,0:T(8,128)} %get-tuple-element.21) | copy-start | bytes 786436
  13.7 9.6 %collective-permute-start.2 = (f32[4,128,128]{2,1,0:T(8,128)}, f32[4,128,128]{2,1,0:T(8,128)}, u32[]{:S(2)}, u32[]{:S(2)}) collective-permute-start(f32[4,128,128]{2,1,0:T(8,128)} %get-tuple-element.22), channel_id=1, source_target_pairs={{0,1},{1,0},{2,3},{3,2},{4,5},{5,4},{6,7},{7,6},{8,9},{9,8},{10,11... | collective-permute-start | bytes 786440 | tf_op jit(solution)/shard_map/ppermute | solution.py:421
  14.9 17.3 %copy-start = (f32[512,8]{1,0:T(8,128)S(1)}, f32[512,8]{1,0:T(8,128)}, u32[]{:S(2)}) copy-start(f32[512,8]{1,0:T(8,128)} %constant.32.clone.tw) | copy-start | bytes 49156
  14.9 17.3 %copy-start.3 = (bf16[1024,256]{1,0:T(8,128)(2,1)S(1)}, bf16[1024,256]{1,0:T(8,128)(2,1)}, u32[]{:S(2)}) copy-start(bf16[1024,256]{1,0:T(8,128)(2,1)} %constant.34.clone.t_lo) | copy-start | bytes 1572868
  14.9 17.3 %copy-start.4 = (bf16[1024,256]{1,0:T(8,128)(2,1)S(1)}, bf16[1024,256]{1,0:T(8,128)(2,1)}, u32[]{:S(2)}) copy-start(bf16[1024,256]{1,0:T(8,128)(2,1)} %constant.33.clone.t_hi) | copy-start | bytes 1572868
  16.9 22.9 %collective-permute-start.1 = (f32[8,128,128]{2,1,0:T(8,128)}, f32[8,128,128]{2,1,0:T(8,128)S(1)}, u32[]{:S(2)}, u32[]{:S(2)}) collective-permute-start(f32[8,128,128]{2,1,0:T(8,128)} %pad_maximum_fusion), channel_id=1, source_target_pairs={{0,1},{1,0},{2,3},{3,2},{4,5},{5,4},{6,7},{7,6},{8,9},{9,8},{10,11... | collective-permute-start | bytes 1572872 | tf_op jit(solution)/shard_map/ppermute | solution.py:421
  18.8 13.4 %all-to-all-start.1 = ((f32[8,128,128]{2,1,0:T(8,128)}), f32[8,128,128]{2,1,0:T(8,128)S(1)}, u32[]{:S(2)}, u32[]{:S(2)}) async-start(f32[8,128,128]{2,1,0:T(8,128)} %get-tuple-element.23), calls=%async_computation.1 | async-start | bytes 1048576 | tf_op jit(solution)/shard_map/all_to_all | solution.py:447
  25.0 25.8 %collective-permute-start.3 = (f32[8,128,128]{2,1,0:T(8,128)S(1)}, f32[8,128,128]{2,1,0:T(8,128)S(1)}, u32[]{:S(2)}, u32[]{:S(2)}) collective-permute-start(f32[8,128,128]{2,1,0:T(8,128)S(1)} %pad_maximum_fusion.1.refs_0_), channel_id=1, source_target_pairs={{0,2},{2,0},{1,3},{3,1},{4,6},{6,4},{5,7},{7,5},{8,10},{10,8},{9,1... | collective-permute-start | bytes 1572872 | tf_op jit(solution)/shard_map/ppermute | solution.py:421
  34.5 13.2 %all-to-all-start.2 = ((f32[8,128,128]{2,1,0:T(8,128)}), f32[8,128,128]{2,1,0:T(8,128)S(1)}, u32[]{:S(2)}, u32[]{:S(2)}) async-start(f32[8,128,128]{2,1,0:T(8,128)} %bitcast.5), calls=%async_computation.2 | async-start | bytes 1048576 | tf_op jit(solution)/shard_map/all_to_all | solution.py:457
  38.0 12.8 %copy-start.9 = (f32[4,128,128]{2,1,0:T(8,128)S(1)}, f32[4,128,128]{2,1,0:T(8,128)}, u32[]{:S(2)}) copy-start(f32[4,128,128]{2,1,0:T(8,128)} %get-tuple-element.15.refs_0_) | copy-start | bytes 786436
  38.0 12.8 %copy-start.10 = (f32[4,128,128]{2,1,0:T(8,128)S(1)}, f32[4,128,128]{2,1,0:T(8,128)}, u32[]{:S(2)}) copy-start(f32[4,128,128]{2,1,0:T(8,128)} %get-tuple-element.16) | copy-start | bytes 786436
  47.7 30.6 %collective-permute-start.5 = (f32[8,128,128]{2,1,0:T(8,128)S(1)}, f32[8,128,128]{2,1,0:T(8,128)}, u32[]{:S(2)}, u32[]{:S(2)}) collective-permute-start(f32[8,128,128]{2,1,0:T(8,128)S(1)} %all-to-all-done.2.both), channel_id=1, source_target_pairs={{0,1},{1,0},{2,3},{3,2},{4,5},{5,4},{6,7},{7,6},{8,9},{9,8},{10,11... | collective-permute-start | bytes 1572872 | tf_op jit(solution)/shard_map/ppermute | solution.py:421
  53.2 21.6 %collective-permute-start.4 = (f32[4,128,128]{2,1,0:T(8,128)}, f32[4,128,128]{2,1,0:T(8,128)}, u32[]{:S(2)}, u32[]{:S(2)}) collective-permute-start(f32[4,128,128]{2,1,0:T(8,128)} %get-tuple-element.24.refs_0_), channel_id=1, source_target_pairs={{0,2},{2,0},{1,3},{3,1},{4,6},{6,4},{5,7},{7,5},{8,10},{10,8},{9,1... | collective-permute-start | bytes 786440 | tf_op jit(solution)/shard_map/ppermute | solution.py:421
  53.2 25.1 %collective-permute-start.7 = (f32[4,128,128]{2,1,0:T(8,128)}, f32[4,128,128]{2,1,0:T(8,128)}, u32[]{:S(2)}, u32[]{:S(2)}) collective-permute-start(f32[4,128,128]{2,1,0:T(8,128)} %get-tuple-element.26.refs_0_), channel_id=1, source_target_pairs={{0,2},{2,0},{1,3},{3,1},{4,6},{6,4},{5,7},{7,5},{8,10},{10,8},{9,1... | collective-permute-start | bytes 786440 | tf_op jit(solution)/shard_map/ppermute | solution.py:421
  56.1 22.2 %all-to-all-start = ((f32[8,128,128]{2,1,0:T(8,128)}), f32[8,128,128]{2,1,0:T(8,128)S(1)}, u32[]{:S(2)}, u32[]{:S(2)}) async-start(f32[8,128,128]{2,1,0:T(8,128)} %fusion.1.refs_0_), calls=%async_computation | async-start | bytes 1048576 | tf_op jit(solution)/shard_map/all_to_all | solution.py:466
  59.9 18.4 %copy-start.1 = (bf16[512,512]{1,0:T(8,128)(2,1)S(1)}, bf16[512,512]{1,0:T(8,128)(2,1)}, u32[]{:S(2)}) copy-start(bf16[512,512]{1,0:T(8,128)(2,1)} %constant.36.clone.t_lo) | copy-start | bytes 1572868
  59.9 18.4 %copy-start.2 = (bf16[512,512]{1,0:T(8,128)(2,1)S(1)}, bf16[512,512]{1,0:T(8,128)(2,1)}, u32[]{:S(2)}) copy-start(bf16[512,512]{1,0:T(8,128)(2,1)} %constant.35.clone.t_hi) | copy-start | bytes 1572868
  60.0 25.1 %copy-start.5 = (bf16[512,512]{1,0:T(8,128)(2,1)S(1)}, bf16[512,512]{1,0:T(8,128)(2,1)}, u32[]{:S(2)}) copy-start(bf16[512,512]{1,0:T(8,128)(2,1)} %constant.38.clone.refs_6_) | copy-start | bytes 1572868
  60.0 25.1 %copy-start.6 = (bf16[512,512]{1,0:T(8,128)(2,1)S(1)}, bf16[512,512]{1,0:T(8,128)(2,1)}, u32[]{:S(2)}) copy-start(bf16[512,512]{1,0:T(8,128)(2,1)} %constant.37.clone.refs_5_) | copy-start | bytes 1572868
  60.0 25.1 %copy-start.7 = (f32[8,512]{1,0:T(8,128)S(1)}, f32[8,512]{1,0:T(8,128)}, u32[]{:S(2)}) copy-start(f32[8,512]{1,0:T(8,128)} %constant.28.clone.tw._.refs_4_) | copy-start | bytes 49156
  74.8 10.3 %collective-permute-start.6 = (f32[4,128,128]{2,1,0:T(8,128)}, f32[4,128,128]{2,1,0:T(8,128)}, u32[]{:S(2)}, u32[]{:S(2)}) collective-permute-start(f32[4,128,128]{2,1,0:T(8,128)} %collective-permute-done.4.refs_0_.refs_2_), channel_id=1, source_target_pairs={{0,1},{1,0},{2,3},{3,2},{4,5},{5,4},{6,7},{7,6},{8,9},{9,8},{10,11... | collective-permute-start | bytes 786440 | tf_op jit(solution)/shard_map/ppermute | solution.py:421
  78.3 11.6 %collective-permute-start.8 = (f32[4,128,128]{2,1,0:T(8,128)}, f32[4,128,128]{2,1,0:T(8,128)}, u32[]{:S(2)}, u32[]{:S(2)}) collective-permute-start(f32[4,128,128]{2,1,0:T(8,128)} %collective-permute-done.7.refs_2_), channel_id=1, source_target_pairs={{0,1},{1,0},{2,3},{3,2},{4,5},{5,4},{6,7},{7,6},{8,9},{9,8},{10,11... | collective-permute-start | bytes 786440 | tf_op jit(solution)/shard_map/ppermute | solution.py:421
  81.2 13.6 %all-to-all-start.3 = ((f32[8,128,128]{2,1,0:T(8,128)}), f32[8,128,128]{2,1,0:T(8,128)S(1)}, u32[]{:S(2)}, u32[]{:S(2)}) async-start(f32[8,128,128]{2,1,0:T(8,128)} %bitcast.6), calls=%async_computation.3 | async-start | bytes 1048576 | tf_op jit(solution)/shard_map/all_to_all | solution.py:476
  89.9 4.9 %copy-start.8 = (bf16[256,256]{1,0:T(8,128)(2,1)S(1)}, bf16[256,256]{1,0:T(8,128)(2,1)}, u32[]{:S(2)}) copy-start(bf16[256,256]{1,0:T(8,128)(2,1)} %constant.39.clone.order) | copy-start | bytes 393220

commit v4 on v3

--- a/solution.py
+++ b/solution.py
@@ -440,7 +440,7 @@
     blocks.append(rest)
     far.append(send(blocks[1][3], PAIRS))
     later = zeros_after(far[0])[0, 0]
-    onward = jnp.concatenate([blocks[0][2] + far[0], blocks[1][2] + far[1] + later], axis=0)
+    onward = jnp.concatenate([blocks[0][2] + far[0], blocks[1][2] + far[1]], axis=0)
     skip = send(onward, SKIPS)
     near = send(jnp.concatenate([blocks[c][1] + later for c in range(2)], axis=0), PAIRS)
 

time: 96.6 us -> 107 us (1.11)
  waiting for transfers between devices: 36.7 us -> 47.3 us
  other arithmetic: 4.7 us -> 3.1 us
  starting transfers between devices: 25.8 us -> 27 us
    ppermute x9, waiting for transfers between devices: 24.8 us -> 38 us  [send(): return lax.ppermute(value, 'narrow', pairs)]
    all_to_all x1, waiting for transfers between devices: 4.52 us -> 0.01 us  [fast_body(): rows_in = lax.all_to_all(sorted_, 'wide', 0, 0).reshape(MY, LANES)]
    all_to_all x1, waiting for transfers between devices: 7.26 us -> 9.2 us  [fast_body(): half = lax.all_to_all(rows_out.reshape(wide, rows, LANES), 'wide', 0, 0)]
    add x1, other arithmetic: 1.61 us -> 0.03 us  [fast_body(): blocks[1][2] + far[1]]
    ppermute x9, starting transfers between devices: 11 us -> 12.2 us  [send(): return lax.ppermute(value, 'narrow', pairs)]
  transfers between devices with their start and end apart: 13 -> 13, of which waited for: 9 -> 7; matrix products, arithmetic and copies ran while one was open for 6% -> 2% of each run, Pallas kernels for 22% -> 20%
where the time goes in v4:
time: 107 us; the launch traced here: 106 us
  waiting for transfers between devices  47.3 us (44%)
  starting transfers between devices  27 us (25%)
  Pallas kernels  26.9 us (25%)
  other arithmetic  3.1 us (3%)
  local copies, waits for them, and re-layouts  1.1 us (1%)
    ppermute x9, waiting for transfers between devices, send(): return lax.ppermute(value, 'narrow', pairs)  38 us
    ppermute x9, starting transfers between devices, send(): return lax.ppermute(value, 'narrow', pairs)  12.2 us
    pallas_call x2, Pallas kernels, project_x(): pl.pallas_call(functools.partial(x_kernel, shards), grid_spec=pltpu.Prefe...  10 us
    pallas_call x2, Pallas kernels, back_x(): pl.pallas_call(x_back_kernel, grid_spec=pltpu.PrefetchScalarGridSpec(num_...  9.6 us
    all_to_all x1, waiting for transfers between devices, fast_body(): half = lax.all_to_all(rows_out.reshape(wide, rows, LANES), 'wide', 0, 0)  9.2 us
    pallas_call x7, Pallas kernels, whole(): pl.pallas_call(kernel, out_shape=shapes, in_specs=[in_vmem] * len(args) +...  7.25 us
    all_to_all x1, starting transfers between devices, fast_body(): lax.all_to_all(rows_out.reshape(wide, angle_rows, LANES), 'wide', 0, 0)  3.87 us
    all_to_all x1, starting transfers between devices, fast_body(): half = lax.all_to_all(rows_out.reshape(wide, rows, LANES), 'wide', 0, 0)  3.73 us
  transfers between devices with their start and end apart: 13, of which 7 were waited for; matrix products, arithmetic and copies ran while one was open for 2% of the time, Pallas kernels for 20%

profile of v4, /device:TPU:0, one launch (start us, length us, event | category | flops | bytes accessed | tf_op | source)
XLA Modules:
  0.0 106.2 jit_solution(11867659492664814785)
XLA Ops:
  0.6 4.7 %shard_map.149 = (f32[4,128,128]{2,1,0:T(8,128)}, f32[4,128,128]{2,1,0:T(8,128)}, f32[4,128,128]{2,1,0:T(8,128)}, f32[4,128,128]{2,1,0:T(8,128)}) custom-call(s32[1]{0:T(128)} %bitcast.place, f32[2,2,128,2048]{3,2,1,0:T(8,128)} %cur.3, f32[8,512]{1,0:T(8,128)} %constant.28.clone.tw._.refs_4_, bf16[512,512]{1,0:T(8,128)(2,1)} %constant.29.clone.t_hi, ...), custom_call_target="tpu_custom_call" | custom-call | flops 1048576 | bytes 65536 | tf_op jit(solution)/shard_map/pallas_call | solution.py:370
  5.3 3.0 %collective-permute-start = (f32[4,128,128]{2,1,0:T(8,128)}, f32[4,128,128]{2,1,0:T(8,128)S(1)}, u32[]{:S(2)}, u32[]{:S(2)}) collective-permute-start(f32[4,128,128]{2,1,0:T(8,128)} %get-tuple-element.18), channel_id=1, source_target_pairs={{0,1},{1,0},{2,3},{3,2},{4,5},{5,4},{6,7},{7,6},{8,9},{9,8},{10,11... | collective-permute-start | bytes 786440 | tf_op jit(solution)/shard_map/ppermute | solution.py:421
  8.3 5.3 %shard_map.150 = (f32[8,128,128]{2,1,0:T(8,128)}, f32[4,128,128]{2,1,0:T(8,128)}, f32[4,128,128]{2,1,0:T(8,128)}, f32[4,128,128]{2,1,0:T(8,128)}, f32[4,128,128]{2,1,0:T(8,128)}) custom-call(s32[1]{0:T(128)} %bitcast.place, f32[2,2,128,2048]{3,2,1,0:T(8,128)} %cur.3, f32[8,512]{1,0:T(8,128)} %constant.28.clone.tw._.refs_4_, ...), custom_call_target="tpu_custom_call" | custom-call | flops 1048576 | bytes 65536 | tf_op jit(solution)/shard_map/pallas_call | solution.py:370
  13.7 1.1 %collective-permute-done.refs_0_ = f32[4,128,128]{2,1,0:T(8,128)S(1)} collective-permute-done((f32[4,128,128]{2,1,0:T(8,128)}, f32[4,128,128]{2,1,0:T(8,128)S(1)}, u32[]{:S(2)}, u32[]{:S(2)}) %collective-permute-start) | collective-permute-done | bytes 262176 | tf_op jit(solution)/shard_map/ppermute | solution.py:421
  14.9 0.5 slice.6
  15.4 0.7 broadcast_add_fusion
  16.0 0.8 pad_maximum_fusion
  16.9 1.7 %collective-permute-start.1 = (f32[8,128,128]{2,1,0:T(8,128)}, f32[8,128,128]{2,1,0:T(8,128)S(1)}, u32[]{:S(2)}, u32[]{:S(2)}) collective-permute-start(f32[8,128,128]{2,1,0:T(8,128)} %pad_maximum_fusion), channel_id=1, source_target_pairs={{0,1},{1,0},{2,3},{3,2},{4,5},{5,4},{6,7},{7,6},{8,9},{9,8},{10,11... | collective-permute-start | bytes 1572872 | tf_op jit(solution)/shard_map/ppermute | solution.py:421
  18.6 3.7 %all-to-all-start.1 = ((f32[8,128,128]{2,1,0:T(8,128)}), f32[8,128,128]{2,1,0:T(8,128)S(1)}, u32[]{:S(2)}, u32[]{:S(2)}) async-start(f32[8,128,128]{2,1,0:T(8,128)} %get-tuple-element.23), calls=%async_computation.1 | async-start | bytes 1048576 | tf_op jit(solution)/shard_map/all_to_all | solution.py:447
  22.3 0.4 collective-permute-start.2
  22.8 13.0 %collective-permute-done.2 = f32[4,128,128]{2,1,0:T(8,128)S(1)} collective-permute-done((f32[4,128,128]{2,1,0:T(8,128)}, f32[4,128,128]{2,1,0:T(8,128)S(1)}, u32[]{:S(2)}, u32[]{:S(2)}) %collective-permute-start.2) | collective-permute-done | bytes 262176 | tf_op jit(solution)/shard_map/ppermute | solution.py:421
  35.8 0.0 copy-done.12
  35.9 2.5 %collective-permute-start.3 = (f32[8,128,128]{2,1,0:T(8,128)S(1)}, f32[8,128,128]{2,1,0:T(8,128)S(1)}, u32[]{:S(2)}, u32[]{:S(2)}) collective-permute-start(f32[8,128,128]{2,1,0:T(8,128)S(1)} %pad_maximum_fusion.1.refs_0_), channel_id=1, source_target_pairs={{0,2},{2,0},{1,3},{3,1},{4,6},{6,4},{5,7},{7,5},{8,10},{10,8},{9,1... | collective-permute-start | bytes 1572872 | tf_op jit(solution)/shard_map/ppermute | solution.py:421
  38.4 0.0 all-to-all-done.1
  38.4 0.0 copy-done.3
  38.4 2.3 %shard_map.153 = f32[1024,128]{1,0:T(8,128)} custom-call(f32[1024,128]{1,0:T(8,128)S(1)} %bitcast.7, f32[512,8]{1,0:T(8,128)S(1)} %copy-done, bf16[1024,256]{1,0:T(8,128)(2,1)S(1)} %copy-done.4, bf16[1024,256]{1,0:T(8,128)(2,1)S(1)} %copy-done.3, f32[8,128,128]{2,1,0:T(8,128)S(1)} %pad_maximum_fusion.1.refs_0_), custom_call_target="tpu_custom_call" | custom-call | flops 1048576 | bytes 65536 | tf_op jit(solution)/shard_map/pallas_call | solution.py:322
  40.7 3.7 %all-to-all-start.2 = ((f32[8,128,128]{2,1,0:T(8,128)}), f32[8,128,128]{2,1,0:T(8,128)S(1)}, u32[]{:S(2)}, u32[]{:S(2)}) async-start(f32[8,128,128]{2,1,0:T(8,128)} %bitcast.5), calls=%async_computation.2 | async-start | bytes 1048576 | tf_op jit(solution)/shard_map/all_to_all | solution.py:457
  44.5 0.0 collective-permute-done.1.refs_0_
  44.5 0.5 slice.7
  45.0 9.2 %all-to-all-done.2.both = f32[8,128,128]{2,1,0:T(8,128)S(1)} async-done(((f32[8,128,128]{2,1,0:T(8,128)}), f32[8,128,128]{2,1,0:T(8,128)S(1)}, u32[]{:S(2)}, u32[]{:S(2)}) %all-to-all-start.2) | async-done | bytes 524320 | tf_op jit(solution)/shard_map/all_to_all | solution.py:457
  54.2 1.6 %collective-permute-start.5 = (f32[8,128,128]{2,1,0:T(8,128)S(1)}, f32[8,128,128]{2,1,0:T(8,128)}, u32[]{:S(2)}, u32[]{:S(2)}) collective-permute-start(f32[8,128,128]{2,1,0:T(8,128)S(1)} %all-to-all-done.2.both), channel_id=1, source_target_pairs={{0,1},{1,0},{2,3},{3,2},{4,5},{5,4},{6,7},{7,6},{8,9},{9,8},{10,11... | collective-permute-start | bytes 1572872 | tf_op jit(solution)/shard_map/ppermute | solution.py:421
  55.8 4.6 %collective-permute-done.3 = f32[8,128,128]{2,1,0:T(8,128)S(1)} collective-permute-done((f32[8,128,128]{2,1,0:T(8,128)S(1)}, f32[8,128,128]{2,1,0:T(8,128)S(1)}, u32[]{:S(2)}, u32[]{:S(2)}) %collective-permute-start.3) | collective-permute-done | bytes 524320 | tf_op jit(solution)/shard_map/ppermute | solution.py:421
  60.4 0.0 copy-done.9
  60.4 1.5 %fusion.1.refs_0_ = f32[8,128,128]{2,1,0:T(8,128)} fusion(f32[8,128,128]{2,1,0:T(8,128)S(1)} %collective-permute-done.3, f32[8,128,128]{2,1,0:T(8,128)S(1)} %collective-permute-done.1.refs_0_, f32[4,128,128]{2,1,0:T(8,128)S(1)} %copy-done.10, f32[4,128,128]{2,1,0:T(8,128)S(1)} %copy-done.9, f32[]{:T(128)} %bitcast.2), kind=kLoop, calls=%fused_computation.2 | loop fusion | flops 524288 | bytes 2097156 | tf_op jit(solution)/shard_map/add | solution.py:461
  61.9 0.8 shard_map.154
  62.8 0.0 collective-permute-start.4
  62.8 2.9 %collective-permute-start.7 = (f32[4,128,128]{2,1,0:T(8,128)}, f32[4,128,128]{2,1,0:T(8,128)}, u32[]{:S(2)}, u32[]{:S(2)}) collective-permute-start(f32[4,128,128]{2,1,0:T(8,128)} %get-tuple-element.26.refs_0_), channel_id=1, source_target_pairs={{0,2},{2,0},{1,3},{3,1},{4,6},{6,4},{5,7},{7,5},{8,10},{10,8},{9,1... | collective-permute-start | bytes 786440 | tf_op jit(solution)/shard_map/ppermute | solution.py:421
  65.7 3.5 %all-to-all-start = ((f32[8,128,128]{2,1,0:T(8,128)}), f32[8,128,128]{2,1,0:T(8,128)S(1)}, u32[]{:S(2)}, u32[]{:S(2)}) async-start(f32[8,128,128]{2,1,0:T(8,128)} %fusion.1.refs_0_), calls=%async_computation | async-start | bytes 1048576 | tf_op jit(solution)/shard_map/all_to_all | solution.py:466
  69.2 0.0 copy-start.1
  69.2 0.0 copy-start.2
  69.2 0.0 copy-start.5
  69.2 0.0 copy-start.6
  69.2 0.0 copy-start.7
  69.2 14.6 %collective-permute-done.4.refs_0_.refs_2_ = f32[4,128,128]{2,1,0:T(8,128)} collective-permute-done((f32[4,128,128]{2,1,0:T(8,128)}, f32[4,128,128]{2,1,0:T(8,128)}, u32[]{:S(2)}, u32[]{:S(2)}) %collective-permute-start.4) | collective-permute-done | bytes 262176 | tf_op jit(solution)/shard_map/ppermute | solution.py:421
  83.9 0.0 collective-permute-start.6
  83.9 4.6 %collective-permute-done.7.refs_2_ = f32[4,128,128]{2,1,0:T(8,128)} collective-permute-done((f32[4,128,128]{2,1,0:T(8,128)}, f32[4,128,128]{2,1,0:T(8,128)}, u32[]{:S(2)}, u32[]{:S(2)}) %collective-permute-start.7) | collective-permute-done | bytes 262176 | tf_op jit(solution)/shard_map/ppermute | solution.py:421
  88.5 0.0 collective-permute-start.8
  88.5 0.0 collective-permute-done.5.refs_1_
  88.5 0.0 all-to-all-done
  88.5 2.8 %shard_map.156 = f32[1024,128]{1,0:T(8,128)} custom-call(f32[1024,128]{1,0:T(8,128)S(1)} %bitcast.8, f32[512,8]{1,0:T(8,128)S(1)} %copy-done, bf16[512,512]{1,0:T(8,128)(2,1)S(1)} %copy-done.2, bf16[512,512]{1,0:T(8,128)(2,1)S(1)} %copy-done.1, f32[8,128]{1,0:T(8,128)S(1)} %shard_map.155.refs_0_), custom_call_target="tpu_custom_call" | custom-call | flops 1048576 | bytes 65536 | tf_op jit(solution)/shard_map/pallas_call | solution.py:322
  91.4 3.9 %all-to-all-start.3 = ((f32[8,128,128]{2,1,0:T(8,128)}), f32[8,128,128]{2,1,0:T(8,128)S(1)}, u32[]{:S(2)}, u32[]{:S(2)}) async-start(f32[8,128,128]{2,1,0:T(8,128)} %bitcast.6), calls=%async_computation.3 | async-start | bytes 1048576 | tf_op jit(solution)/shard_map/all_to_all | solution.py:476
  95.2 0.0 collective-permute-done.6.refs_3_
  95.3 4.8 %shard_map.158 = (f32[2,2,128,2048]{3,2,1,0:T(8,128)}, f32[8,128]{1,0:T(8,128)}) custom-call(s32[1]{0:T(128)} %bitcast.place, f32[8,512]{1,0:T(8,128)S(1)} %copy-done.7, f32[4,128,128]{2,1,0:T(8,128)} %get-tuple-element.24.refs_0_, f32[8,128,128]{2,1,0:T(8,128)} %collective-permute-done.5.refs_1_, f32[4,128,128]{2,1,0:T(8,128)} %collective-permute-done.4.refs_0_.refs_2_, ...), custom_call_target="tpu_custom_call" | custom-call | flops 137438953472 | bytes 536870912 | tf_op jit(solution)/shard_map/pallas_call | solution.py:392
  100.1 0.0 collective-permute-done.8.refs_3_
  100.1 4.8 %shard_map.159 = (f32[2,2,128,2048]{3,2,1,0:T(8,128)}, f32[8,128]{1,0:T(8,128)}) custom-call(s32[1]{0:T(128)} %bitcast.place, f32[2,2,128,2048]{3,2,1,0:T(8,128)} %get-tuple-element.25._, f32[4,128,128]{2,1,0:T(8,128)} %get-tuple-element.26.refs_0_, f32[8,128,128]{2,1,0:T(8,128)} %collective-permute-done.5.refs_1_, ...), custom_call_target="tpu_custom_call", output_to_operand_aliasing={{0}: (1, {})} | custom-call | flops 1048576 | bytes 65536 | tf_op jit(solution)/shard_map/pallas_call | solution.py:392
  104.9 0.1 all-to-all-done.3.blocks
  105.0 0.0 copy-done.8
  105.0 1.3 %shard_map.157 = f32[2,2,128,256]{3,2,1,0:T(8,128)} custom-call(f32[8,128,128]{2,1,0:T(8,128)S(1)} %all-to-all-done.3.blocks, bf16[256,256]{1,0:T(8,128)(2,1)S(1)} %copy-done.8), custom_call_target="tpu_custom_call" | custom-call | flops 1048576 | bytes 65536 | tf_op jit(solution)/shard_map/pallas_call | solution.py:322
  (27 shorter events, 0.1 us)
Async XLA Ops:
  5.3 9.5 %collective-permute-start = (f32[4,128,128]{2,1,0:T(8,128)}, f32[4,128,128]{2,1,0:T(8,128)S(1)}, u32[]{:S(2)}, u32[]{:S(2)}) collective-permute-start(f32[4,128,128]{2,1,0:T(8,128)} %get-tuple-element.18), channel_id=1, source_target_pairs={{0,1},{1,0},{2,3},{3,2},{4,5},{5,4},{6,7},{7,6},{8,9},{9,8},{10,11... | collective-permute-start | bytes 786440 | tf_op jit(solution)/shard_map/ppermute | solution.py:421
  13.7 1.7 %copy-start.13 = (f32[4,128,128]{2,1,0:T(8,128)S(1)}, f32[4,128,128]{2,1,0:T(8,128)}, u32[]{:S(2)}) copy-start(f32[4,128,128]{2,1,0:T(8,128)} %get-tuple-element.17) | copy-start | bytes 786436
  13.7 1.7 %copy-start.14 = (f32[4,128,128]{2,1,0:T(8,128)S(1)}, f32[4,128,128]{2,1,0:T(8,128)}, u32[]{:S(2)}) copy-start(f32[4,128,128]{2,1,0:T(8,128)} %get-tuple-element.19) | copy-start | bytes 786436
  13.7 9.1 %copy-start.11 = (f32[4,128,128]{2,1,0:T(8,128)S(1)}, f32[4,128,128]{2,1,0:T(8,128)}, u32[]{:S(2)}) copy-start(f32[4,128,128]{2,1,0:T(8,128)} %get-tuple-element.20) | copy-start | bytes 786436
  13.7 22.1 %copy-start.12 = (f32[4,128,128]{2,1,0:T(8,128)S(1)}, f32[4,128,128]{2,1,0:T(8,128)}, u32[]{:S(2)}) copy-start(f32[4,128,128]{2,1,0:T(8,128)} %get-tuple-element.21) | copy-start | bytes 786436
  14.8 23.5 %copy-start = (f32[512,8]{1,0:T(8,128)S(1)}, f32[512,8]{1,0:T(8,128)}, u32[]{:S(2)}) copy-start(f32[512,8]{1,0:T(8,128)} %constant.32.clone.tw) | copy-start | bytes 49156
  14.8 23.5 %copy-start.3 = (bf16[1024,256]{1,0:T(8,128)(2,1)S(1)}, bf16[1024,256]{1,0:T(8,128)(2,1)}, u32[]{:S(2)}) copy-start(bf16[1024,256]{1,0:T(8,128)(2,1)} %constant.34.clone.t_lo) | copy-start | bytes 1572868
  14.8 23.5 %copy-start.4 = (bf16[1024,256]{1,0:T(8,128)(2,1)S(1)}, bf16[1024,256]{1,0:T(8,128)(2,1)}, u32[]{:S(2)}) copy-start(bf16[1024,256]{1,0:T(8,128)(2,1)} %constant.33.clone.t_hi) | copy-start | bytes 1572868
  16.9 27.6 %collective-permute-start.1 = (f32[8,128,128]{2,1,0:T(8,128)}, f32[8,128,128]{2,1,0:T(8,128)S(1)}, u32[]{:S(2)}, u32[]{:S(2)}) collective-permute-start(f32[8,128,128]{2,1,0:T(8,128)} %pad_maximum_fusion), channel_id=1, source_target_pairs={{0,1},{1,0},{2,3},{3,2},{4,5},{5,4},{6,7},{7,6},{8,9},{9,8},{10,11... | collective-permute-start | bytes 1572872 | tf_op jit(solution)/shard_map/ppermute | solution.py:421
  18.6 19.8 %all-to-all-start.1 = ((f32[8,128,128]{2,1,0:T(8,128)}), f32[8,128,128]{2,1,0:T(8,128)S(1)}, u32[]{:S(2)}, u32[]{:S(2)}) async-start(f32[8,128,128]{2,1,0:T(8,128)} %get-tuple-element.23), calls=%async_computation.1 | async-start | bytes 1048576 | tf_op jit(solution)/shard_map/all_to_all | solution.py:447
  22.3 13.5 %collective-permute-start.2 = (f32[4,128,128]{2,1,0:T(8,128)}, f32[4,128,128]{2,1,0:T(8,128)S(1)}, u32[]{:S(2)}, u32[]{:S(2)}) collective-permute-start(f32[4,128,128]{2,1,0:T(8,128)} %get-tuple-element.22), channel_id=1, source_target_pairs={{0,1},{1,0},{2,3},{3,2},{4,5},{5,4},{6,7},{7,6},{8,9},{9,8},{10,11... | collective-permute-start | bytes 786440 | tf_op jit(solution)/shard_map/ppermute | solution.py:421
  35.9 24.5 %collective-permute-start.3 = (f32[8,128,128]{2,1,0:T(8,128)S(1)}, f32[8,128,128]{2,1,0:T(8,128)S(1)}, u32[]{:S(2)}, u32[]{:S(2)}) collective-permute-start(f32[8,128,128]{2,1,0:T(8,128)S(1)} %pad_maximum_fusion.1.refs_0_), channel_id=1, source_target_pairs={{0,2},{2,0},{1,3},{3,1},{4,6},{6,4},{5,7},{7,5},{8,10},{10,8},{9,1... | collective-permute-start | bytes 1572872 | tf_op jit(solution)/shard_map/ppermute | solution.py:421
  40.7 13.5 %all-to-all-start.2 = ((f32[8,128,128]{2,1,0:T(8,128)}), f32[8,128,128]{2,1,0:T(8,128)S(1)}, u32[]{:S(2)}, u32[]{:S(2)}) async-start(f32[8,128,128]{2,1,0:T(8,128)} %bitcast.5), calls=%async_computation.2 | async-start | bytes 1048576 | tf_op jit(solution)/shard_map/all_to_all | solution.py:457
  44.4 16.0 %copy-start.9 = (f32[4,128,128]{2,1,0:T(8,128)S(1)}, f32[4,128,128]{2,1,0:T(8,128)}, u32[]{:S(2)}) copy-start(f32[4,128,128]{2,1,0:T(8,128)} %get-tuple-element.15.refs_0_) | copy-start | bytes 786436
  44.4 16.0 %copy-start.10 = (f32[4,128,128]{2,1,0:T(8,128)S(1)}, f32[4,128,128]{2,1,0:T(8,128)}, u32[]{:S(2)}) copy-start(f32[4,128,128]{2,1,0:T(8,128)} %get-tuple-element.16) | copy-start | bytes 786436
  54.2 34.3 %collective-permute-start.5 = (f32[8,128,128]{2,1,0:T(8,128)S(1)}, f32[8,128,128]{2,1,0:T(8,128)}, u32[]{:S(2)}, u32[]{:S(2)}) collective-permute-start(f32[8,128,128]{2,1,0:T(8,128)S(1)} %all-to-all-done.2.both), channel_id=1, source_target_pairs={{0,1},{1,0},{2,3},{3,2},{4,5},{5,4},{6,7},{7,6},{8,9},{9,8},{10,11... | collective-permute-start | bytes 1572872 | tf_op jit(solution)/shard_map/ppermute | solution.py:421
  62.8 21.1 %collective-permute-start.4 = (f32[4,128,128]{2,1,0:T(8,128)}, f32[4,128,128]{2,1,0:T(8,128)}, u32[]{:S(2)}, u32[]{:S(2)}) collective-permute-start(f32[4,128,128]{2,1,0:T(8,128)} %get-tuple-element.24.refs_0_), channel_id=1, source_target_pairs={{0,2},{2,0},{1,3},{3,1},{4,6},{6,4},{5,7},{7,5},{8,10},{10,8},{9,1... | collective-permute-start | bytes 786440 | tf_op jit(solution)/shard_map/ppermute | solution.py:421
  62.8 25.7 %collective-permute-start.7 = (f32[4,128,128]{2,1,0:T(8,128)}, f32[4,128,128]{2,1,0:T(8,128)}, u32[]{:S(2)}, u32[]{:S(2)}) collective-permute-start(f32[4,128,128]{2,1,0:T(8,128)} %get-tuple-element.26.refs_0_), channel_id=1, source_target_pairs={{0,2},{2,0},{1,3},{3,1},{4,6},{6,4},{5,7},{7,5},{8,10},{10,8},{9,1... | collective-permute-start | bytes 786440 | tf_op jit(solution)/shard_map/ppermute | solution.py:421
  65.7 22.8 %all-to-all-start = ((f32[8,128,128]{2,1,0:T(8,128)}), f32[8,128,128]{2,1,0:T(8,128)S(1)}, u32[]{:S(2)}, u32[]{:S(2)}) async-start(f32[8,128,128]{2,1,0:T(8,128)} %fusion.1.refs_0_), calls=%async_computation | async-start | bytes 1048576 | tf_op jit(solution)/shard_map/all_to_all | solution.py:466
  69.2 19.3 %copy-start.1 = (bf16[512,512]{1,0:T(8,128)(2,1)S(1)}, bf16[512,512]{1,0:T(8,128)(2,1)}, u32[]{:S(2)}) copy-start(bf16[512,512]{1,0:T(8,128)(2,1)} %constant.36.clone.t_lo) | copy-start | bytes 1572868
  69.2 19.3 %copy-start.2 = (bf16[512,512]{1,0:T(8,128)(2,1)S(1)}, bf16[512,512]{1,0:T(8,128)(2,1)}, u32[]{:S(2)}) copy-start(bf16[512,512]{1,0:T(8,128)(2,1)} %constant.35.clone.t_hi) | copy-start | bytes 1572868
  69.2 26.0 %copy-start.5 = (bf16[512,512]{1,0:T(8,128)(2,1)S(1)}, bf16[512,512]{1,0:T(8,128)(2,1)}, u32[]{:S(2)}) copy-start(bf16[512,512]{1,0:T(8,128)(2,1)} %constant.38.clone.refs_6_) | copy-start | bytes 1572868
  69.2 26.0 %copy-start.6 = (bf16[512,512]{1,0:T(8,128)(2,1)S(1)}, bf16[512,512]{1,0:T(8,128)(2,1)}, u32[]{:S(2)}) copy-start(bf16[512,512]{1,0:T(8,128)(2,1)} %constant.37.clone.refs_5_) | copy-start | bytes 1572868
  69.2 26.0 %copy-start.7 = (f32[8,512]{1,0:T(8,128)S(1)}, f32[8,512]{1,0:T(8,128)}, u32[]{:S(2)}) copy-start(f32[8,512]{1,0:T(8,128)} %constant.28.clone.tw._.refs_4_) | copy-start | bytes 49156
  83.9 11.4 %collective-permute-start.6 = (f32[4,128,128]{2,1,0:T(8,128)}, f32[4,128,128]{2,1,0:T(8,128)}, u32[]{:S(2)}, u32[]{:S(2)}) collective-permute-start(f32[4,128,128]{2,1,0:T(8,128)} %collective-permute-done.4.refs_0_.refs_2_), channel_id=1, source_target_pairs={{0,1},{1,0},{2,3},{3,2},{4,5},{5,4},{6,7},{7,6},{8,9},{9,8},{10,11... | collective-permute-start | bytes 786440 | tf_op jit(solution)/shard_map/ppermute | solution.py:421
  88.5 11.6 %collective-permute-start.8 = (f32[4,128,128]{2,1,0:T(8,128)}, f32[4,128,128]{2,1,0:T(8,128)}, u32[]{:S(2)}, u32[]{:S(2)}) collective-permute-start(f32[4,128,128]{2,1,0:T(8,128)} %collective-permute-done.7.refs_2_), channel_id=1, source_target_pairs={{0,1},{1,0},{2,3},{3,2},{4,5},{5,4},{6,7},{7,6},{8,9},{9,8},{10,11... | collective-permute-start | bytes 786440 | tf_op jit(solution)/shard_map/ppermute | solution.py:421
  91.4 13.6 %all-to-all-start.3 = ((f32[8,128,128]{2,1,0:T(8,128)}), f32[8,128,128]{2,1,0:T(8,128)S(1)}, u32[]{:S(2)}, u32[]{:S(2)}) async-start(f32[8,128,128]{2,1,0:T(8,128)} %bitcast.6), calls=%async_computation.3 | async-start | bytes 1048576 | tf_op jit(solution)/shard_map/all_to_all | solution.py:476
  100.0 4.9 %copy-start.8 = (bf16[256,256]{1,0:T(8,128)(2,1)S(1)}, bf16[256,256]{1,0:T(8,128)(2,1)}, u32[]{:S(2)}) copy-start(bf16[256,256]{1,0:T(8,128)(2,1)} %constant.39.clone.order) | copy-start | bytes 393220
